TPU v7x, 32 devices: a whole 2x2x4 slice. The times are simulated.
32 devices in a mesh: seq: 8 (over z, y), tp: 4 (over x, core).
Axes of the slice: x: 2, y: 2, z: 4, core: 2. Of those that a mesh axis runs over, the one named last changes fastest.
Arguments:
- states: bfloat16 [64, 3072], P(None, 'seq'), may hold values from -20 to 20
- norm_gain: bfloat16 [3072], P('seq'), may hold values from 0.25 to 1.75
- w_qkv: bfloat16 [3, 3072, 3072], P(None, 'seq', 'tp'), may hold values from -0.109375 to 0.109375
- w_out: bfloat16 [3072, 3072], P('tp', 'seq'), may hold values from -0.109375 to 0.109375
- cache: bfloat16 [192, 2, 64, 3072], P('seq', None, None, 'tp'), may hold values from -400 to 400
- context_len: int32 [64], replicated, may hold values from 1 to 4096, as said below
- block_owner: int32 [192], P('seq'), may hold values from 0 to 64, as said below
- block_index: int32 [192], P('seq'), may hold values from 0 to 63, as said below
Outputs:
- hidden: bfloat16 [64, 3072], P('tp', 'seq')
- updated: bfloat16 [192, 2, 64, 3072], P('seq', None, None, 'tp')
Inputs may be any that keep to these rules, and one draw needn't show every extreme that they name: `context_len`: A request of length n owns exactly ceil(n / 64) pool blocks, with block_index 0, 1, ... once each; at least one pool block is unused. `context_len`: exactly 1 request own 64/2 blocks or more; every other request owns at most 2 blocks, all on one index of seq. `block_owner`: the value 64 marks an unused block. `block_index`: 0 for an unused block.
All inputs are finite; a program needn't handle non-finite values.
Results may differ from a plain program's by a relative error of at most 0.0068.
Values may be sent and summed in bfloat16 or wider, within the bound.
No kernel may reach another device: no remote copies, remote signals or barrier semaphores. Data moves between devices by JAX's collectives and lax.ppermute only.
A program may use at most 128 MiB of HBM per device.

v0:
```python
import jax
import jax.numpy as jnp
from jax import lax
from jax.sharding import PartitionSpec as P

HEAD_DIM = 96


EPSILON = 1e-05
NEG_FLOOR = -1e30


def rotate(values, positions):
    half_dim = HEAD_DIM // 2
    frequency = 10000.0 ** (-jnp.arange(half_dim, dtype=jnp.float32) * 2.0 / HEAD_DIM)
    angles = positions.astype(jnp.float32)[:, None] * frequency[None, :]
    cosine = jnp.cos(angles)[:, None, :]
    sine_part = jnp.sin(angles)[:, None, :]
    front_half = values[..., :half_dim]
    back_half = values[..., half_dim:]
    return jnp.concatenate(
        [front_half * cosine - back_half * sine_part, back_half * cosine + front_half * sine_part],
        axis=-1,
    )


def finish(projected, positions):
    row_count = projected.shape[0]
    columns = projected.shape[2]
    head_count = columns // HEAD_DIM
    query = rotate(
        projected[:, 0].reshape(row_count, head_count, HEAD_DIM), positions
    ) * HEAD_DIM ** (-0.5)
    keys_new = rotate(projected[:, 1].reshape(row_count, head_count, HEAD_DIM), positions)
    return (
        query.astype(jnp.bfloat16).reshape(row_count, columns),
        keys_new.astype(jnp.bfloat16).reshape(row_count, columns),
        projected[:, 2].astype(jnp.bfloat16),
    )


def shards(states, norm_gain, w_qkv, w_out, cache, context_len, block_owner, block_index):
    requests = states.shape[0]
    seq_count = lax.axis_size("seq")
    wide_states = states.astype(jnp.float32)
    sum_squares = lax.psum(jnp.sum(wide_states * wide_states, axis=1), "seq")
    inverse = lax.rsqrt(sum_squares / (states.shape[1] * seq_count) + EPSILON)
    normed = (wide_states * inverse[:, None] * norm_gain.astype(jnp.float32)[None, :]).astype(
        jnp.bfloat16
    )
    positions = context_len - 1
    local_term = jnp.einsum("rd,cdh->rch", normed, w_qkv, preferred_element_type=jnp.float32)
    projected = lax.psum(local_term, "seq")
    query, keys_new, values_new = finish(projected, positions)
    blocks, _, tokens, columns = cache.shape
    head_count = columns // HEAD_DIM
    block_live = block_owner < requests
    owner_row = jnp.minimum(block_owner, requests - 1)
    last_position = positions[owner_row]
    block_hit = block_live & (block_index == last_position // tokens)
    slot_hit = block_hit[:, None] & (
        jnp.arange(tokens, dtype=jnp.int32)[None, :] == (last_position % tokens)[:, None]
    )
    fresh_rows = jnp.stack([keys_new[owner_row], values_new[owner_row]], axis=1)
    updated = jnp.where(slot_hit[:, None, :, None], fresh_rows[:, :, None, :], cache)
    query_rows = query[owner_row].reshape(blocks, head_count, HEAD_DIM)
    key_cache = updated[:, 0].reshape(blocks, tokens, head_count, HEAD_DIM)
    value_cache = updated[:, 1].reshape(blocks, tokens, head_count, HEAD_DIM)
    scores = jnp.einsum("bhd,bthd->bht", query_rows, key_cache, preferred_element_type=jnp.float32)
    token_position = block_index[:, None] * tokens + jnp.arange(tokens, dtype=jnp.int32)[None, :]
    visible = block_live[:, None] & (token_position < context_len[owner_row][:, None])
    masked = jnp.where(visible[:, None, :], scores, NEG_FLOOR)
    block_max = jnp.max(masked, axis=-1)
    weights = jnp.where(visible[:, None, :], jnp.exp(masked - block_max[..., None]), 0.0).astype(
        jnp.bfloat16
    )
    block_sum = jnp.sum(weights.astype(jnp.float32), axis=-1)
    block_out = jnp.einsum(
        "bht,bthd->bhd", weights, value_cache, preferred_element_type=jnp.float32
    ).reshape(blocks, columns)
    segment = jnp.where(block_live, block_owner, requests)
    member = segment[None, :] == jnp.arange(requests, dtype=jnp.int32)[:, None]
    local_max = jnp.max(jnp.where(member[:, :, None], block_max[None, :, :], NEG_FLOOR), axis=1)
    factor = jnp.exp(block_max - local_max[owner_row])
    member_matrix = member.astype(jnp.float32)
    totals = jnp.dot(member_matrix, block_sum * factor, precision=lax.Precision.HIGHEST)
    outputs = jnp.dot(
        member_matrix,
        block_out * jnp.repeat(factor, HEAD_DIM, axis=1),
        precision=lax.Precision.HIGHEST,
    )
    received = (
        lax.all_to_all(local_max[None], "seq", split_axis=1, concat_axis=0, tiled=True),
        lax.all_to_all(totals[None], "seq", split_axis=1, concat_axis=0, tiled=True),
        lax.all_to_all(outputs[None], "seq", split_axis=1, concat_axis=0, tiled=True),
    )
    highest = jnp.max(received[0], axis=0)
    source_scale = jnp.exp(received[0] - highest[None])
    share_total = jnp.sum(received[1] * source_scale, axis=0)
    share_out = jnp.sum(received[2] * jnp.repeat(source_scale, HEAD_DIM, axis=2), axis=0)
    share_attended = (share_out / jnp.repeat(share_total, HEAD_DIM, axis=1)).astype(jnp.bfloat16)
    terms = jnp.dot(
        lax.all_gather(share_attended, "seq", axis=0, tiled=True),
        w_out,
        preferred_element_type=jnp.float32,
    )
    summed = lax.psum_scatter(terms, "tp", scatter_dimension=0, tiled=True)
    row_count = summed.shape[0]
    residual_rows = lax.dynamic_slice_in_dim(
        wide_states, lax.axis_index("tp") * row_count, row_count, 0
    )
    hidden = (summed + residual_rows).astype(jnp.bfloat16)
    return (hidden, updated)


def solution(mesh):
    return jax.shard_map(
        shards,
        mesh=mesh,
        in_specs=(
            P(None, "seq"),
            P("seq"),
            P(None, "seq", "tp"),
            P("tp", "seq"),
            P("seq", None, None, "tp"),
            P(),
            P("seq"),
            P("seq"),
        ),
        out_specs=(P("tp", "seq"), P("seq", None, None, "tp")),
        check_vma=False,
    )
```

profile of v0, /device:TPU:0, one launch (start us, length us, event | category | flops | bytes accessed | tf_op | source)
XLA Modules:
  0.0 222.9 jit_solution(12325342863786237233)
XLA Ops:
  7.3 0.8 convert_element_type.43
  8.1 0.9 multiply_reduce_fusion
  9.0 23.1 %psum.14 = f32[64]{0:T(128)S(1)} all-reduce(f32[64]{0:T(128)S(1)} %multiply_reduce_fusion), channel_id=1, replica_groups=mesh['seq'=8,'tp'=4] {'seq'}, use_global_device_ids=true, to_apply=%region_1.0 | all-reduce | flops 64 | bytes 512 | tf_op jit(solution)/shard_map/psum | solution.py:46
  32.1 2.1 fusion.9
  34.2 0.7 broadcast_add_fusion
  34.9 0.7 broadcast_select_fusion.1
  35.6 0.7 broadcast_multiply_fusion.1
  36.2 0.7 gather_fusion.2
  37.0 0.7 gather_fusion
  38.1 66.5 %all-reduce.2.cloned.1.call-done = f32[64,3,768]{2,0,1:T(8,128)} async-done(((f32[64,3,768]{2,0,1:T(8,128)}), f32[64,3,768]{2,0,1:T(8,128)}) %all-reduce.2.cloned.1.call-update) | async-done | bytes 589840 | tf_op jit(solution)/shard_map/psum | solution.py:53
  104.6 1.0 fusion.23
  106.4 0.6 gather_fusion.1
  107.2 0.9 fusion.6
  109.7 2.7 %broadcast_select_fusion = bf16[24,2,64,768]{3,2,1,0:T(8,128)(2,1)S(1)} fusion(bf16[24,2,64,768]{3,2,1,0:T(8,128)(2,1)} %param.12, pred[24,64]{1,0:T(8,128)(4,1)S(1)} %get-tuple-element.25, bf16[24,2,768]{2,1,0:T(2,128)(2,1)S(1)} %copy.25), kind=kLoop, calls=%fused_computation.6 | loop fusion | flops 2359296 | bytes 9512448 | tf_op jit(solution)/shard_map/jit(_where)/select_n | solution.py:65
  112.4 2.7 %fusion.22 = (bf16[24,1,64,768]{3,2,1,0:T(8,128)(2,1)}, bf16[24,1,64,768]{3,2,1,0:T(8,128)(2,1)}) fusion(bf16[24,2,64,768]{3,2,1,0:T(8,128)(2,1)S(1)} %broadcast_select_fusion), kind=kLoop, calls=%fused_computation.69 | loop fusion | bytes 9437184 | tf_op jit(solution)/shard_map/slice | solution.py:68
  115.1 0.9 copy-done.2
  116.0 6.4 %reshape_squeeze.14 = bf16[24,64,8,96]{3,2,1,0:T(8,128)(2,1)} reshape(bf16[24,1,64,768]{3,2,1,0:T(8,128)(2,1)} %get-tuple-element.5) | data formatting | bytes 4718592 | tf_op jit(solution)/shard_map/reshape;squeeze | solution.py:67
  122.4 3.6 %fusion.2 = f32[24,8,1,64]{3,2,1,0:T(1,128)S(1)} fusion(bf16[24,8,96,1]{2,3,1,0:T(2,128)(2,1)S(1)} %reshape.267, bf16[24,64,8,96]{3,2,1,0:T(8,128)(2,1)} %reshape_squeeze.14), kind=kOutput, calls=%fused_computation.9 | convolution fusion | flops 2359296 | bytes 2445312 | tf_op jit(solution)/shard_map/bhd,bthd->bht/dot_general | solution.py:69
  127.1 0.9 fusion.14
  128.0 3.6 %all-to-all-start.2 = ((f32[1,64,8]{2,0,1:T(1,128)}), f32[1,64,8]{2,0,1:T(1,128)S(1)}, u32[]{:S(2)}, u32[]{:S(2)}) async-start(f32[1,64,8]{2,0,1:T(1,128)} %bitcast.15), calls=%async_computation.2 | async-start | bytes 65536 | tf_op jit(solution)/shard_map/all_to_all | solution.py:94
  131.6 6.4 %reshape_squeeze.15 = bf16[24,64,8,96]{3,2,1,0:T(8,128)(2,1)} reshape(bf16[24,1,64,768]{3,2,1,0:T(8,128)(2,1)} %get-tuple-element.4) | data formatting | bytes 4718592 | tf_op jit(solution)/shard_map/reshape;squeeze | solution.py:68
  138.1 2.9 %fusion = f32[24,8,1,96]{3,2,1,0:T(1,128)S(1)} fusion(bf16[24,64,8,96]{3,2,1,0:T(8,128)(2,1)} %reshape_squeeze.15, bf16[24,8,64,1]{2,1,0,3:T(8,128)(2,1)S(1)} %get-tuple-element.12), kind=kOutput, calls=%fused_computation.7 | convolution fusion | flops 2359296 | bytes 2457600 | tf_op jit(solution)/shard_map/bht,bthd->bhd/dot_general | solution.py:78
  141.0 0.7 copy.28
  141.8 6.0 %all-to-all-start.1 = ((f32[1,64,8]{2,0,1:T(1,128)}), f32[1,64,8]{2,0,1:T(1,128)S(1)}, u32[]{:S(2)}, u32[]{:S(2)}) async-start(f32[1,64,8]{2,0,1:T(1,128)} %copy.28), calls=%async_computation.1 | async-start | bytes 65536 | tf_op jit(solution)/shard_map/all_to_all | solution.py:93
  148.2 0.9 copy.27
  149.1 5.4 %all-to-all-done.1 = f32[1,64,8]{2,0,1:T(1,128)S(1)} async-done(((f32[1,64,8]{2,0,1:T(1,128)}), f32[1,64,8]{2,0,1:T(1,128)S(1)}, u32[]{:S(2)}, u32[]{:S(2)}) %all-to-all-start.1) | async-done | bytes 2080 | tf_op jit(solution)/shard_map/all_to_all | solution.py:93
  154.5 3.4 %all-to-all-start = ((f32[1,64,768]{2,0,1:T(1,128)}), f32[1,64,768]{2,0,1:T(1,128)S(1)}, u32[]{:S(2)}, u32[]{:S(2)}) async-start(f32[1,64,768]{2,0,1:T(1,128)} %copy.27), calls=%async_computation | async-start | bytes 393216 | tf_op jit(solution)/shard_map/all_to_all | solution.py:95
  158.8 6.8 %all-to-all-done = f32[1,64,768]{2,0,1:T(1,128)S(1)} async-done(((f32[1,64,768]{2,0,1:T(1,128)}), f32[1,64,768]{2,0,1:T(1,128)S(1)}, u32[]{:S(2)}, u32[]{:S(2)}) %all-to-all-start) | async-done | bytes 196640 | tf_op jit(solution)/shard_map/all_to_all | solution.py:95
  165.7 30.5 %all_gather.3 = bf16[64,768]{1,0:T(8,128)(2,1)S(1)} all-gather(bf16[8,768]{1,0:T(8,128)(2,1)S(1)} %divide_convert_fusion), channel_id=1, replica_groups=mesh['seq'=8,'tp'=4] {'seq'}, dimensions={0}, use_global_device_ids=true | all-gather | bytes 110592 | tf_op jit(solution)/shard_map/all_gather | solution.py:103
  196.2 0.8 fusion.24
  197.1 17.6 %reduce-scatter.2.cloned.1.call-done = f32[16,384]{1,0:T(8,128)} async-done(((f32[64,384]{1,0:T(8,128)}), f32[16,384]{1,0:T(8,128)}) %reduce-scatter.2.cloned.1.call-update) | async-done | bytes 24592 | tf_op jit(solution)/shard_map/reduce_scatter | solution.py:107
  214.7 1.3 add_convert_fusion.1
  (61 shorter events, 5.5 us)
Async XLA Ops:
  7.2 24.9 %copy-start = (bf16[3,384,768]{2,1,0:T(8,128)(2,1)S(1)}, bf16[3,384,768]{2,1,0:T(8,128)(2,1)}, u32[]{:S(2)}) copy-start(bf16[3,384,768]{2,1,0:T(8,128)(2,1)} %param.10) | copy-start | bytes 5308420
  7.2 29.9 %copy-start.1 = (s32[64]{0:T(128)S(1)}, s32[64]{0:T(128)}, u32[]{:S(2)}) copy-start(s32[64]{0:T(128)} %param.13) | copy-start | bytes 772
  7.2 29.7 %copy-start.5 = (s32[24]{0:T(128)S(1)}, s32[24]{0:T(128)}, u32[]{:S(2)}) copy-start(s32[24]{0:T(128)} %param.14) | copy-start | bytes 292
  7.2 29.7 %copy-start.6 = (s32[24]{0:T(128)S(1)}, s32[24]{0:T(128)}, u32[]{:S(2)}) copy-start(s32[24]{0:T(128)} %param.15) | copy-start | bytes 292
  7.2 97.3 %all-reduce.2.cloned.1.call-start = ((), (), s32[]{:S(2)}) async-start(), calls=%async_computation.4 | async-start | bytes 1179648 | tf_op jit(solution)/shard_map/psum | solution.py:53
  112.4 3.6 %copy-start.2 = (bf16[24,2,64,768]{3,2,1,0:T(8,128)(2,1)}, bf16[24,2,64,768]{3,2,1,0:T(8,128)(2,1)S(1)}, u32[]{:S(2)}) copy-start(bf16[24,2,64,768]{3,2,1,0:T(8,128)(2,1)S(1)} %broadcast_select_fusion) | copy-start | bytes 14155780
  128.0 13.8 %all-to-all-start.2 = ((f32[1,64,8]{2,0,1:T(1,128)}), f32[1,64,8]{2,0,1:T(1,128)S(1)}, u32[]{:S(2)}, u32[]{:S(2)}) async-start(f32[1,64,8]{2,0,1:T(1,128)} %bitcast.15), calls=%async_computation.2 | async-start | bytes 65536 | tf_op jit(solution)/shard_map/all_to_all | solution.py:94
  138.1 58.2 %copy-start.3 = (bf16[768,384]{1,0:T(8,128)(2,1)S(1)}, bf16[768,384]{1,0:T(8,128)(2,1)}, u32[]{:S(2)}) copy-start(bf16[768,384]{1,0:T(8,128)(2,1)} %param.11) | copy-start | bytes 1769476
  138.1 59.0 %copy-start.4 = (bf16[64,384]{1,0:T(8,128)(2,1)S(1)}, bf16[64,384]{1,0:T(8,128)(2,1)}, u32[]{:S(2)}) copy-start(bf16[64,384]{1,0:T(8,128)(2,1)} %param.8) | copy-start | bytes 147460
  141.8 12.7 %all-to-all-start.1 = ((f32[1,64,8]{2,0,1:T(1,128)}), f32[1,64,8]{2,0,1:T(1,128)S(1)}, u32[]{:S(2)}, u32[]{:S(2)}) async-start(f32[1,64,8]{2,0,1:T(1,128)} %copy.28), calls=%async_computation.1 | async-start | bytes 65536 | tf_op jit(solution)/shard_map/all_to_all | solution.py:93
  154.5 11.1 %all-to-all-start = ((f32[1,64,768]{2,0,1:T(1,128)}), f32[1,64,768]{2,0,1:T(1,128)S(1)}, u32[]{:S(2)}, u32[]{:S(2)}) async-start(f32[1,64,768]{2,0,1:T(1,128)} %copy.27), calls=%async_computation | async-start | bytes 393216 | tf_op jit(solution)/shard_map/all_to_all | solution.py:95
  157.9 56.8 %reduce-scatter.2.cloned.1.call-start = ((), (), s32[]{:S(2)}) async-start(), calls=%async_computation.5 | async-start | bytes 122880 | tf_op jit(solution)/shard_map/reduce_scatter | solution.py:107
Sparse Core Ops, SparseCore 0:
  34.4 70.1 all-reduce.1
  197.2 17.4 reduce-scatter.1
where the time goes:
time: 224 us; the launch traced here: 223 us
  waiting for transfers between devices  96.3 us (43%)
  blocking collectives  53.7 us (24%)
  local copies, waits for them, and re-layouts  25.5 us (11%)
  between operations  14.3 us (6%)
  starting transfers between devices  13.1 us (6%)
  matrix products  10.6 us (5%)
  other arithmetic  9.27 us (4%)
    psum x1, waiting for transfers between devices, shards(): projected = lax.psum(local_term, 'seq')  66.5 us
    all_gather x1, blocking collectives, shards(): lax.all_gather(share_attended, 'seq', axis=0, tiled=True)  30.5 us
    psum x1, blocking collectives, shards(): sum_squares = lax.psum(jnp.sum(wide_states * wide_states, axis=1), 'seq')  23.1 us
    reduce_scatter x1, waiting for transfers between devices, shards(): summed = lax.psum_scatter(terms, 'tp', scatter_dimension=0, tiled=True)  17.6 us
    all_to_all x1, waiting for transfers between devices, shards(): lax.all_to_all(outputs[None], 'seq', split_axis=1, concat_axis=0, tiled=T...  6.81 us
    another operation x1, local copies, waits for them, and re-layouts, shards(): value_cache = updated[:, 1].reshape(blocks, tokens, head_count, HEAD_DIM)  6.43 us
    another operation x1, local copies, waits for them, and re-layouts, shards(): key_cache = updated[:, 0].reshape(blocks, tokens, head_count, HEAD_DIM)  6.43 us
    all_to_all x1, starting transfers between devices, shards(): lax.all_to_all(local_max[None], 'seq', split_axis=1, concat_axis=0, tiled...  6.01 us
  transfers between devices with their start and end apart: 5, of which 4 were waited for; matrix products, arithmetic and copies ran while one was open for 7% of the time, Pallas kernels for 0%

commit v1 on v0

v1 whole, which is shorter than its diff:
```python
import functools

import jax
import jax.numpy as jnp
from jax import lax
from jax.experimental import pallas as pl
from jax.experimental.pallas import tpu as pltpu
from jax.sharding import PartitionSpec as P

HEAD_DIM = 96
EPSILON = 1e-05
NEG_FLOOR = -1e30
LANES = 128
GROUP = 4

VMEM = pltpu.MemorySpace.VMEM


def split3(value):
    high = value.astype(jnp.bfloat16).astype(jnp.float32)
    rest = value - high
    mid = rest.astype(jnp.bfloat16).astype(jnp.float32)
    low = (rest - mid).astype(jnp.bfloat16).astype(jnp.float32)
    return high, mid, low


def project_kernel(states_ref, gain_ref, w_ref, out_ref, w_buf, sems):
    parts = w_ref.shape[0]
    columns = w_ref.shape[2]
    peers, share, _ = out_ref.shape
    copies = [pltpu.make_async_copy(w_ref.at[c], w_buf.at[c], sems.at[c]) for c in range(parts)]
    for copy in copies:
        copy.start()
    wide = states_ref[...].astype(jnp.float32)
    scaled = (wide * gain_ref[...].astype(jnp.float32)).astype(jnp.bfloat16)
    squares = jnp.sum(wide * wide, axis=1, keepdims=True)
    high, mid, low = split3(squares)
    lane = lax.broadcasted_iota(jnp.int32, (wide.shape[0], LANES), 1)
    stat = jnp.where(lane == 0, high, jnp.where(lane == 1, mid, jnp.where(lane == 2, low, 0.0)))
    for d in range(peers):
        out_ref[d, :, parts * columns :] = stat[d * share : (d + 1) * share].astype(jnp.bfloat16)
    for c in range(parts):
        copies[c].wait()
        term = jnp.dot(scaled, w_buf[c], preferred_element_type=jnp.float32)
        for d in range(peers):
            out_ref[d, :, c * columns : (c + 1) * columns] = term[
                d * share : (d + 1) * share
            ].astype(jnp.bfloat16)


def finish_kernel(width, recv_ref, cos_ref, sin_ref, out_ref):
    peers, _, _ = recv_ref.shape
    columns = cos_ref.shape[1]
    total = recv_ref[0].astype(jnp.float32)
    for d in range(1, peers):
        total = total + recv_ref[d].astype(jnp.float32)
    squares = jnp.sum(total[:, 3 * columns :], axis=1, keepdims=True)
    inverse = lax.rsqrt(squares * (1.0 / width) + EPSILON)
    cosine = cos_ref[...]
    sine = sin_ref[...]
    half = HEAD_DIM // 2
    front = lax.broadcasted_iota(jnp.int32, cosine.shape, 1) % HEAD_DIM < half

    def rotated(x):
        other = jnp.where(front, -pltpu.roll(x, columns - half, 1), pltpu.roll(x, half, 1))
        return x * cosine + other * sine

    query = rotated(total[:, :columns] * inverse) * HEAD_DIM ** (-0.5)
    keys_new = rotated(total[:, columns : 2 * columns] * inverse)
    values_new = total[:, 2 * columns : 3 * columns] * inverse
    for d in range(peers):
        out_ref[d, :, :columns] = query.astype(jnp.bfloat16)
        out_ref[d, :, columns : 2 * columns] = keys_new.astype(jnp.bfloat16)
        out_ref[d, :, 2 * columns :] = values_new.astype(jnp.bfloat16)


def attend_kernel(
    qkv_ref, owner_ref, seen_ref, slot_ref, cache_ref, out_ref, updated_ref, rows_q, fresh, sums
):
    step = pl.program_id(0)
    requests = qkv_ref.shape[0]
    blocks = owner_ref.shape[0] // (HEADS := 8)
    group, _, tokens, columns = cache_ref.shape
    peers = out_ref.shape[0]
    lane_head = lax.broadcasted_iota(jnp.int32, (HEADS, columns), 1) // HEAD_DIM
    head_mask = lane_head == lax.broadcasted_iota(jnp.int32, (HEADS, columns), 0)

    @pl.when(step == 0)
    def _():
        pick = owner_ref[...] == lax.broadcasted_iota(jnp.int32, (blocks * HEADS, requests), 1)
        pick = pick.astype(jnp.float32).astype(jnp.bfloat16)
        own = jnp.dot(pick, qkv_ref[...], preferred_element_type=jnp.float32)
        own = own.reshape(blocks, HEADS, 3 * columns)
        rows = jnp.where(head_mask[None], own[:, :, :columns], 0.0)
        rows_q[...] = rows.reshape(blocks * HEADS, columns).astype(jnp.bfloat16)
        fresh[...] = own[:, 0, columns:]

    rows = group * HEADS
    seen = seen_ref[pl.ds(step * rows, rows), :]
    slots = slot_ref[pl.ds(step * rows, rows), :]
    token = lax.broadcasted_iota(jnp.int32, (tokens, columns), 0)
    keys, values = [], []
    for g in range(group):
        b = step * group + g
        hit = token == slots[g * HEADS : g * HEADS + 1, 0:1]
        row = fresh[pl.ds(b, 1), :]
        key = jnp.where(hit, row[:, :columns], cache_ref[g, 0].astype(jnp.float32))
        value = jnp.where(hit, row[:, columns:], cache_ref[g, 1].astype(jnp.float32))
        keys.append(key.astype(jnp.bfloat16))
        values.append(value.astype(jnp.bfloat16))
        updated_ref[g, 0] = keys[-1]
        updated_ref[g, 1] = values[-1]
    keys = jnp.concatenate(keys, axis=0)
    values = jnp.concatenate(values, axis=0)
    scores = lax.dot_general(
        rows_q[pl.ds(pl.multiple_of(step * rows, rows), rows), :],
        keys,
        (((1,), (1,)), ((), ())),
        preferred_element_type=jnp.float32,
    )
    column = lax.broadcasted_iota(jnp.int32, scores.shape, 1)
    row = lax.broadcasted_iota(jnp.int32, scores.shape, 0)
    visible = (column // tokens == row // HEADS) & (column % tokens < seen)
    masked = jnp.where(visible, scores, NEG_FLOOR)
    top = jnp.max(masked, axis=1, keepdims=True)
    weights = jnp.where(visible, jnp.exp(masked - top), 0.0).astype(jnp.bfloat16)
    mass = jnp.sum(weights.astype(jnp.float32), axis=1, keepdims=True)
    part = jnp.dot(weights, values, preferred_element_type=jnp.float32)
    part = part * jnp.where(mass > 0.0, 1.0 / mass, 0.0)
    part = jnp.where(head_mask[None], part.reshape(group, HEADS, columns), 0.0)
    part = jnp.sum(part, axis=1)
    lane = lax.broadcasted_iota(jnp.int32, (rows, LANES), 1)
    head = lax.broadcasted_iota(jnp.int32, (rows, LANES), 0) % HEADS
    stat = jnp.zeros((rows, LANES), jnp.float32)
    for j, term in enumerate(split3(top) + split3(mass)):
        stat = jnp.where(lane == head + j * HEADS, term, stat)
    owner = owner_ref[pl.ds(step * rows, rows), :].astype(jnp.float32)
    stat = jnp.where((lane == 6 * HEADS) & (head == 0), owner, stat)
    stat = jnp.sum(stat.reshape(group, HEADS, LANES), axis=1)
    sums[step, :, :columns] = part
    sums[step, :, columns:] = stat

    @pl.when(step == pl.num_programs(0) - 1)
    def _():
        whole = sums[...].reshape(blocks, columns + LANES).astype(jnp.bfloat16)
        for d in range(peers):
            out_ref[d] = whole


def output_kernel(place_ref, recv_ref, w_ref, states_ref, own_ref, *rest):
    sends, product = rest[:-1], rest[-1]
    heads = 8
    peers, blocks, wide = recv_ref.shape
    columns = wide - LANES
    requests = states_ref.shape[0]
    total_blocks = peers * blocks
    both = recv_ref[...].astype(jnp.float32).reshape(total_blocks, wide).astype(jnp.bfloat16)
    parts, stat = both[:, :columns], both[:, columns:]
    row = lax.broadcasted_iota(jnp.int32, (3 * heads, LANES), 0)
    lane = lax.broadcasted_iota(jnp.int32, (3 * heads, LANES), 1)
    wanted = (row // heads == lane // (3 * heads)) & (row % heads == lane % heads)
    wanted = (wanted & (row < 2 * heads)) | ((row >= 2 * heads) & (lane == 6 * heads))
    stat = lax.dot_general(
        wanted.astype(jnp.float32).astype(jnp.bfloat16),
        stat,
        (((1,), (1,)), ((), ())),
        preferred_element_type=jnp.float32,
    )
    owner = stat[2 * heads : 2 * heads + 1]
    request = lax.broadcasted_iota(jnp.int32, (requests, total_blocks), 0).astype(jnp.float32)
    member = owner == request
    lane_head = lax.broadcasted_iota(jnp.int32, (requests, columns), 1) // HEAD_DIM
    attended = jnp.zeros((requests, columns), jnp.float32)
    for h in range(heads):
        top = jnp.where(member, stat[h : h + 1], NEG_FLOOR)
        highest = jnp.max(top, axis=1, keepdims=True)
        factor = jnp.where(member, jnp.exp(top - highest) * stat[heads + h : heads + h + 1], 0.0)
        factor = factor / jnp.sum(factor, axis=1, keepdims=True)
        joined = jnp.dot(factor.astype(jnp.bfloat16), parts, preferred_element_type=jnp.float32)
        attended = jnp.where(lane_head == h, joined, attended)
    product[...] = jnp.dot(
        attended.astype(jnp.bfloat16), w_ref[...], preferred_element_type=jnp.float32
    )
    place = place_ref[0]
    share = own_ref.shape[0]
    mine = pl.ds(pl.multiple_of(place * share, share), share)
    own_ref[...] = product[mine, :] + states_ref[mine, :].astype(jnp.float32)
    for m, send in enumerate(sends, 1):
        theirs = pl.ds(pl.multiple_of((place ^ m) * share, share), share)
        send[...] = product[theirs, :].astype(send.dtype)


def shards(states, norm_gain, w_qkv, w_out, cache, context_len, block_owner, block_index):
    requests, depth = states.shape
    peers = lax.axis_size("seq")
    ranks = lax.axis_size("tp")
    parts, _, columns = w_qkv.shape
    blocks, _, tokens, _ = cache.shape
    heads = columns // HEAD_DIM
    share = requests // peers
    out_columns = w_out.shape[1]
    limit = pltpu.CompilerParams(vmem_limit_bytes=40 * 1024 * 1024)

    terms = pl.pallas_call(
        project_kernel,
        out_shape=jax.ShapeDtypeStruct((peers, share, parts * columns + LANES), jnp.bfloat16),
        in_specs=[
            pl.BlockSpec(memory_space=VMEM),
            pl.BlockSpec(memory_space=VMEM),
            pl.BlockSpec(memory_space=pl.ANY),
        ],
        out_specs=pl.BlockSpec(memory_space=VMEM),
        scratch_shapes=[
            pltpu.VMEM((parts, depth, columns), jnp.bfloat16),
            pltpu.SemaphoreType.DMA((parts,)),
        ],
        compiler_params=limit,
        name="project",
    )(states, norm_gain.reshape(1, depth), w_qkv)
    received = lax.all_to_all(terms, "seq", split_axis=0, concat_axis=0, tiled=True)

    positions = lax.dynamic_slice_in_dim(context_len, lax.axis_index("seq") * share, share) - 1
    half = HEAD_DIM // 2
    pair = (jnp.arange(columns, dtype=jnp.int32) % half).astype(jnp.float32)
    frequency = 10000.0 ** (-pair * 2.0 / HEAD_DIM)
    angles = positions.astype(jnp.float32)[:, None] * frequency[None, :]
    shown = pl.pallas_call(
        functools.partial(finish_kernel, depth * peers),
        out_shape=jax.ShapeDtypeStruct((peers, share, parts * columns), jnp.bfloat16),
        compiler_params=limit,
        name="finish",
    )(received, jnp.cos(angles), jnp.sin(angles))
    qkv = lax.all_to_all(shown, "seq", split_axis=0, concat_axis=0, tiled=True)
    qkv = qkv.reshape(requests, parts * columns)

    live = block_owner < requests
    length = context_len[jnp.minimum(block_owner, requests - 1)]
    seen = jnp.where(live, jnp.clip(length - block_index * tokens, 0, tokens), 0)
    last = live & (block_index == (length - 1) // tokens)
    slot = jnp.where(last, (length - 1) % tokens, -1)

    def by_head(value):
        return jnp.repeat(value.astype(jnp.int32), heads)[:, None]

    steps = blocks // GROUP
    joined = pl.BlockSpec((GROUP, 2, tokens, columns), lambda i: (i, 0, 0, 0))
    whole = [
        pl.BlockSpec((requests, parts * columns), lambda i: (0, 0)),
        pl.BlockSpec((blocks * heads, 1), lambda i: (0, 0)),
        pl.BlockSpec((blocks * heads, 1), lambda i: (0, 0)),
        pl.BlockSpec((blocks * heads, 1), lambda i: (0, 0)),
    ]
    partial_rows, updated = pl.pallas_call(
        attend_kernel,
        grid=(steps,),
        out_shape=(
            jax.ShapeDtypeStruct((peers, blocks, columns + LANES), jnp.bfloat16),
            jax.ShapeDtypeStruct(cache.shape, cache.dtype),
        ),
        in_specs=whole + [joined],
        out_specs=(
            pl.BlockSpec((peers, blocks, columns + LANES), lambda i: (0, 0, 0)),
            joined,
        ),
        scratch_shapes=[
            pltpu.VMEM((blocks * heads, columns), jnp.bfloat16),
            pltpu.VMEM((blocks, 2 * columns), jnp.float32),
            pltpu.VMEM((steps, GROUP, columns + LANES), jnp.float32),
        ],
        compiler_params=limit,
        name="attend",
    )(qkv, by_head(block_owner), by_head(seen), by_head(slot), cache)
    gathered = lax.all_to_all(partial_rows, "seq", split_axis=0, concat_axis=0, tiled=True)

    place = lax.axis_index("tp")
    rows = requests // ranks
    own, *sends = pl.pallas_call(
        output_kernel,
        out_shape=tuple(
            jax.ShapeDtypeStruct((rows, out_columns), jnp.float32) for _ in range(ranks)
        ),
        in_specs=[pl.BlockSpec(memory_space=pltpu.MemorySpace.SMEM)]
        + [pl.BlockSpec(memory_space=VMEM)] * 3,
        out_specs=tuple(pl.BlockSpec(memory_space=VMEM) for _ in range(ranks)),
        scratch_shapes=[pltpu.VMEM((requests, out_columns), jnp.float32)],
        compiler_params=limit,
        name="output",
    )(place.reshape(1).astype(jnp.int32), gathered, w_out, states)
    total = own
    for m, send in enumerate(sends, 1):
        total = total + lax.ppermute(send, "tp", [(i, i ^ m) for i in range(ranks)])
    return (total.astype(jnp.bfloat16), updated)


def solution(mesh):
    return jax.shard_map(
        shards,
        mesh=mesh,
        in_specs=(
            P(None, "seq"),
            P("seq"),
            P(None, "seq", "tp"),
            P("tp", "seq"),
            P("seq", None, None, "tp"),
            P(),
            P("seq"),
            P("seq"),
        ),
        out_specs=(P("tp", "seq"), P("seq", None, None, "tp")),
        check_vma=False,
    )
```

time: 224 us -> 65.9 us (0.29)
  waiting for transfers between devices: 96.3 us -> 28.1 us
  blocking collectives: 53.7 us -> 0 us
  local copies, waits for them, and re-layouts: 25.5 us -> 7.82 us
  between operations: 14.3 us -> 0.75 us
  matrix products: 10.6 us -> 0 us
  Pallas kernels: 0 us -> 9.79 us
  other arithmetic: 9.27 us -> 2.2 us
  starting transfers between devices: 13.1 us -> 16.6 us
    psum x1 -> x0, waiting for transfers between devices: 66.5 us -> none  [shards(): projected = lax.psum(local_term, 'seq')]
    all_gather x1 -> x0, blocking collectives: 30.5 us -> none  [shards(): lax.all_gather(share_attended, 'seq', axis=0, tiled=True)]
    psum x1 -> x0, blocking collectives: 23.1 us -> none  [shards(): sum_squares = lax.psum(jnp.sum(wide_states * wide_states, axis=1), 'seq')]
    reduce_scatter x1 -> x0, waiting for transfers between devices: 17.6 us -> none  [shards(): summed = lax.psum_scatter(terms, 'tp', scatter_dimension=0, tiled=True)]
    another operation x5 -> x3, local copies, waits for them, and re-layouts: 13.2 us -> 0.26 us  [by_head(): return jnp.repeat(value.astype(jnp.int32), heads)[:, None]]
    all_to_all x3, waiting for transfers between devices: 12.3 us -> 25.2 us  [the longest x1 10.2 us: shards(): lax.all_to_all(partial_rows, 'seq', split_axis=0, concat_axis=0, tiled=True)]
    dot_general x6 -> x0, matrix products: 10.6 us -> none  [the longest x1 3.59 us: shards(): jnp.einsum('bhd,bthd->bht', query_rows, key_cache, preferred_element_type...]
    pallas_call x0 -> x4, Pallas kernels: none -> 9.79 us  [the longest x1 5.75 us: shards(): pl.pallas_call(attend_kernel, grid=(steps,), out_shape=(jax.ShapeDtypeStr...]
  transfers between devices with their start and end apart: 5 -> 6, of which waited for: 4 -> 5; matrix products, arithmetic and copies ran while one was open for 7% -> 6% of each run, Pallas kernels for 0% -> 0%
where the time goes in v1:
time: 65.9 us; the launch traced here: 65.3 us
  waiting for transfers between devices  28.1 us (43%)
  starting transfers between devices  16.6 us (25%)
  Pallas kernels  9.79 us (15%)
  local copies, waits for them, and re-layouts  7.82 us (12%)
  other arithmetic  2.2 us (3%)
  between operations  0.75 us (1%)
    all_to_all x1, waiting for transfers between devices, shards(): lax.all_to_all(partial_rows, 'seq', split_axis=0, concat_axis=0, tiled=True)  10.2 us
    all_to_all x1, waiting for transfers between devices, shards(): lax.all_to_all(terms, 'seq', split_axis=0, concat_axis=0, tiled=True)  9.05 us
    all_to_all x1, starting transfers between devices, shards(): lax.all_to_all(terms, 'seq', split_axis=0, concat_axis=0, tiled=True)  7.43 us
    all_to_all x1, waiting for transfers between devices, shards(): qkv = lax.all_to_all(shown, 'seq', split_axis=0, concat_axis=0, tiled=True)  5.93 us
    pallas_call x1, Pallas kernels, shards(): pl.pallas_call(attend_kernel, grid=(steps,), out_shape=(jax.ShapeDtypeStr...  5.75 us
    unnamed x14, local copies, waits for them, and re-layouts  4.63 us
    all_to_all x1, starting transfers between devices, shards(): lax.all_to_all(partial_rows, 'seq', split_axis=0, concat_axis=0, tiled=True)  3.64 us
    all_to_all x1, starting transfers between devices, shards(): qkv = lax.all_to_all(shown, 'seq', split_axis=0, concat_axis=0, tiled=True)  3.59 us
  transfers between devices with their start and end apart: 6, of which 5 were waited for; matrix products, arithmetic and copies ran while one was open for 6% of the time, Pallas kernels for 0%

profile of v1, /device:TPU:0, one launch (start us, length us, event | category | flops | bytes accessed | tf_op | source)
XLA Modules:
  0.0 65.3 jit_solution(11618529321954798309)
XLA Ops:
  0.6 0.0 copy-start.5
  0.7 0.7 %reshape.28.gain_ref = bf16[1,384]{1,0:T(2,128)(2,1)S(1)} reshape(bf16[384]{0:T(512)(128)(2,1)} %param.9) | data formatting | bytes 1536 | tf_op jit(solution)/shard_map/reshape | solution.py:219
  1.3 1.5 %copy-done.1 = bf16[3,384,768]{2,1,0:T(8,128)(2,1)S(1)} copy-done((bf16[3,384,768]{2,1,0:T(8,128)(2,1)S(1)}, bf16[3,384,768]{2,1,0:T(8,128)(2,1)}, u32[]{:S(2)}) %copy-start.1) | copy-done | bytes 1769496
  2.8 0.8 %copy-done.3 = bf16[64,384]{1,0:T(8,128)(2,1)S(1)} copy-done((bf16[64,384]{1,0:T(8,128)(2,1)S(1)}, bf16[64,384]{1,0:T(8,128)(2,1)}, u32[]{:S(2)}) %copy-start.3) | copy-done | bytes 49176
  3.6 1.9 %project.1 = bf16[8,8,2432]{2,1,0:T(8,128)(2,1)} custom-call(bf16[64,384]{1,0:T(8,128)(2,1)S(1)} %copy-done.3, bf16[1,384]{1,0:T(2,128)(2,1)S(1)} %reshape.28.gain_ref, bf16[3,384,768]{2,1,0:T(8,128)(2,1)S(1)} %copy-done.1), custom_call_target="tpu_custom_call" | custom-call | tf_op jit(solution)/shard_map/project/pallas_call | solution.py:204
  5.6 0.0 copy-start.2
  5.6 7.4 %all-to-all-start = ((bf16[8,8,2432]{2,1,0:T(8,128)(2,1)}), bf16[8,8,2432]{2,1,0:T(8,128)(2,1)S(1)}, u32[]{:S(2)}, u32[]{:S(2)}) async-start(bf16[8,8,2432]{2,1,0:T(8,128)(2,1)} %project.1), calls=%async_computation | async-start | bytes 622592 | tf_op jit(solution)/shard_map/all_to_all | solution.py:220
  13.0 0.7 %add_convert_fusion.1 = f32[8]{0:T(128)S(1)} fusion(s32[64]{0:T(128)} %param.13, s32[]{:T(128)S(6)} %select_n.35), kind=kLoop, calls=%fused_computation.22 | loop fusion | flops 16 | bytes 68 | tf_op jit(solution)/shard_map/convert_element_type | solution.py:226
  13.7 0.2 multiply_sine_fusion
  13.9 9.0 %all-to-all-done.recv_ref = bf16[8,8,2432]{2,1,0:T(8,128)(2,1)S(1)} async-done(((bf16[8,8,2432]{2,1,0:T(8,128)(2,1)}), bf16[8,8,2432]{2,1,0:T(8,128)(2,1)S(1)}, u32[]{:S(2)}, u32[]{:S(2)}) %all-to-all-start) | async-done | bytes 311328 | tf_op jit(solution)/shard_map/all_to_all | solution.py:220
  23.0 0.9 %finish.1 = bf16[8,8,2304]{2,1,0:T(8,128)(2,1)} custom-call(bf16[8,8,2432]{2,1,0:T(8,128)(2,1)S(1)} %all-to-all-done.recv_ref, f32[8,768]{1,0:T(8,128)S(1)} %get-tuple-element.15.cos_ref, f32[8,768]{1,0:T(8,128)S(1)} %get-tuple-element.14.sin_ref), custom_call_target="tpu_custom_call" | custom-call | tf_op jit(solution)/shard_map/finish/pallas_call | solution.py:227
  23.9 3.6 %all-to-all-start.1 = ((bf16[8,8,2304]{2,1,0:T(8,128)(2,1)}), bf16[8,8,2304]{2,1,0:T(8,128)(2,1)S(1)}, u32[]{:S(2)}, u32[]{:S(2)}) async-start(bf16[8,8,2304]{2,1,0:T(8,128)(2,1)} %finish.1), calls=%async_computation.1 | async-start | bytes 589824 | tf_op jit(solution)/shard_map/all_to_all | solution.py:233
  27.5 0.7 %compare_select_fusion = s32[24]{0:T(128)S(1)} fusion(s32[24]{0:T(128)} %param.14), kind=kLoop, calls=%fused_computation.14 | loop fusion | flops 96 | bytes 192 | tf_op jit(solution)/shard_map/select_n | solution.py:237
  28.1 1.4 %gather_fusion = s32[24]{0:T(128)S(1)} fusion(s32[64]{0:T(128)} %param.13, s32[1024]{0:T(1024)S(1)} %pad_clamp_fusion), kind=kCustom, calls=%fused_computation | custom fusion | bytes 288 | tf_op jit(solution)/shard_map/gather | solution.py:237
  29.5 0.7 %broadcast_in_dim.17 = s32[24,8]{1,0:T(8,128)S(1)} broadcast(s32[24]{0:T(128)} %param.14), dimensions={0} | broadcast | bytes 864 | tf_op jit(solution)/shard_map/broadcast_in_dim | solution.py:243
  30.2 0.1 broadcast_in_dim_reshape.12.owner_ref
  30.4 0.1 broadcast_in_dim.19
  30.4 0.1 broadcast_in_dim_reshape.13.seen_ref
  30.5 0.1 broadcast_in_dim.20
  30.6 0.1 broadcast_in_dim_reshape.14.slot_ref
  30.7 5.9 %all-to-all-done.1 = bf16[8,8,2304]{2,1,0:T(8,128)(2,1)S(1)} async-done(((bf16[8,8,2304]{2,1,0:T(8,128)(2,1)}), bf16[8,8,2304]{2,1,0:T(8,128)(2,1)S(1)}, u32[]{:S(2)}, u32[]{:S(2)}) %all-to-all-start.1) | async-done | bytes 294944 | tf_op jit(solution)/shard_map/all_to_all | solution.py:233
  36.6 2.3 %copy-done = bf16[24,2,64,768]{3,2,1,0:T(8,128)(2,1)S(1)} copy-done((bf16[24,2,64,768]{3,2,1,0:T(8,128)(2,1)S(1)}, bf16[24,2,64,768]{3,2,1,0:T(8,128)(2,1)}, u32[]{:S(2)}) %copy-start) | copy-done | bytes 4718616
  39.0 5.7 %attend.1 = (bf16[8,24,896]{2,1,0:T(8,128)(2,1)}, bf16[24,2,64,768]{3,2,1,0:T(8,128)(2,1)}) custom-call(bf16[64,2304]{1,0:T(8,128)(2,1)S(1)} %bitcast.2, s32[192,1]{1,0:T(8,128)S(1)} %broadcast_in_dim_reshape.12.owner_ref, s32[192,1]{1,0:T(8,128)S(1)} %broadcast_in_dim_reshape.13.seen_ref, s32[192,1]{1,0:T(8,128)S(1)} %broadcast_in_dim_reshape.14.slot_ref, ...), custom_call_target="tpu_custom_call" | custom-call | tf_op jit(solution)/shard_map/attend/pallas_call | solution.py:253
  44.7 3.6 %all-to-all-start.2 = ((bf16[8,24,896]{2,1,0:T(8,128)(2,1)}), bf16[8,24,896]{2,1,0:T(8,128)(2,1)S(1)}, u32[]{:S(2)}, u32[]{:S(2)}) async-start(bf16[8,24,896]{2,1,0:T(8,128)(2,1)} %get-tuple-element.8), calls=%async_computation.2 | async-start | bytes 688128 | tf_op jit(solution)/shard_map/all_to_all | solution.py:273
  48.4 10.2 %all-to-all-done.2.recv_ref = bf16[8,24,896]{2,1,0:T(8,128)(2,1)S(1)} async-done(((bf16[8,24,896]{2,1,0:T(8,128)(2,1)}), bf16[8,24,896]{2,1,0:T(8,128)(2,1)S(1)}, u32[]{:S(2)}, u32[]{:S(2)}) %all-to-all-start.2) | async-done | bytes 344096 | tf_op jit(solution)/shard_map/all_to_all | solution.py:273
  58.5 1.2 %output.1 = (f32[16,384]{1,0:T(8,128)S(1)}, f32[16,384]{1,0:T(8,128)S(1)}, f32[16,384]{1,0:T(8,128)S(1)}, f32[16,384]{1,0:T(8,128)S(1)}) custom-call(s32[1]{0:T(128)} %bitcast.place_ref, bf16[8,24,896]{2,1,0:T(8,128)(2,1)S(1)} %all-to-all-done.2.recv_ref, bf16[768,384]{1,0:T(8,128)(2,1)S(1)} %copy-done.2, bf16[64,384]{1,0:T(8,128)(2,1)S(1)} %copy-done.4), custom_call_target="tpu_custom_call" | custom-call | tf_op jit(solution)/shard_map/output/pallas_call | solution.py:277
  59.8 0.1 collective-permute-start
  59.8 1.6 %collective-permute-start.1 = (f32[16,384]{1,0:T(8,128)S(1)}, f32[16,384]{1,0:T(8,128)S(1)}, u32[]{:S(2)}, u32[]{:S(2)}) collective-permute-start(f32[16,384]{1,0:T(8,128)S(1)} %get-tuple-element.11), channel_id=1, source_target_pairs={{0,2},{1,3},{2,0},{3,1},{4,6},{5,7},{6,4},{7,5},{8,10},{9,11},{10,... | collective-permute-start | bytes 73736 | tf_op jit(solution)/shard_map/ppermute | solution.py:291
  61.4 0.3 collective-permute-start.2
  61.7 2.0 %collective-permute-done.1 = f32[16,384]{1,0:T(8,128)S(1)} collective-permute-done((f32[16,384]{1,0:T(8,128)S(1)}, f32[16,384]{1,0:T(8,128)S(1)}, u32[]{:S(2)}, u32[]{:S(2)}) %collective-permute-start.1) | collective-permute-done | bytes 24608 | tf_op jit(solution)/shard_map/ppermute | solution.py:291
  63.7 0.9 %collective-permute-done.2 = f32[16,384]{1,0:T(8,128)S(1)} collective-permute-done((f32[16,384]{1,0:T(8,128)S(1)}, f32[16,384]{1,0:T(8,128)S(1)}, u32[]{:S(2)}, u32[]{:S(2)}) %collective-permute-start.2) | collective-permute-done | bytes 24608 | tf_op jit(solution)/shard_map/ppermute | solution.py:291
  64.7 0.6 add_convert_fusion
  (13 shorter events, 0.1 us)
Async XLA Ops:
  0.6 29.7 %copy-start.5 = (s32[24]{0:T(128)S(1)}, s32[24]{0:T(128)}, u32[]{:S(2)}) copy-start(s32[24]{0:T(128)} %param.14) | copy-start | bytes 292
  0.6 29.7 %copy-start.6 = (s32[24]{0:T(128)S(1)}, s32[24]{0:T(128)}, u32[]{:S(2)}) copy-start(s32[24]{0:T(128)} %param.15) | copy-start | bytes 292
  1.3 1.5 %copy-start.1 = (bf16[3,384,768]{2,1,0:T(8,128)(2,1)S(1)}, bf16[3,384,768]{2,1,0:T(8,128)(2,1)}, u32[]{:S(2)}) copy-start(bf16[3,384,768]{2,1,0:T(8,128)(2,1)} %w_ref.2) | copy-start | bytes 5308420
  2.8 0.8 %copy-start.3 = (bf16[64,384]{1,0:T(8,128)(2,1)S(1)}, bf16[64,384]{1,0:T(8,128)(2,1)}, u32[]{:S(2)}) copy-start(bf16[64,384]{1,0:T(8,128)(2,1)} %states_ref.3) | copy-start | bytes 147460
  5.6 53.0 %copy-start.2 = (bf16[768,384]{1,0:T(8,128)(2,1)S(1)}, bf16[768,384]{1,0:T(8,128)(2,1)}, u32[]{:S(2)}) copy-start(bf16[768,384]{1,0:T(8,128)(2,1)} %w_ref.3) | copy-start | bytes 1769476
  5.6 53.0 %copy-start.4 = (bf16[64,384]{1,0:T(8,128)(2,1)S(1)}, bf16[64,384]{1,0:T(8,128)(2,1)}, u32[]{:S(2)}) copy-start(bf16[64,384]{1,0:T(8,128)(2,1)} %states_ref.3) | copy-start | bytes 147460
  5.6 17.4 %all-to-all-start = ((bf16[8,8,2432]{2,1,0:T(8,128)(2,1)}), bf16[8,8,2432]{2,1,0:T(8,128)(2,1)S(1)}, u32[]{:S(2)}, u32[]{:S(2)}) async-start(bf16[8,8,2432]{2,1,0:T(8,128)(2,1)} %project.1), calls=%async_computation | async-start | bytes 622592 | tf_op jit(solution)/shard_map/all_to_all | solution.py:220
  23.9 12.7 %all-to-all-start.1 = ((bf16[8,8,2304]{2,1,0:T(8,128)(2,1)}), bf16[8,8,2304]{2,1,0:T(8,128)(2,1)S(1)}, u32[]{:S(2)}, u32[]{:S(2)}) async-start(bf16[8,8,2304]{2,1,0:T(8,128)(2,1)} %finish.1), calls=%async_computation.1 | async-start | bytes 589824 | tf_op jit(solution)/shard_map/all_to_all | solution.py:233
  36.6 2.3 %copy-start = (bf16[24,2,64,768]{3,2,1,0:T(8,128)(2,1)S(1)}, bf16[24,2,64,768]{3,2,1,0:T(8,128)(2,1)}, u32[]{:S(2)}) copy-start(bf16[24,2,64,768]{3,2,1,0:T(8,128)(2,1)} %cache_ref.1) | copy-start | bytes 14155780
  44.7 13.8 %all-to-all-start.2 = ((bf16[8,24,896]{2,1,0:T(8,128)(2,1)}), bf16[8,24,896]{2,1,0:T(8,128)(2,1)S(1)}, u32[]{:S(2)}, u32[]{:S(2)}) async-start(bf16[8,24,896]{2,1,0:T(8,128)(2,1)} %get-tuple-element.8), calls=%async_computation.2 | async-start | bytes 688128 | tf_op jit(solution)/shard_map/all_to_all | solution.py:273
  59.8 1.9 %collective-permute-start = (f32[16,384]{1,0:T(8,128)S(1)}, f32[16,384]{1,0:T(8,128)S(1)}, u32[]{:S(2)}, u32[]{:S(2)}) collective-permute-start(f32[16,384]{1,0:T(8,128)S(1)} %get-tuple-element.10), channel_id=1, source_target_pairs={{0,1},{1,0},{2,3},{3,2},{4,5},{5,4},{6,7},{7,6},{8,9},{9,8},{10,11... | collective-permute-start | bytes 73736 | tf_op jit(solution)/shard_map/ppermute | solution.py:291
  59.8 3.9 %collective-permute-start.1 = (f32[16,384]{1,0:T(8,128)S(1)}, f32[16,384]{1,0:T(8,128)S(1)}, u32[]{:S(2)}, u32[]{:S(2)}) collective-permute-start(f32[16,384]{1,0:T(8,128)S(1)} %get-tuple-element.11), channel_id=1, source_target_pairs={{0,2},{1,3},{2,0},{3,1},{4,6},{5,7},{6,4},{7,5},{8,10},{9,11},{10,... | collective-permute-start | bytes 73736 | tf_op jit(solution)/shard_map/ppermute | solution.py:291
  61.4 3.3 %collective-permute-start.2 = (f32[16,384]{1,0:T(8,128)S(1)}, f32[16,384]{1,0:T(8,128)S(1)}, u32[]{:S(2)}, u32[]{:S(2)}) collective-permute-start(f32[16,384]{1,0:T(8,128)S(1)} %get-tuple-element.12), channel_id=1, source_target_pairs={{0,3},{1,2},{2,1},{3,0},{4,7},{5,6},{6,5},{7,4},{8,11},{9,10},{10,... | collective-permute-start | bytes 73736 | tf_op jit(solution)/shard_map/ppermute | solution.py:291

commit v2 on v1

v2 whole, which is shorter than its diff:
```python
import functools

import jax
import jax.numpy as jnp
from jax import lax
from jax.experimental import pallas as pl
from jax.experimental.pallas import tpu as pltpu
from jax.sharding import PartitionSpec as P

HEAD_DIM = 96
EPSILON = 1e-05
NEG_FLOOR = -1e30
LANES = 128
GROUP = 4

VMEM = pltpu.MemorySpace.VMEM
HBM = pltpu.MemorySpace.HBM
SMEM = pltpu.MemorySpace.SMEM
HEADS = 8
ROWS = 16


def split3(value):
    high = value.astype(jnp.bfloat16).astype(jnp.float32)
    rest = value - high
    mid = rest.astype(jnp.bfloat16).astype(jnp.float32)
    low = (rest - mid).astype(jnp.bfloat16).astype(jnp.float32)
    return high, mid, low


def project_kernel(states_ref, gain_ref, w_ref, out_ref, states_buf, gain_buf, w_buf, sems):
    parts = w_ref.shape[0]
    columns = w_ref.shape[2]
    peers, share, _ = out_ref.shape
    small = [
        pltpu.make_async_copy(states_ref, states_buf, sems.at[parts]),
        pltpu.make_async_copy(gain_ref, gain_buf, sems.at[parts + 1]),
    ]
    copies = [pltpu.make_async_copy(w_ref.at[c], w_buf.at[c], sems.at[c]) for c in range(parts)]
    for copy in small + copies:
        copy.start()
    for copy in small:
        copy.wait()
    wide = states_buf[...].astype(jnp.float32)
    gain = gain_buf[...].astype(jnp.float32)
    scaled = (wide * gain.reshape(1, wide.shape[1])).astype(jnp.bfloat16)
    squares = jnp.sum(wide * wide, axis=1, keepdims=True)
    high, mid, low = split3(squares)
    lane = lax.broadcasted_iota(jnp.int32, (wide.shape[0], LANES), 1)
    stat = jnp.where(lane == 0, high, jnp.where(lane == 1, mid, jnp.where(lane == 2, low, 0.0)))
    for d in range(peers):
        out_ref[d, :, parts * columns :] = stat[d * share : (d + 1) * share].astype(jnp.bfloat16)
    for c in range(parts):
        copies[c].wait()
        term = jnp.dot(scaled, w_buf[c], preferred_element_type=jnp.float32)
        for d in range(peers):
            out_ref[d, :, c * columns : (c + 1) * columns] = term[
                d * share : (d + 1) * share
            ].astype(jnp.bfloat16)


def finish_kernel(width, recv_ref, cos_ref, sin_ref, out_ref):
    peers, _, _ = recv_ref.shape
    columns = cos_ref.shape[1]
    total = recv_ref[0].astype(jnp.float32)
    for d in range(1, peers):
        total = total + recv_ref[d].astype(jnp.float32)
    squares = jnp.sum(total[:, 3 * columns :], axis=1, keepdims=True)
    inverse = lax.rsqrt(squares * (1.0 / width) + EPSILON)
    cosine = cos_ref[...]
    sine = sin_ref[...]
    half = HEAD_DIM // 2
    front = lax.broadcasted_iota(jnp.int32, cosine.shape, 1) % HEAD_DIM < half

    def rotated(x):
        other = jnp.where(front, -pltpu.roll(x, columns - half, 1), pltpu.roll(x, half, 1))
        return x * cosine + other * sine

    query = rotated(total[:, :columns] * inverse) * HEAD_DIM ** (-0.5)
    keys_new = rotated(total[:, columns : 2 * columns] * inverse)
    values_new = total[:, 2 * columns : 3 * columns] * inverse
    for d in range(peers):
        out_ref[d, :, :columns] = query.astype(jnp.bfloat16)
        out_ref[d, :, columns : 2 * columns] = keys_new.astype(jnp.bfloat16)
        out_ref[d, :, 2 * columns :] = values_new.astype(jnp.bfloat16)


def stage_kernel(cache_ref, keys_ref, sem):
    copy = pltpu.make_async_copy(cache_ref.at[:, 0], keys_ref, sem)
    copy.start()
    copy.wait()


def read_block(b, owner_ref, index_ref, length_ref, tokens):
    requests = length_ref.shape[0]
    owner = owner_ref[b]
    reach = length_ref[jnp.minimum(owner, requests - 1)] - index_ref[b] * tokens
    live = owner < requests
    seen = jnp.where(live, jnp.clip(reach, 0, tokens), 0)
    slot = jnp.where(live & (reach >= 1) & (reach <= tokens), reach - 1, -1)
    return owner, seen, slot


def plan_kernel(
    tokens, owner_ref, index_ref, length_ref, pick_ref, single_ref, seen_ref, slot_ref, name_ref
):
    blocks = owner_ref.shape[0]
    requests = pick_ref.shape[1]
    padded = single_ref.shape[0]
    lane = lax.broadcasted_iota(jnp.int32, (HEADS, requests), 1)
    sole = lax.broadcasted_iota(jnp.int32, (padded, requests), 0)
    wide = lax.broadcasted_iota(jnp.int32, (padded, requests), 1)
    single = jnp.zeros((padded, requests), jnp.float32)
    picks = []
    for b in range(blocks):
        owner, seen, slot = read_block(b, owner_ref, index_ref, length_ref, tokens)
        here = pl.ds(b * HEADS, HEADS)
        picks.append((lane == owner).astype(jnp.float32))
        single = jnp.where((sole == b) & (wide == owner), 1.0, single)
        seen_ref[here, :] = jnp.full((HEADS, LANES), seen, jnp.int32)
        slot_ref[here, :] = jnp.full((HEADS, LANES), slot, jnp.int32)
        name_ref[here, :] = jnp.full((HEADS, LANES), owner, jnp.int32).astype(jnp.float32)
    pick_ref[...] = jnp.concatenate(picks, axis=0).astype(jnp.bfloat16)
    single_ref[...] = single.astype(jnp.bfloat16)


def attend_kernel(
    qkv_ref, pick_ref, single_ref, seen_ref, slot_ref, name_ref, keys_ref, cache_ref, out_ref, token_ref, near, sems
):
    blocks, _, tokens, columns = cache_ref.shape
    peers = out_ref.shape[0]
    steps = blocks // GROUP
    copies = [
        pltpu.make_async_copy(
            cache_ref.at[pl.ds(step * GROUP, GROUP), 1],
            near.at[pl.ds(step * GROUP, GROUP)],
            sems.at[step],
        )
        for step in range(steps)
    ]
    for copy in copies:
        copy.start()
    token_ref[...] = jnp.zeros_like(token_ref)

    def iota(shape, dim):
        return lax.broadcasted_iota(jnp.int32, shape, dim)

    def one_hot(hit):
        return hit.astype(jnp.float32).astype(jnp.bfloat16)

    rows = blocks * HEADS
    padded = single_ref.shape[0]
    own = jnp.dot(pick_ref[...], qkv_ref[:, :columns], preferred_element_type=jnp.float32)
    head_mask = iota((rows, columns), 1) // HEAD_DIM == iota((rows, columns), 0) % HEADS
    queries = jnp.where(head_mask, own, 0.0).astype(jnp.bfloat16)
    fresh = jnp.dot(single_ref[...], qkv_ref[:, columns:], preferred_element_type=jnp.float32)
    fresh = fresh.astype(jnp.bfloat16)
    contract = (((1,), (1,)), ((), ()))
    mine = iota((rows, padded), 1) == iota((rows, padded), 0) // HEADS
    newest = lax.dot_general(
        queries, fresh[:, :columns], contract, preferred_element_type=jnp.float32
    )
    newest = jnp.sum(jnp.where(mine, newest, 0.0), axis=1, keepdims=True)

    size = GROUP * HEADS
    width = GROUP * tokens
    scores = []
    for step in range(steps):
        keys = keys_ref[step * GROUP : (step + 1) * GROUP].reshape(width, columns)
        scores.append(
            lax.dot_general(
                queries[step * size : (step + 1) * size],
                keys,
                contract,
                preferred_element_type=jnp.float32,
            )
        )
    scores = jnp.concatenate(scores, axis=0)
    column = iota((rows, width), 1)
    same = column // tokens == iota((rows, width), 0) // HEADS % GROUP
    place = jnp.where(same, column % tokens, tokens)

    def across(value):
        return jnp.concatenate([value] * (width // LANES), axis=1)

    latest = place == across(slot_ref[...])
    visible = place < across(seen_ref[...])
    masked = jnp.where(visible, jnp.where(latest, newest, scores), NEG_FLOOR)
    top = jnp.max(masked, axis=1, keepdims=True)
    weights = jnp.where(visible, jnp.exp(masked - top), 0.0)
    weights = weights.astype(jnp.bfloat16).astype(jnp.float32)
    mass = jnp.sum(weights, axis=1, keepdims=True)
    last = jnp.sum(jnp.where(latest, weights, 0.0), axis=1, keepdims=True)
    weights = jnp.where(latest, 0.0, weights).astype(jnp.bfloat16)
    last = jnp.where(mine, last, 0.0).astype(jnp.bfloat16)
    parts = []
    for step in range(steps):
        copies[step].wait()
        values = near[step * GROUP : (step + 1) * GROUP].reshape(width, columns)
        parts.append(
            jnp.dot(
                weights[step * size : (step + 1) * size],
                values,
                preferred_element_type=jnp.float32,
            )
        )
    part = jnp.concatenate(parts, axis=0)
    part = part + jnp.dot(last, fresh[:, columns:], preferred_element_type=jnp.float32)
    part = part * jnp.where(mass > 0.0, 1.0 / mass, 0.0)
    part = jnp.where(head_mask, part, 0.0).astype(jnp.bfloat16)
    lane = iota((rows, LANES), 1)
    head = iota((rows, LANES), 0) % HEADS
    stat = jnp.where((lane == 6 * HEADS) & (head == 0), name_ref[...], 0.0)
    for j, term in enumerate(split3(top) + split3(mass)):
        stat = jnp.where(lane == head + j * HEADS, term, stat)
    fold = one_hot(iota((padded, rows), 1) // HEADS == iota((padded, rows), 0))
    part = jnp.dot(fold, part, preferred_element_type=jnp.float32)
    stat = jnp.dot(fold, stat.astype(jnp.bfloat16), preferred_element_type=jnp.float32)
    part = part[:blocks].astype(jnp.bfloat16)
    stat = stat[:blocks].astype(jnp.bfloat16)
    for d in range(peers):
        out_ref[d, :, :columns] = part
        out_ref[d, :, columns:] = stat


def append_kernel(
    owner_ref,
    index_ref,
    length_ref,
    qkv_ref,
    token_ref,
    cache_ref,
    updated_ref,
    end_ref,
    wide,
    near,
    loads,
    stores,
):
    blocks, _, tokens, columns = cache_ref.shape
    requests = qkv_ref.shape[0]
    steps = blocks // GROUP

    def load(step):
        part = pl.ds(step * GROUP, GROUP)
        return pltpu.make_async_copy(cache_ref.at[part], near.at[part], loads.at[step])

    def store(step):
        part = pl.ds(step * GROUP, GROUP)
        return pltpu.make_async_copy(near.at[part], updated_ref.at[part], stores.at[step])

    for step in range(steps):
        load(step).start()
    end_ref[...] = jnp.zeros_like(end_ref)
    wide[...] = qkv_ref[:, columns:].astype(jnp.float32)
    row = lax.broadcasted_iota(jnp.int32, (ROWS, columns), 0)

    def change(b, owner, slot):
        first = pl.multiple_of(slot // ROWS * ROWS, ROWS)
        fresh = wide[pl.ds(jnp.minimum(owner, requests - 1), 1), :]
        hit = row == slot - first
        for c in range(2):
            old = near[b, c, pl.ds(first, ROWS), :].astype(jnp.float32)
            both = jnp.where(hit, fresh[:, c * columns : (c + 1) * columns], old)
            near[b, c, pl.ds(first, ROWS), :] = both.astype(jnp.bfloat16)

    for step in range(steps):
        load(step).wait()
        for b in range(step * GROUP, (step + 1) * GROUP):
            owner, _, slot = read_block(b, owner_ref, index_ref, length_ref, tokens)
            pl.when(slot >= 0)(functools.partial(change, b, owner, slot))
        store(step).start()
    for step in range(steps):
        store(step).wait()


def output_kernel(place_ref, token_ref, recv_ref, w_ref, states_ref, own_ref, *rest):
    sends, product = rest[:-1], rest[-1]
    heads = HEADS
    peers, blocks, wide = recv_ref.shape
    columns = wide - LANES
    requests = states_ref.shape[0]
    total_blocks = peers * blocks
    both = recv_ref[...].astype(jnp.float32).reshape(total_blocks, wide).astype(jnp.bfloat16)
    parts, stat = both[:, :columns], both[:, columns:]
    row = lax.broadcasted_iota(jnp.int32, (3 * heads, LANES), 0)
    lane = lax.broadcasted_iota(jnp.int32, (3 * heads, LANES), 1)
    wanted = (row // heads == lane // (3 * heads)) & (row % heads == lane % heads)
    wanted = (wanted & (row < 2 * heads)) | ((row >= 2 * heads) & (lane == 6 * heads))
    stat = lax.dot_general(
        wanted.astype(jnp.float32).astype(jnp.bfloat16),
        stat,
        (((1,), (1,)), ((), ())),
        preferred_element_type=jnp.float32,
    )
    owner = stat[2 * heads : 2 * heads + 1]
    request = lax.broadcasted_iota(jnp.int32, (requests, total_blocks), 0).astype(jnp.float32)
    member = owner == request
    lane_head = lax.broadcasted_iota(jnp.int32, (requests, columns), 1) // HEAD_DIM
    attended = jnp.zeros((requests, columns), jnp.float32)
    for h in range(heads):
        top = jnp.where(member, stat[h : h + 1], NEG_FLOOR)
        highest = jnp.max(top, axis=1, keepdims=True)
        factor = jnp.where(member, jnp.exp(top - highest) * stat[heads + h : heads + h + 1], 0.0)
        factor = factor / jnp.sum(factor, axis=1, keepdims=True)
        joined = jnp.dot(factor.astype(jnp.bfloat16), parts, preferred_element_type=jnp.float32)
        attended = jnp.where(lane_head == h, joined, attended)
    product[...] = jnp.dot(
        attended.astype(jnp.bfloat16), w_ref[...], preferred_element_type=jnp.float32
    )
    place = place_ref[0]
    share = own_ref.shape[0]
    mine = pl.ds(pl.multiple_of(place * share, share), share)
    own_ref[...] = product[mine, :] + states_ref[mine, :].astype(jnp.float32)
    for m, send in enumerate(sends, 1):
        theirs = pl.ds(pl.multiple_of((place ^ m) * share, share), share)
        send[...] = product[theirs, :].astype(send.dtype)


def shards(states, norm_gain, w_qkv, w_out, cache, context_len, block_owner, block_index):
    requests, depth = states.shape
    peers = lax.axis_size("seq")
    ranks = lax.axis_size("tp")
    parts, _, columns = w_qkv.shape
    blocks, _, tokens, _ = cache.shape
    share = requests // peers
    out_columns = w_out.shape[1]
    limit = pltpu.CompilerParams(vmem_limit_bytes=24 * 1024 * 1024)
    most_room = pltpu.CompilerParams(vmem_limit_bytes=50 * 1024 * 1024)
    all_room = pltpu.CompilerParams(vmem_limit_bytes=60 * 1024 * 1024)

    terms = pl.pallas_call(
        project_kernel,
        out_shape=jax.ShapeDtypeStruct((peers, share, parts * columns + LANES), jnp.bfloat16),
        in_specs=[pl.BlockSpec(memory_space=HBM)] * 3,
        out_specs=pl.BlockSpec(memory_space=VMEM),
        scratch_shapes=[
            pltpu.VMEM(states.shape, jnp.bfloat16),
            pltpu.VMEM(norm_gain.shape, jnp.bfloat16),
            pltpu.VMEM((parts, depth, columns), jnp.bfloat16),
            pltpu.SemaphoreType.DMA((parts + 2,)),
        ],
        compiler_params=all_room,
        name="project",
    )(states, norm_gain, w_qkv)
    received = lax.all_to_all(terms, "seq", split_axis=0, concat_axis=0, tiled=True)

    positions = lax.dynamic_slice_in_dim(context_len, lax.axis_index("seq") * share, share) - 1
    half = HEAD_DIM // 2
    pair = (jnp.arange(columns, dtype=jnp.int32) % half).astype(jnp.float32)
    frequency = 10000.0 ** (-pair * 2.0 / HEAD_DIM)
    angles = positions.astype(jnp.float32)[:, None] * frequency[None, :]
    shown = pl.pallas_call(
        functools.partial(finish_kernel, depth * peers),
        out_shape=jax.ShapeDtypeStruct((peers, share, parts * columns), jnp.bfloat16),
        compiler_params=limit,
        name="finish",
    )(received, jnp.cos(angles), jnp.sin(angles))
    qkv = lax.all_to_all(shown, "seq", split_axis=0, concat_axis=0, tiled=True)
    qkv = qkv.reshape(requests, parts * columns)

    table = (block_owner, block_index, context_len)
    padded = blocks + -blocks % 16
    rows = blocks * HEADS
    plan = pl.pallas_call(
        functools.partial(plan_kernel, tokens),
        out_shape=(
            jax.ShapeDtypeStruct((rows, requests), jnp.bfloat16),
            jax.ShapeDtypeStruct((padded, requests), jnp.bfloat16),
            jax.ShapeDtypeStruct((rows, LANES), jnp.int32),
            jax.ShapeDtypeStruct((rows, LANES), jnp.int32),
            jax.ShapeDtypeStruct((rows, LANES), jnp.float32),
        ),
        in_specs=[pl.BlockSpec(memory_space=SMEM)] * 3,
        compiler_params=limit,
        name="plan",
    )(*table)
    keys = pl.pallas_call(
        stage_kernel,
        out_shape=jax.ShapeDtypeStruct((blocks, tokens, columns), cache.dtype),
        in_specs=[pl.BlockSpec(memory_space=HBM)],
        out_specs=pl.BlockSpec(memory_space=VMEM),
        scratch_shapes=[pltpu.SemaphoreType.DMA],
        compiler_params=most_room,
        name="stage",
    )(cache)
    partial_rows, token = pl.pallas_call(
        attend_kernel,
        out_shape=(
            jax.ShapeDtypeStruct((peers, blocks, columns + LANES), jnp.bfloat16),
            jax.ShapeDtypeStruct((8, LANES), jnp.float32),
        ),
        in_specs=[pl.BlockSpec(memory_space=VMEM)] * 7 + [pl.BlockSpec(memory_space=HBM)],
        scratch_shapes=[
            pltpu.VMEM((blocks, tokens, columns), jnp.bfloat16),
            pltpu.SemaphoreType.DMA((blocks // GROUP,)),
        ],
        compiler_params=most_room,
        name="attend",
    )(qkv, *plan, keys, cache)
    updated, token = pl.pallas_call(
        append_kernel,
        out_shape=(
            jax.ShapeDtypeStruct(cache.shape, cache.dtype),
            jax.ShapeDtypeStruct((8, LANES), jnp.float32),
        ),
        in_specs=[pl.BlockSpec(memory_space=SMEM)] * 3
        + [pl.BlockSpec(memory_space=VMEM), pl.BlockSpec(memory_space=pl.ANY)]
        + [pl.BlockSpec(memory_space=HBM)],
        out_specs=(pl.BlockSpec(memory_space=HBM), pl.BlockSpec(memory_space=VMEM)),
        scratch_shapes=[
            pltpu.VMEM((requests, 2 * columns), jnp.float32),
            pltpu.VMEM(cache.shape, jnp.bfloat16),
            pltpu.SemaphoreType.DMA((blocks // GROUP,)),
            pltpu.SemaphoreType.DMA((blocks // GROUP,)),
        ],
        compiler_params=most_room,
        cost_estimate=pl.CostEstimate(flops=0, bytes_accessed=2 * cache.size * 2, transcendentals=0),
        name="append",
    )(*table, qkv, token, cache)
    gathered = lax.all_to_all(partial_rows, "seq", split_axis=0, concat_axis=0, tiled=True)

    place = lax.axis_index("tp")
    kept = requests // ranks
    own, *sends = pl.pallas_call(
        output_kernel,
        out_shape=tuple(
            jax.ShapeDtypeStruct((kept, out_columns), jnp.float32) for _ in range(ranks)
        ),
        in_specs=[pl.BlockSpec(memory_space=SMEM), pl.BlockSpec(memory_space=pl.ANY)]
        + [pl.BlockSpec(memory_space=VMEM)] * 3,
        out_specs=tuple(pl.BlockSpec(memory_space=VMEM) for _ in range(ranks)),
        scratch_shapes=[pltpu.VMEM((requests, out_columns), jnp.float32)],
        compiler_params=limit,
        name="output",
    )(place.reshape(1).astype(jnp.int32), token, gathered, w_out, states)
    total = own
    for m, send in enumerate(sends, 1):
        total = total + lax.ppermute(send, "tp", [(i, i ^ m) for i in range(ranks)])
    return (total.astype(jnp.bfloat16), updated)


def solution(mesh):
    return jax.shard_map(
        shards,
        mesh=mesh,
        in_specs=(
            P(None, "seq"),
            P("seq"),
            P(None, "seq", "tp"),
            P("tp", "seq"),
            P("seq", None, None, "tp"),
            P(),
            P("seq"),
            P("seq"),
        ),
        out_specs=(P("tp", "seq"), P("seq", None, None, "tp")),
        check_vma=False,
    )
```

time: 65.9 us -> 59.6 us (0.904)
  local copies, waits for them, and re-layouts: 7.82 us -> 0.03 us
  Pallas kernels: 9.79 us -> 15.6 us
  waiting for transfers between devices: 28.1 us -> 24.5 us
  other arithmetic: 2.2 us -> 1.52 us
    pallas_call x2 -> x5, Pallas kernels: 6.95 us -> 12.1 us  [the longest x1 4.43 us: shards(): pl.pallas_call(append_kernel, out_shape=(jax.ShapeDtypeStruct(cache.shape...]
    unnamed x14 -> x10, local copies, waits for them, and re-layouts: 4.63 us -> 0.03 us
    all_to_all x1, waiting for transfers between devices: 10.2 us -> 5.75 us  [shards(): lax.all_to_all(partial_rows, 'seq', split_axis=0, concat_axis=0, tiled=True)]
    gather x1 -> x0, local copies, waits for them, and re-layouts: 1.35 us -> none  [shards(): length = context_len[jnp.minimum(block_owner, requests - 1)]]
    broadcast_in_dim x3 -> x0, local copies, waits for them, and re-layouts: 0.87 us -> none  [by_head(): return jnp.repeat(value.astype(jnp.int32), heads)[:, None]]
    all_to_all x1, waiting for transfers between devices: 5.93 us -> 6.74 us  [shards(): qkv = lax.all_to_all(shown, 'seq', split_axis=0, concat_axis=0, tiled=True)]
    reshape x1 -> x0, local copies, waits for them, and re-layouts: 0.69 us -> none  [shards(): norm_gain.reshape(1, depth)]
    pallas_call x1, Pallas kernels: 1.92 us -> 2.6 us  [shards(): pl.pallas_call(project_kernel, out_shape=jax.ShapeDtypeStruct((peers, sha...]
  transfers between devices with their start and end apart: 6 -> 6, of which waited for: 5 -> 5; matrix products, arithmetic and copies ran while one was open for 6% -> 2% of each run, Pallas kernels for 0% -> 12%
where the time goes in v2:
time: 59.6 us; the launch traced here: 59.1 us
  waiting for transfers between devices  24.5 us (41%)
  starting transfers between devices  16.7 us (28%)
  Pallas kernels  15.6 us (26%)
  other arithmetic  1.52 us (3%)
  between operations  0.76 us (1%)
    all_to_all x1, waiting for transfers between devices, shards(): lax.all_to_all(terms, 'seq', split_axis=0, concat_axis=0, tiled=True)  9.05 us
    all_to_all x1, starting transfers between devices, shards(): lax.all_to_all(terms, 'seq', split_axis=0, concat_axis=0, tiled=True)  7.42 us
    all_to_all x1, waiting for transfers between devices, shards(): qkv = lax.all_to_all(shown, 'seq', split_axis=0, concat_axis=0, tiled=True)  6.74 us
    all_to_all x1, waiting for transfers between devices, shards(): lax.all_to_all(partial_rows, 'seq', split_axis=0, concat_axis=0, tiled=True)  5.75 us
    pallas_call x1, Pallas kernels, shards(): pl.pallas_call(append_kernel, out_shape=(jax.ShapeDtypeStruct(cache.shape...  4.43 us
    pallas_call x1, Pallas kernels, shards(): pl.pallas_call(attend_kernel, out_shape=(jax.ShapeDtypeStruct((peers, blo...  4.04 us
    all_to_all x1, starting transfers between devices, shards(): lax.all_to_all(partial_rows, 'seq', split_axis=0, concat_axis=0, tiled=True)  3.78 us
    all_to_all x1, starting transfers between devices, shards(): qkv = lax.all_to_all(shown, 'seq', split_axis=0, concat_axis=0, tiled=True)  3.59 us
  transfers between devices with their start and end apart: 6, of which 5 were waited for; matrix products, arithmetic and copies ran while one was open for 2% of the time, Pallas kernels for 12%

profile of v2, /device:TPU:0, one launch (start us, length us, event | category | flops | bytes accessed | tf_op | source)
XLA Modules:
  0.0 59.1 jit_solution(13791035934992502991)
XLA Ops:
  0.6 2.6 %project.1 = bf16[8,8,2432]{2,1,0:T(8,128)(2,1)} custom-call(bf16[64,384]{1,0:T(8,128)(2,1)} %states_ref.3, bf16[384]{0:T(512)(128)(2,1)} %gain_ref.1, bf16[3,384,768]{2,1,0:T(8,128)(2,1)} %w_ref.2), custom_call_target="tpu_custom_call" | custom-call | tf_op jit(solution)/shard_map/project/pallas_call | solution.py:332
  3.2 0.0 copy-start.2
  3.2 0.0 copy-start.3
  3.3 0.0 copy-start.4
  3.3 7.4 %all-to-all-start = ((bf16[8,8,2432]{2,1,0:T(8,128)(2,1)}), bf16[8,8,2432]{2,1,0:T(8,128)(2,1)S(1)}, u32[]{:S(2)}, u32[]{:S(2)}) async-start(bf16[8,8,2432]{2,1,0:T(8,128)(2,1)} %project.1), calls=%async_computation | async-start | bytes 622592 | tf_op jit(solution)/shard_map/all_to_all | solution.py:346
  10.7 0.7 %add_convert_fusion.1 = f32[8]{0:T(128)S(1)} fusion(s32[64]{0:T(128)} %length_ref.3, s32[]{:T(128)S(6)} %select_n.14), kind=kLoop, calls=%fused_computation.12 | loop fusion | flops 16 | bytes 68 | tf_op jit(solution)/shard_map/convert_element_type | solution.py:352
  11.4 0.2 multiply_sine_fusion
  11.6 9.0 %all-to-all-done.recv_ref = bf16[8,8,2432]{2,1,0:T(8,128)(2,1)S(1)} async-done(((bf16[8,8,2432]{2,1,0:T(8,128)(2,1)}), bf16[8,8,2432]{2,1,0:T(8,128)(2,1)S(1)}, u32[]{:S(2)}, u32[]{:S(2)}) %all-to-all-start) | async-done | bytes 311328 | tf_op jit(solution)/shard_map/all_to_all | solution.py:346
  20.7 0.9 %finish.1 = bf16[8,8,2304]{2,1,0:T(8,128)(2,1)} custom-call(bf16[8,8,2432]{2,1,0:T(8,128)(2,1)S(1)} %all-to-all-done.recv_ref, f32[8,768]{1,0:T(8,128)S(1)} %get-tuple-element.29.cos_ref, f32[8,768]{1,0:T(8,128)S(1)} %get-tuple-element.28.sin_ref), custom_call_target="tpu_custom_call" | custom-call | tf_op jit(solution)/shard_map/finish/pallas_call | solution.py:353
  21.6 3.6 %all-to-all-start.1 = ((bf16[8,8,2304]{2,1,0:T(8,128)(2,1)}), bf16[8,8,2304]{2,1,0:T(8,128)(2,1)S(1)}, u32[]{:S(2)}, u32[]{:S(2)}) async-start(bf16[8,8,2304]{2,1,0:T(8,128)(2,1)} %finish.1), calls=%async_computation.1 | async-start | bytes 589824 | tf_op jit(solution)/shard_map/all_to_all | solution.py:359
  25.2 1.7 %stage.1.keys_ref = bf16[24,64,768]{2,1,0:T(8,128)(2,1)S(1)} custom-call(bf16[24,2,64,768]{3,2,1,0:T(8,128)(2,1)} %cache_ref.5), custom_call_target="tpu_custom_call" | custom-call | tf_op jit(solution)/shard_map/stage/pallas_call | solution.py:378
  26.8 0.0 copy-done.2
  26.9 0.0 copy-done.3
  26.9 0.0 copy-done.4
  26.9 0.7 %plan.1 = (bf16[192,64]{1,0:T(8,128)(2,1)S(1)}, bf16[32,64]{1,0:T(8,128)(2,1)S(1)}, s32[192,128]{1,0:T(8,128)S(1)}, s32[192,128]{1,0:T(8,128)S(1)}, f32[192,128]{1,0:T(8,128)S(1)}) custom-call(s32[24]{0:T(128)S(1)} %copy-done.2, s32[24]{0:T(128)S(1)} %copy-done.3, s32[64]{0:T(128)S(1)} %copy-done.4), custom_call_target="tpu_custom_call" | custom-call | tf_op jit(solution)/shard_map/plan/pallas_call | solution.py:365
  27.6 6.7 %all-to-all-done.1 = bf16[8,8,2304]{2,1,0:T(8,128)(2,1)S(1)} async-done(((bf16[8,8,2304]{2,1,0:T(8,128)(2,1)}), bf16[8,8,2304]{2,1,0:T(8,128)(2,1)S(1)}, u32[]{:S(2)}, u32[]{:S(2)}) %all-to-all-start.1) | async-done | bytes 294944 | tf_op jit(solution)/shard_map/all_to_all | solution.py:359
  34.3 4.0 %attend.1 = (bf16[8,24,896]{2,1,0:T(8,128)(2,1)}, f32[8,128]{1,0:T(8,128)S(1)}) custom-call(bf16[64,2304]{1,0:T(8,128)(2,1)S(1)} %bitcast.2, bf16[192,64]{1,0:T(8,128)(2,1)S(1)} %get-tuple-element.15.pick_ref, bf16[32,64]{1,0:T(8,128)(2,1)S(1)} %get-tuple-element.16.single_ref, s32[192,128]{1,0:T(8,128)S(1)} %get-tuple-element.17.seen_ref, ...), custom_call_target="tpu_custom_call" | custom-call | tf_op jit(solution)/shard_map/attend/pallas_call | solution.py:387
  38.4 0.0 copy-start
  38.4 0.0 copy-start.1
  38.4 3.8 %all-to-all-start.2 = ((bf16[8,24,896]{2,1,0:T(8,128)(2,1)}), bf16[8,24,896]{2,1,0:T(8,128)(2,1)S(1)}, u32[]{:S(2)}, u32[]{:S(2)}) async-start(bf16[8,24,896]{2,1,0:T(8,128)(2,1)} %get-tuple-element.22), calls=%async_computation.2 | async-start | bytes 688128 | tf_op jit(solution)/shard_map/all_to_all | solution.py:421
  42.2 4.4 %append.1 = (bf16[24,2,64,768]{3,2,1,0:T(8,128)(2,1)}, f32[8,128]{1,0:T(8,128)S(1)}) custom-call(s32[24]{0:T(128)S(1)} %copy-done.2, s32[24]{0:T(128)S(1)} %copy-done.3, s32[64]{0:T(128)S(1)} %copy-done.4, bf16[64,2304]{1,0:T(8,128)(2,1)S(1)} %bitcast.3, f32[8,128]{1,0:T(8,128)S(1)} %get-tuple-element.20.token_ref, bf16[24,2,64,768]{3,2,1,0:T(8,128)(2,1)} %cache_ref.5), custom_call_target="tpu_custom_call" | custom-call | bytes 9437184 | tf_op jit(solution)/shard_map/append/pallas_call | solution.py:401
  46.6 5.8 %all-to-all-done.2.recv_ref = bf16[8,24,896]{2,1,0:T(8,128)(2,1)S(1)} async-done(((bf16[8,24,896]{2,1,0:T(8,128)(2,1)}), bf16[8,24,896]{2,1,0:T(8,128)(2,1)S(1)}, u32[]{:S(2)}, u32[]{:S(2)}) %all-to-all-start.2) | async-done | bytes 344096 | tf_op jit(solution)/shard_map/all_to_all | solution.py:421
  52.4 0.0 copy-done
  52.4 0.0 copy-done.1
  52.4 1.2 %output.1 = (f32[16,384]{1,0:T(8,128)S(1)}, f32[16,384]{1,0:T(8,128)S(1)}, f32[16,384]{1,0:T(8,128)S(1)}, f32[16,384]{1,0:T(8,128)S(1)}) custom-call(s32[1]{0:T(128)} %bitcast.place_ref, f32[8,128]{1,0:T(8,128)S(1)} %get-tuple-element.21.token_ref, bf16[8,24,896]{2,1,0:T(8,128)(2,1)S(1)} %all-to-all-done.2.recv_ref, bf16[768,384]{1,0:T(8,128)(2,1)S(1)} %copy-done, ...), custom_call_target="tpu_custom_call" | custom-call | tf_op jit(solution)/shard_map/output/pallas_call | solution.py:425
  53.6 0.1 collective-permute-start
  53.7 1.6 %collective-permute-start.1 = (f32[16,384]{1,0:T(8,128)S(1)}, f32[16,384]{1,0:T(8,128)S(1)}, u32[]{:S(2)}, u32[]{:S(2)}) collective-permute-start(f32[16,384]{1,0:T(8,128)S(1)} %get-tuple-element.25), channel_id=1, source_target_pairs={{0,2},{1,3},{2,0},{3,1},{4,6},{5,7},{6,4},{7,5},{8,10},{9,11},{10,... | collective-permute-start | bytes 73736 | tf_op jit(solution)/shard_map/ppermute | solution.py:439
  55.2 0.3 collective-permute-start.2
  55.5 0.0 collective-permute-done
  55.5 2.0 %collective-permute-done.1 = f32[16,384]{1,0:T(8,128)S(1)} collective-permute-done((f32[16,384]{1,0:T(8,128)S(1)}, f32[16,384]{1,0:T(8,128)S(1)}, u32[]{:S(2)}, u32[]{:S(2)}) %collective-permute-start.1) | collective-permute-done | bytes 24608 | tf_op jit(solution)/shard_map/ppermute | solution.py:439
  57.6 0.9 %collective-permute-done.2 = f32[16,384]{1,0:T(8,128)S(1)} collective-permute-done((f32[16,384]{1,0:T(8,128)S(1)}, f32[16,384]{1,0:T(8,128)S(1)}, u32[]{:S(2)}, u32[]{:S(2)}) %collective-permute-start.2) | collective-permute-done | bytes 24608 | tf_op jit(solution)/shard_map/ppermute | solution.py:439
  58.5 0.6 %add_convert_fusion = bf16[16,384]{1,0:T(8,128)(2,1)} fusion(f32[16,384]{1,0:T(8,128)S(1)} %collective-permute-done.2, f32[16,384]{1,0:T(8,128)S(1)} %collective-permute-done.1, f32[16,384]{1,0:T(8,128)S(1)} %get-tuple-element.23, f32[16,384]{1,0:T(8,128)S(1)} %collective-permute-done), kind=kLoop, calls=%fused_computation.2 | loop fusion | flops 24576 | bytes 110592 | tf_op jit(solution)/shard_map/convert_element_type | solution.py:440
  (1 shorter events, 0.0 us)
Async XLA Ops:
  3.2 23.6 %copy-start.2 = (s32[24]{0:T(128)S(1)}, s32[24]{0:T(128)}, u32[]{:S(2)}) copy-start(s32[24]{0:T(128)} %owner_ref.3) | copy-start | bytes 292
  3.2 23.6 %copy-start.3 = (s32[24]{0:T(128)S(1)}, s32[24]{0:T(128)}, u32[]{:S(2)}) copy-start(s32[24]{0:T(128)} %index_ref.3) | copy-start | bytes 292
  3.3 23.6 %copy-start.4 = (s32[64]{0:T(128)S(1)}, s32[64]{0:T(128)}, u32[]{:S(2)}) copy-start(s32[64]{0:T(128)} %length_ref.3) | copy-start | bytes 772
  3.3 17.4 %all-to-all-start = ((bf16[8,8,2432]{2,1,0:T(8,128)(2,1)}), bf16[8,8,2432]{2,1,0:T(8,128)(2,1)S(1)}, u32[]{:S(2)}, u32[]{:S(2)}) async-start(bf16[8,8,2432]{2,1,0:T(8,128)(2,1)} %project.1), calls=%async_computation | async-start | bytes 622592 | tf_op jit(solution)/shard_map/all_to_all | solution.py:346
  21.6 12.7 %all-to-all-start.1 = ((bf16[8,8,2304]{2,1,0:T(8,128)(2,1)}), bf16[8,8,2304]{2,1,0:T(8,128)(2,1)S(1)}, u32[]{:S(2)}, u32[]{:S(2)}) async-start(bf16[8,8,2304]{2,1,0:T(8,128)(2,1)} %finish.1), calls=%async_computation.1 | async-start | bytes 589824 | tf_op jit(solution)/shard_map/all_to_all | solution.py:359
  38.4 14.0 %copy-start = (bf16[768,384]{1,0:T(8,128)(2,1)S(1)}, bf16[768,384]{1,0:T(8,128)(2,1)}, u32[]{:S(2)}) copy-start(bf16[768,384]{1,0:T(8,128)(2,1)} %w_ref.3) | copy-start | bytes 1769476
  38.4 14.0 %copy-start.1 = (bf16[64,384]{1,0:T(8,128)(2,1)S(1)}, bf16[64,384]{1,0:T(8,128)(2,1)}, u32[]{:S(2)}) copy-start(bf16[64,384]{1,0:T(8,128)(2,1)} %states_ref.3) | copy-start | bytes 147460
  38.4 14.0 %all-to-all-start.2 = ((bf16[8,24,896]{2,1,0:T(8,128)(2,1)}), bf16[8,24,896]{2,1,0:T(8,128)(2,1)S(1)}, u32[]{:S(2)}, u32[]{:S(2)}) async-start(bf16[8,24,896]{2,1,0:T(8,128)(2,1)} %get-tuple-element.22), calls=%async_computation.2 | async-start | bytes 688128 | tf_op jit(solution)/shard_map/all_to_all | solution.py:421
  53.6 1.9 %collective-permute-start = (f32[16,384]{1,0:T(8,128)S(1)}, f32[16,384]{1,0:T(8,128)S(1)}, u32[]{:S(2)}, u32[]{:S(2)}) collective-permute-start(f32[16,384]{1,0:T(8,128)S(1)} %get-tuple-element.24), channel_id=1, source_target_pairs={{0,1},{1,0},{2,3},{3,2},{4,5},{5,4},{6,7},{7,6},{8,9},{9,8},{10,11... | collective-permute-start | bytes 73736 | tf_op jit(solution)/shard_map/ppermute | solution.py:439
  53.7 3.9 %collective-permute-start.1 = (f32[16,384]{1,0:T(8,128)S(1)}, f32[16,384]{1,0:T(8,128)S(1)}, u32[]{:S(2)}, u32[]{:S(2)}) collective-permute-start(f32[16,384]{1,0:T(8,128)S(1)} %get-tuple-element.25), channel_id=1, source_target_pairs={{0,2},{1,3},{2,0},{3,1},{4,6},{5,7},{6,4},{7,5},{8,10},{9,11},{10,... | collective-permute-start | bytes 73736 | tf_op jit(solution)/shard_map/ppermute | solution.py:439
  55.2 3.3 %collective-permute-start.2 = (f32[16,384]{1,0:T(8,128)S(1)}, f32[16,384]{1,0:T(8,128)S(1)}, u32[]{:S(2)}, u32[]{:S(2)}) collective-permute-start(f32[16,384]{1,0:T(8,128)S(1)} %get-tuple-element.26), channel_id=1, source_target_pairs={{0,3},{1,2},{2,1},{3,0},{4,7},{5,6},{6,5},{7,4},{8,11},{9,10},{10,... | collective-permute-start | bytes 73736 | tf_op jit(solution)/shard_map/ppermute | solution.py:439

commit v3 on v2

v3 whole, which is shorter than its diff:
```python
import functools

import jax
import jax.numpy as jnp
from jax import lax
from jax.experimental import pallas as pl
from jax.experimental.pallas import tpu as pltpu
from jax.sharding import PartitionSpec as P

HEAD_DIM = 96
EPSILON = 1e-05
NEG_FLOOR = -1e30
LANES = 128
GROUP = 4

VMEM = pltpu.MemorySpace.VMEM
HBM = pltpu.MemorySpace.HBM
SMEM = pltpu.MemorySpace.SMEM
HEADS = 8
ROWS = 16


def split3(value):
    high = value.astype(jnp.bfloat16).astype(jnp.float32)
    rest = value - high
    mid = rest.astype(jnp.bfloat16).astype(jnp.float32)
    low = (rest - mid).astype(jnp.bfloat16).astype(jnp.float32)
    return high, mid, low


def lanes_of(terms):
    lane = lax.broadcasted_iota(jnp.int32, (terms[0].shape[0], LANES), 1)
    out = jnp.zeros(lane.shape, jnp.float32)
    for j, term in enumerate(terms):
        out = jnp.where(lane == j, term, out)
    return out


def project_kernel(
    place_ref, states_ref, gain_ref, w_ref, sent_ref, kept_ref, states_buf, gain_buf, w_buf, sems
):
    parts, _, columns = w_ref.shape
    half = sent_ref.shape[0]
    small = [
        pltpu.make_async_copy(states_ref, states_buf, sems.at[parts]),
        pltpu.make_async_copy(gain_ref, gain_buf, sems.at[parts + 1]),
    ]
    copies = [pltpu.make_async_copy(w_ref.at[c], w_buf.at[c], sems.at[c]) for c in range(parts)]
    for copy in small + copies:
        copy.start()
    for copy in small:
        copy.wait()
    side = place_ref[0] % 2
    rows = [
        states_buf[pl.ds(pl.multiple_of(first * half, half), half), :].astype(jnp.float32)
        for first in (1 - side, side)
    ]
    wide = jnp.concatenate(rows, axis=0)
    gain = gain_buf[...].astype(jnp.float32)
    scaled = (wide * gain.reshape(1, wide.shape[1])).astype(jnp.bfloat16)
    squares = jnp.sum(wide * wide, axis=1, keepdims=True)
    stat = lanes_of(split3(squares))
    sent_ref[:, parts * columns :] = stat[:half].astype(jnp.bfloat16)
    kept_ref[:, parts * columns :] = stat[half:]
    for c in range(parts):
        copies[c].wait()
        term = jnp.dot(scaled, w_buf[c], preferred_element_type=jnp.float32)
        here = slice(c * columns, (c + 1) * columns)
        sent_ref[:, here] = term[:half].astype(jnp.bfloat16)
        kept_ref[:, here] = term[half:]


def halve_kernel(place_ref, kept_ref, recv_ref, after_ref, *rest):
    sends, query_ref, fresh_ref, total = rest[:-3], rest[-3], rest[-2], rest[-1]
    columns = query_ref.shape[1] - LANES
    share = fresh_ref.shape[0]
    half = kept_ref.shape[0]
    total[...] = kept_ref[...] + recv_ref[...].astype(jnp.float32)
    squares = jnp.sum(total[:, 3 * columns :], axis=1, keepdims=True)
    stat = lanes_of(split3(squares))
    query_ref[:, :columns] = total[:, :columns]
    query_ref[:, columns:] = stat
    query = total[:, :columns].astype(jnp.bfloat16)
    stat = stat.astype(jnp.bfloat16)
    line = place_ref[0] // 2

    def rows_of(group):
        return total[pl.ds(pl.multiple_of(group * share, share), share), columns : 3 * columns]

    fresh_ref[...] = rows_of(line)
    for m, send in enumerate(sends, 1):
        other = rows_of(line ^ m)
        both = jnp.concatenate([other[:, :columns], other[:, columns:]], axis=0)
        send[:half, :columns] = query
        send[:half, columns:] = stat
        send[half:, :columns] = both.astype(jnp.bfloat16)
        send[half:, columns:] = jnp.zeros((2 * share, LANES), jnp.bfloat16)


def finish_kernel(width, place_ref, after_ref, query_ref, fresh_ref, cos_ref, sin_ref, *rest):
    received, out_ref, news_ref = rest[:-2], rest[-2], rest[-1]
    half, columns = out_ref.shape
    share = fresh_ref.shape[0]
    total = query_ref[...]
    fresh = fresh_ref[...]
    for piece in received:
        total = total + piece[:half, :].astype(jnp.float32)
        extra = piece[half:, :columns].astype(jnp.float32)
        fresh = fresh + jnp.concatenate([extra[:share], extra[share:]], axis=1)
    squares = jnp.sum(total[:, columns:], axis=1, keepdims=True)
    inverse = lax.rsqrt(squares * (1.0 / width) + EPSILON)
    span = HEAD_DIM // 2

    def rotated(x, cosine, sine):
        front = lax.broadcasted_iota(jnp.int32, x.shape, 1) % HEAD_DIM < span
        other = jnp.where(front, -pltpu.roll(x, columns - span, 1), pltpu.roll(x, span, 1))
        return x * cosine + other * sine

    query = rotated(total[:, :columns] * inverse, cos_ref[...], sin_ref[...])
    query = (query * HEAD_DIM ** (-0.5)).astype(jnp.bfloat16)
    out_ref[...] = query
    line = place_ref[0] // 2
    groups = half // share
    mine = jnp.zeros((share, columns), jnp.float32)
    scale = jnp.zeros((share, 1), jnp.float32)
    cosine, sine = mine, mine
    wide = query.astype(jnp.float32)
    for group in range(groups):
        here = slice(group * share, (group + 1) * share)
        mine = jnp.where(line == group, wide[here], mine)
        scale = jnp.where(line == group, inverse[here], scale)
        cosine = jnp.where(line == group, cos_ref[here, :], cosine)
        sine = jnp.where(line == group, sin_ref[here, :], sine)
    key = rotated(fresh[:, :columns] * scale, cosine, sine).astype(jnp.bfloat16)
    value = (fresh[:, columns:] * scale).astype(jnp.bfloat16)
    product = mine * key.astype(jnp.float32)
    lane_head = lax.broadcasted_iota(jnp.int32, product.shape, 1) // HEAD_DIM
    lane = lax.broadcasted_iota(jnp.int32, (share, LANES), 1)
    first = (place_ref[0] % 2) * half + line * share
    owner = lax.broadcasted_iota(jnp.int32, (share, LANES), 0) + first
    stat = jnp.where(lane == 6 * HEADS, owner.astype(jnp.float32), 0.0)
    for h in range(HEADS):
        score = jnp.sum(jnp.where(lane_head == h, product, 0.0), axis=1, keepdims=True)
        for j, term in enumerate(split3(score)):
            stat = jnp.where(lane == j * HEADS + h, term, stat)
        stat = jnp.where(lane == 3 * HEADS + h, 1.0, stat)
    none = jnp.where(lane == 6 * HEADS, -1.0, 0.0)
    both = jnp.concatenate([value.astype(jnp.float32), key.astype(jnp.float32)], axis=0)
    news_ref[:, :columns] = both.astype(jnp.bfloat16)
    news_ref[:, columns:] = jnp.concatenate([stat, none], axis=0).astype(jnp.bfloat16)


def stage_keys_kernel(cache_ref, keys_ref, updated_ref, loads, stores):
    steps = cache_ref.shape[0] // GROUP

    def load(step):
        part = pl.ds(step * GROUP, GROUP)
        return pltpu.make_async_copy(cache_ref.at[part, 0], keys_ref.at[part], loads.at[step])

    def store(step):
        part = pl.ds(step * GROUP, GROUP)
        return pltpu.make_async_copy(keys_ref.at[part], updated_ref.at[part, 0], stores.at[step])

    for step in range(steps):
        load(step).start()
    for step in range(steps):
        load(step).wait()
        store(step).start()
    for step in range(steps):
        store(step).wait()


def stage_values_kernel(cache_ref, held_ref, updated_ref, near, loads, stores):
    steps = cache_ref.shape[0] // GROUP

    def load(step):
        part = pl.ds(step * GROUP, GROUP)
        return pltpu.make_async_copy(cache_ref.at[part, 1], near.at[part], loads.at[step])

    def store(step):
        part = pl.ds(step * GROUP, GROUP)
        return pltpu.make_async_copy(near.at[part], updated_ref.at[part, 1], stores.at[step])

    for step in range(steps):
        load(step).start()
    for step in range(steps):
        load(step).wait()
        store(step).start()
    for step in range(steps):
        store(step).wait()


def read_block(b, owner_ref, index_ref, length_ref, tokens):
    requests = length_ref.shape[0]
    owner = owner_ref[b]
    reach = length_ref[jnp.minimum(owner, requests - 1)] - index_ref[b] * tokens
    live = owner < requests
    old = jnp.where(live, jnp.clip(reach - 1, 0, tokens), 0)
    slot = jnp.where(live & (reach >= 1) & (reach <= tokens), reach - 1, -1)
    return owner, old, slot


def plan_kernel(
    tokens,
    place_ref,
    owner_ref,
    index_ref,
    length_ref,
    mine_ref,
    other_ref,
    seen_ref,
    name_ref,
):
    blocks = owner_ref.shape[0]
    half = mine_ref.shape[1]
    side = place_ref[0] % 2
    lane = lax.broadcasted_iota(jnp.int32, (HEADS, half), 1)
    picks = [], []
    for b in range(blocks):
        owner, old, _ = read_block(b, owner_ref, index_ref, length_ref, tokens)
        here = pl.ds(b * HEADS, HEADS)
        for pick, first in zip(picks, (side, 1 - side)):
            pick.append((lane == owner - first * half).astype(jnp.float32))
        seen_ref[here, :] = jnp.full((HEADS, LANES), old, jnp.int32)
        name_ref[here, :] = jnp.full((HEADS, LANES), owner, jnp.int32).astype(jnp.float32)
    mine_ref[...] = jnp.concatenate(picks[0], axis=0).astype(jnp.bfloat16)
    other_ref[...] = jnp.concatenate(picks[1], axis=0).astype(jnp.bfloat16)


def attend_kernel(
    mine_ref,
    other_ref,
    pick_mine_ref,
    pick_other_ref,
    seen_ref,
    name_ref,
    news_ref,
    keys_ref,
    cache_ref,
    out_ref,
    near,
    sems,
):
    blocks, _, tokens, columns = cache_ref.shape
    extra = news_ref.shape[0]
    steps = blocks // GROUP
    copies = [
        pltpu.make_async_copy(
            cache_ref.at[pl.ds(step * GROUP, GROUP), 1],
            near.at[pl.ds(step * GROUP, GROUP)],
            sems.at[step],
        )
        for step in range(steps)
    ]
    for copy in copies:
        copy.start()
    out_ref[:extra, :] = news_ref[...]

    def iota(shape, dim):
        return lax.broadcasted_iota(jnp.int32, shape, dim)

    rows = blocks * HEADS
    size = GROUP * HEADS
    width = GROUP * tokens
    own = jnp.dot(pick_mine_ref[...], mine_ref[...], preferred_element_type=jnp.float32)
    own = own + jnp.dot(pick_other_ref[...], other_ref[...], preferred_element_type=jnp.float32)
    head_mask = iota((rows, columns), 1) // HEAD_DIM == iota((rows, columns), 0) % HEADS
    queries = jnp.where(head_mask, own, 0.0).astype(jnp.bfloat16)
    scores = []
    for step in range(steps):
        keys = keys_ref[step * GROUP : (step + 1) * GROUP].reshape(width, columns)
        scores.append(
            lax.dot_general(
                queries[step * size : (step + 1) * size],
                keys,
                (((1,), (1,)), ((), ())),
                preferred_element_type=jnp.float32,
            )
        )
    scores = jnp.concatenate(scores, axis=0)
    column = iota((rows, width), 1)
    same = column // tokens == iota((rows, width), 0) // HEADS % GROUP
    place = jnp.where(same, column % tokens, tokens)
    visible = place < jnp.concatenate([seen_ref[...]] * (width // LANES), axis=1)
    masked = jnp.where(visible, scores, NEG_FLOOR)
    top = jnp.max(masked, axis=1, keepdims=True)
    weights = jnp.where(visible, jnp.exp(masked - top), 0.0).astype(jnp.bfloat16)
    mass = jnp.sum(weights.astype(jnp.float32), axis=1, keepdims=True)
    parts = []
    for step in range(steps):
        copies[step].wait()
        values = near[step * GROUP : (step + 1) * GROUP].reshape(width, columns)
        parts.append(
            jnp.dot(
                weights[step * size : (step + 1) * size],
                values,
                preferred_element_type=jnp.float32,
            )
        )
    part = jnp.concatenate(parts, axis=0) * jnp.where(mass > 0.0, 1.0 / mass, 0.0)
    part = jnp.where(head_mask, part, 0.0).astype(jnp.bfloat16)
    lane = iota((rows, LANES), 1)
    head = iota((rows, LANES), 0) % HEADS
    stat = jnp.where((lane == 6 * HEADS) & (head == 0), name_ref[...], 0.0)
    for j, term in enumerate(split3(top) + split3(mass)):
        stat = jnp.where(lane == head + j * HEADS, term, stat)
    padded = blocks + -blocks % 16
    fold = iota((padded, rows), 1) // HEADS == iota((padded, rows), 0)
    fold = fold.astype(jnp.float32).astype(jnp.bfloat16)
    part = jnp.dot(fold, part, preferred_element_type=jnp.float32)
    stat = jnp.dot(fold, stat.astype(jnp.bfloat16), preferred_element_type=jnp.float32)
    out_ref[extra:, :columns] = part[:blocks].astype(jnp.bfloat16)
    out_ref[extra:, columns:] = stat[:blocks].astype(jnp.bfloat16)


def patch_kernel(count, place_ref, owner_ref, index_ref, length_ref, after_ref, *rest):
    pieces, cache_ref, held_ref, updated_ref = rest[:count], rest[count], rest[count + 1], rest[count + 2]
    fresh, patch, loads, stores = rest[count + 3 :]
    blocks, _, tokens, columns = cache_ref.shape
    requests = length_ref.shape[0]
    share = fresh.shape[1] // 2
    half = requests // 2

    def each(do):
        for b in range(blocks):
            owner, _, slot = read_block(b, owner_ref, index_ref, length_ref, tokens)
            first = pl.multiple_of(jnp.maximum(slot, 0) // ROWS * ROWS, ROWS)
            pl.when(slot >= 0)(functools.partial(do, b, owner, slot, first))

    def fetch(b, owner, slot, first):
        return pltpu.make_async_copy(
            cache_ref.at[b, :, pl.ds(first, ROWS), :], patch.at[b], loads.at[b]
        )

    def store(b, owner, slot, first):
        return pltpu.make_async_copy(
            patch.at[b], updated_ref.at[b, :, pl.ds(first, ROWS), :], stores.at[b]
        )

    each(lambda *at: fetch(*at).start())
    for m in range(count):
        fresh[m] = pieces[m][: 2 * share, :columns].astype(jnp.float32)
    row = lax.broadcasted_iota(jnp.int32, (ROWS, columns), 0)

    def change(b, owner, slot, first):
        fetch(b, owner, slot, first).wait()
        request = jnp.minimum(owner, requests - 1)
        device = request % half // share * 2 + request // half
        piece = place_ref[0] ^ device
        line = request % share
        for c in range(2):
            new = fresh[piece, pl.ds(line + (1 - c) * share, 1), :]
            old = patch[b, c].astype(jnp.float32)
            patch[b, c] = jnp.where(row == slot - first, new, old).astype(jnp.bfloat16)
        store(b, owner, slot, first).start()

    each(change)
    each(lambda *at: store(*at).wait())


def output_kernel(count, place_ref, *rest):
    pieces, w_ref, states_ref, own_ref = rest[:count], rest[count], rest[count + 1], rest[count + 2]
    sends, product = rest[count + 3 : -1], rest[-1]
    heads = HEADS
    blocks, wide = pieces[0].shape
    columns = wide - LANES
    requests = states_ref.shape[0]
    total_blocks = count * blocks
    both = [piece[...].astype(jnp.float32) for piece in pieces]
    both = jnp.concatenate(both, axis=0).astype(jnp.bfloat16)
    parts, stat = both[:, :columns], both[:, columns:]
    row = lax.broadcasted_iota(jnp.int32, (3 * heads, LANES), 0)
    lane = lax.broadcasted_iota(jnp.int32, (3 * heads, LANES), 1)
    wanted = (row // heads == lane // (3 * heads)) & (row % heads == lane % heads)
    wanted = (wanted & (row < 2 * heads)) | ((row >= 2 * heads) & (lane == 6 * heads))
    stat = lax.dot_general(
        wanted.astype(jnp.float32).astype(jnp.bfloat16),
        stat,
        (((1,), (1,)), ((), ())),
        preferred_element_type=jnp.float32,
    )
    owner = stat[2 * heads : 2 * heads + 1]
    request = lax.broadcasted_iota(jnp.int32, (requests, total_blocks), 0).astype(jnp.float32)
    member = owner == request
    lane_head = lax.broadcasted_iota(jnp.int32, (requests, columns), 1) // HEAD_DIM
    attended = jnp.zeros((requests, columns), jnp.float32)
    for h in range(heads):
        top = jnp.where(member, stat[h : h + 1], NEG_FLOOR)
        highest = jnp.max(top, axis=1, keepdims=True)
        factor = jnp.where(member, jnp.exp(top - highest) * stat[heads + h : heads + h + 1], 0.0)
        factor = factor / jnp.sum(factor, axis=1, keepdims=True)
        joined = jnp.dot(factor.astype(jnp.bfloat16), parts, preferred_element_type=jnp.float32)
        attended = jnp.where(lane_head == h, joined, attended)
    product[...] = jnp.dot(
        attended.astype(jnp.bfloat16), w_ref[...], preferred_element_type=jnp.float32
    )
    place = place_ref[0]
    share = own_ref.shape[0]
    mine = pl.ds(pl.multiple_of(place * share, share), share)
    own_ref[...] = product[mine, :] + states_ref[mine, :].astype(jnp.float32)
    for m, send in enumerate(sends, 1):
        theirs = pl.ds(pl.multiple_of((place ^ m) * share, share), share)
        send[...] = product[theirs, :].astype(send.dtype)


def shards(states, norm_gain, w_qkv, w_out, cache, context_len, block_owner, block_index):
    requests, depth = states.shape
    peers = lax.axis_size("seq")
    ranks = lax.axis_size("tp")
    parts, _, columns = w_qkv.shape
    blocks, _, tokens, _ = cache.shape
    half = requests // 2
    share = requests // peers
    lines = peers // 2
    out_columns = w_out.shape[1]
    rows = blocks * HEADS
    steps = blocks // GROUP
    limit = pltpu.CompilerParams(vmem_limit_bytes=24 * 1024 * 1024)
    most_room = pltpu.CompilerParams(vmem_limit_bytes=50 * 1024 * 1024)
    all_room = pltpu.CompilerParams(vmem_limit_bytes=60 * 1024 * 1024)
    in_vmem = pl.BlockSpec(memory_space=VMEM)
    in_hbm = pl.BlockSpec(memory_space=HBM)
    in_smem = pl.BlockSpec(memory_space=SMEM)
    anywhere = pl.BlockSpec(memory_space=pl.ANY)
    place = lax.axis_index("seq")
    at = place.reshape(1).astype(jnp.int32)

    def array(*shape, dtype=jnp.bfloat16):
        return jax.ShapeDtypeStruct(shape, dtype)

    def to_peer(value, m):
        return lax.ppermute(value, "seq", [(i, i ^ m) for i in range(peers)])

    def moves(size):
        return pl.CostEstimate(flops=0, bytes_accessed=size, transcendentals=0)

    sent, kept = pl.pallas_call(
        project_kernel,
        out_shape=(
            array(half, parts * columns + LANES),
            array(half, parts * columns + LANES, dtype=jnp.float32),
        ),
        in_specs=[in_smem] + [in_hbm] * 3,
        out_specs=(in_vmem, in_vmem),
        scratch_shapes=[
            pltpu.VMEM(states.shape, jnp.bfloat16),
            pltpu.VMEM(norm_gain.shape, jnp.bfloat16),
            pltpu.VMEM((parts, depth, columns), jnp.bfloat16),
            pltpu.SemaphoreType.DMA((parts + 2,)),
        ],
        compiler_params=all_room,
        name="project",
    )(at, states, norm_gain, w_qkv)
    received = to_peer(sent, 1)

    positions = lax.dynamic_slice_in_dim(context_len, place % 2 * half, half) - 1
    pair = (jnp.arange(columns, dtype=jnp.int32) % (HEAD_DIM // 2)).astype(jnp.float32)
    frequency = 10000.0 ** (-pair * 2.0 / HEAD_DIM)
    angles = positions.astype(jnp.float32)[:, None] * frequency[None, :]

    table = (block_owner, block_index, context_len)
    plan = pl.pallas_call(
        functools.partial(plan_kernel, tokens),
        out_shape=(
            array(rows, half),
            array(rows, half),
            array(rows, LANES, dtype=jnp.int32),
            array(rows, LANES, dtype=jnp.float32),
        ),
        in_specs=[in_smem] * 4,
        compiler_params=limit,
        name="plan",
    )(at, *table)
    keys, updated = pl.pallas_call(
        stage_keys_kernel,
        out_shape=(array(blocks, tokens, columns), array(*cache.shape)),
        in_specs=[in_hbm],
        out_specs=(in_vmem, in_hbm),
        scratch_shapes=[pltpu.SemaphoreType.DMA((steps,))] * 2,
        compiler_params=most_room,
        cost_estimate=moves(cache.size * 2),
        name="stage_keys",
    )(cache)

    *sends, query, fresh = pl.pallas_call(
        halve_kernel,
        out_shape=(
            *(array(half + 2 * share, columns + LANES) for _ in range(1, lines)),
            array(half, columns + LANES, dtype=jnp.float32),
            array(share, 2 * columns, dtype=jnp.float32),
        ),
        in_specs=[in_smem, in_vmem, in_vmem, anywhere],
        scratch_shapes=[pltpu.VMEM((half, parts * columns + LANES), jnp.float32)],
        compiler_params=limit,
        name="halve",
    )(at, kept, received, keys)
    received = [to_peer(send, 2 * m) for m, send in enumerate(sends, 1)]
    updated = pl.pallas_call(
        stage_values_kernel,
        out_shape=array(*cache.shape),
        in_specs=[in_hbm, in_hbm],
        out_specs=in_hbm,
        scratch_shapes=[pltpu.VMEM((blocks, tokens, columns), jnp.bfloat16)]
        + [pltpu.SemaphoreType.DMA((steps,))] * 2,
        input_output_aliases={1: 0},
        compiler_params=most_room,
        cost_estimate=moves(cache.size * 2),
        name="stage_values",
    )(cache, updated)
    mine, news = pl.pallas_call(
        functools.partial(finish_kernel, depth * peers),
        out_shape=(array(half, columns), array(2 * share, columns + LANES)),
        in_specs=[in_smem, in_hbm] + [in_vmem] * (4 + len(received)),
        compiler_params=most_room,
        name="finish",
    )(at, updated, query, fresh, jnp.cos(angles), jnp.sin(angles), *received)
    other = to_peer(mine, 1)

    piece = pl.pallas_call(
        attend_kernel,
        out_shape=array(2 * share + blocks, columns + LANES),
        in_specs=[in_vmem] * 8 + [in_hbm],
        scratch_shapes=[
            pltpu.VMEM((blocks, tokens, columns), jnp.bfloat16),
            pltpu.SemaphoreType.DMA((steps,)),
        ],
        compiler_params=most_room,
        name="attend",
    )(mine, other, *plan, news, keys, cache)
    column = [piece] + [to_peer(piece, 2 * m) for m in range(1, lines)]
    pieces = [p for near in column for p in (near, to_peer(near, 1))]

    rank = lax.axis_index("tp")
    kept_rows = requests // ranks
    own, *sends = pl.pallas_call(
        functools.partial(output_kernel, peers),
        out_shape=tuple(array(kept_rows, out_columns, dtype=jnp.float32) for _ in range(ranks)),
        in_specs=[in_smem] + [in_vmem] * (peers + 2),
        out_specs=(in_vmem,) * ranks,
        scratch_shapes=[pltpu.VMEM((requests, out_columns), jnp.float32)],
        compiler_params=limit,
        name="output",
    )(rank.reshape(1).astype(jnp.int32), *pieces, w_out, states)
    total = own
    for m, send in enumerate(sends, 1):
        total = total + lax.ppermute(send, "tp", [(i, i ^ m) for i in range(ranks)])
    updated = pl.pallas_call(
        functools.partial(patch_kernel, peers),
        out_shape=array(*cache.shape),
        in_specs=[in_smem] * 4 + [anywhere] + [in_vmem] * peers + [in_hbm] * 2,
        out_specs=in_hbm,
        scratch_shapes=[
            pltpu.VMEM((peers, 2 * share, columns), jnp.float32),
            pltpu.VMEM((blocks, 2, ROWS, columns), jnp.bfloat16),
            pltpu.SemaphoreType.DMA((blocks,)),
            pltpu.SemaphoreType.DMA((blocks,)),
        ],
        input_output_aliases={6 + peers: 0},
        compiler_params=most_room,
        cost_estimate=moves(cache.size),
        name="patch",
    )(at, *table, sends[0], *pieces, cache, updated)
    return (total.astype(jnp.bfloat16), updated)


def solution(mesh):
    return jax.shard_map(
        shards,
        mesh=mesh,
        in_specs=(
            P(None, "seq"),
            P("seq"),
            P(None, "seq", "tp"),
            P("tp", "seq"),
            P("seq", None, None, "tp"),
            P(),
            P("seq"),
            P("seq"),
        ),
        out_specs=(P("tp", "seq"), P("seq", None, None, "tp")),
        check_vma=False,
    )
```

time: 59.6 us -> 49.9 us (0.84)
  waiting for transfers between devices: 24.5 us -> 9.94 us
  starting transfers between devices: 16.7 us -> 20.5 us
  Pallas kernels: 15.6 us -> 16.5 us
    all_to_all x3 -> x0, waiting for transfers between devices: 21.5 us -> none  [the longest x1 9.05 us: shards(): lax.all_to_all(terms, 'seq', split_axis=0, concat_axis=0, tiled=True)]
    ppermute x0 -> x12, starting transfers between devices: none -> 18.6 us  [to_peer(): return lax.ppermute(value, 'seq', [(i, i ^ m) for i in range(peers)])]
    all_to_all x3 -> x0, starting transfers between devices: 14.8 us -> none  [the longest x1 7.42 us: shards(): lax.all_to_all(terms, 'seq', split_axis=0, concat_axis=0, tiled=True)]
    ppermute x0 -> x12, waiting for transfers between devices: none -> 9.93 us  [to_peer(): return lax.ppermute(value, 'seq', [(i, i ^ m) for i in range(peers)])]
    ppermute x3, waiting for transfers between devices: 2.95 us -> 0.01 us  [shards(): total = total + lax.ppermute(send, 'tp', [(i, i ^ m) for i in range(ranks)])]
    pallas_call x6 -> x8, Pallas kernels: 14.7 us -> 16.2 us  [the longest x1 3.2 us: shards(): pl.pallas_call(attend_kernel, out_shape=array(2 * share + blocks, columns...]
  transfers between devices with their start and end apart: 6 -> 15, of which waited for: 5 -> 8; matrix products, arithmetic and copies ran while one was open for 2% -> 2% of each run, Pallas kernels for 12% -> 18%
where the time goes in v3:
time: 49.9 us; the launch traced here: 49.6 us
  starting transfers between devices  20.5 us (41%)
  Pallas kernels  16.5 us (33%)
  waiting for transfers between devices  9.94 us (20%)
  other arithmetic  1.77 us (4%)
  between operations  0.81 us (2%)
    ppermute x12, starting transfers between devices, to_peer(): return lax.ppermute(value, 'seq', [(i, i ^ m) for i in range(peers)])  18.6 us
    ppermute x12, waiting for transfers between devices, to_peer(): return lax.ppermute(value, 'seq', [(i, i ^ m) for i in range(peers)])  9.93 us
    pallas_call x1, Pallas kernels, shards(): pl.pallas_call(attend_kernel, out_shape=array(2 * share + blocks, columns...  3.2 us
    pallas_call x1, Pallas kernels, shards(): pl.pallas_call(functools.partial(patch_kernel, peers), out_shape=array(*c...  3.03 us
    pallas_call x1, Pallas kernels, shards(): pl.pallas_call(project_kernel, out_shape=(array(half, parts * columns + L...  2.66 us
    pallas_call x1, Pallas kernels, shards(): pl.pallas_call(stage_values_kernel, out_shape=array(*cache.shape), in_spe...  2.5 us
    pallas_call x1, Pallas kernels, shards(): pl.pallas_call(stage_keys_kernel, out_shape=(array(blocks, tokens, column...  2.49 us
    ppermute x3, starting transfers between devices, shards(): total = total + lax.ppermute(send, 'tp', [(i, i ^ m) for i in range(ranks)])  1.92 us
  transfers between devices with their start and end apart: 15, of which 8 were waited for; matrix products, arithmetic and copies ran while one was open for 2% of the time, Pallas kernels for 18%

profile of v3, /device:TPU:0, one launch (start us, length us, event | category | flops | bytes accessed | tf_op | source)
XLA Modules:
  0.0 49.6 jit_solution(17822566301211408130)
XLA Ops:
  0.6 2.7 %project.1 = (bf16[32,2432]{1,0:T(8,128)(2,1)}, f32[32,2432]{1,0:T(8,128)}) custom-call(s32[1]{0:T(128)} %bitcast.1.place_ref, bf16[64,384]{1,0:T(8,128)(2,1)} %rest_9_.1, bf16[384]{0:T(512)(128)(2,1)} %gain_ref.1, bf16[3,384,768]{2,1,0:T(8,128)(2,1)} %w_ref.1), custom_call_target="tpu_custom_call" | custom-call | tf_op jit(solution)/shard_map/project/pallas_call | solution.py:437
  3.3 3.0 %collective-permute-start = (bf16[32,2432]{1,0:T(8,128)(2,1)}, bf16[32,2432]{1,0:T(8,128)(2,1)S(1)}, u32[]{:S(2)}, u32[]{:S(2)}) collective-permute-start(bf16[32,2432]{1,0:T(8,128)(2,1)} %get-tuple-element.23), channel_id=1, source_target_pairs={{0,4},{4,0},{8,12},{12,8},{16,20},{20,16},{24,28},{28,24},{1,5},{5... | collective-permute-start | bytes 466952 | tf_op jit(solution)/shard_map/ppermute | solution.py:432
  6.3 0.7 %add_convert_fusion.1 = f32[32]{0:T(128)S(1)} fusion(s32[64]{0:T(128)} %length_ref.3, s32[]{:T(128)S(6)} %select_n.21), kind=kLoop, calls=%fused_computation.12 | loop fusion | flops 64 | bytes 260 | tf_op jit(solution)/shard_map/convert_element_type | solution.py:459
  7.1 2.5 %stage_keys.1 = (bf16[24,64,768]{2,1,0:T(8,128)(2,1)S(1)}, bf16[24,2,64,768]{3,2,1,0:T(8,128)(2,1)}) custom-call(bf16[24,2,64,768]{3,2,1,0:T(8,128)(2,1)} %rest_8_.3), custom_call_target="tpu_custom_call" | custom-call | bytes 4718592 | tf_op jit(solution)/shard_map/stage_keys/pallas_call | solution.py:474
  9.6 1.0 %collective-permute-done.recv_ref = bf16[32,2432]{1,0:T(8,128)(2,1)S(1)} collective-permute-done((bf16[32,2432]{1,0:T(8,128)(2,1)}, bf16[32,2432]{1,0:T(8,128)(2,1)S(1)}, u32[]{:S(2)}, u32[]{:S(2)}) %collective-permute-start) | collective-permute-done | bytes 155680 | tf_op jit(solution)/shard_map/ppermute | solution.py:432
  10.7 1.9 %collective-permute-start.1 = (bf16[48,896]{1,0:T(8,128)(2,1)S(1)}, bf16[48,896]{1,0:T(8,128)(2,1)S(1)}, u32[]{:S(2)}, u32[]{:S(2)}) collective-permute-start(bf16[48,896]{1,0:T(8,128)(2,1)S(1)} %get-tuple-element.27), channel_id=1, source_target_pairs={{0,8},{4,12},{8,0},{12,4},{16,24},{20,28},{24,16},{28,20},{1,9},{5... | collective-permute-start | bytes 258056 | tf_op jit(solution)/shard_map/ppermute | solution.py:432
  12.5 2.6 %collective-permute-start.2 = (bf16[48,896]{1,0:T(8,128)(2,1)S(1)}, bf16[48,896]{1,0:T(8,128)(2,1)S(1)}, u32[]{:S(2)}, u32[]{:S(2)}) collective-permute-start(bf16[48,896]{1,0:T(8,128)(2,1)S(1)} %get-tuple-element.28), channel_id=1, source_target_pairs={{0,16},{4,20},{8,24},{12,28},{16,0},{20,4},{24,8},{28,12},{1,17},{... | collective-permute-start | bytes 258056 | tf_op jit(solution)/shard_map/ppermute | solution.py:432
  15.1 0.4 multiply_sine_fusion
  15.6 2.5 %stage_values.1.after_ref.rest_9_ = bf16[24,2,64,768]{3,2,1,0:T(8,128)(2,1)} custom-call(bf16[24,2,64,768]{3,2,1,0:T(8,128)(2,1)} %rest_8_.3, bf16[24,2,64,768]{3,2,1,0:T(8,128)(2,1)} %get-tuple-element.21.held_ref), custom_call_target="tpu_custom_call", output_to_operand_aliasing={{}: (1, {})} | custom-call | bytes 4718592 | tf_op jit(solution)/shard_map/stage_values/pallas_call | solution.py:498
  18.1 2.1 %collective-permute-done.2.rest_1_ = bf16[48,896]{1,0:T(8,128)(2,1)S(1)} collective-permute-done((bf16[48,896]{1,0:T(8,128)(2,1)S(1)}, bf16[48,896]{1,0:T(8,128)(2,1)S(1)}, u32[]{:S(2)}, u32[]{:S(2)}) %collective-permute-start.2) | collective-permute-done | bytes 86048 | tf_op jit(solution)/shard_map/ppermute | solution.py:432
  20.2 1.3 %collective-permute-done.3.rest_2_ = bf16[48,896]{1,0:T(8,128)(2,1)S(1)} collective-permute-done((bf16[48,896]{1,0:T(8,128)(2,1)S(1)}, bf16[48,896]{1,0:T(8,128)(2,1)S(1)}, u32[]{:S(2)}, u32[]{:S(2)}) %collective-permute-start.3) | collective-permute-done | bytes 86048 | tf_op jit(solution)/shard_map/ppermute | solution.py:432
  21.5 0.3 finish.1
  21.9 1.6 %collective-permute-start.4 = (bf16[32,768]{1,0:T(8,128)(2,1)S(1)}, bf16[32,768]{1,0:T(8,128)(2,1)S(1)}, u32[]{:S(2)}, u32[]{:S(2)}) collective-permute-start(bf16[32,768]{1,0:T(8,128)(2,1)S(1)} %get-tuple-element.30.mine_ref), channel_id=1, source_target_pairs={{0,4},{4,0},{8,12},{12,8},{16,20},{20,16},{24,28},{28,24},{1,5},{5... | collective-permute-start | bytes 147464 | tf_op jit(solution)/shard_map/ppermute | solution.py:432
  23.5 0.7 %plan.1 = (bf16[192,32]{1,0:T(8,128)(2,1)S(1)}, bf16[192,32]{1,0:T(8,128)(2,1)S(1)}, s32[192,128]{1,0:T(8,128)S(1)}, f32[192,128]{1,0:T(8,128)S(1)}) custom-call(s32[1]{0:T(128)} %bitcast.1.place_ref, s32[24]{0:T(128)S(1)} %copy-done.4, s32[24]{0:T(128)S(1)} %copy-done.5, s32[64]{0:T(128)S(1)} %copy-done.3), custom_call_target="tpu_custom_call" | custom-call | tf_op jit(solution)/shard_map/plan/pallas_call | solution.py:462
  24.2 1.9 %collective-permute-done.4.other_ref = bf16[32,768]{1,0:T(8,128)(2,1)S(1)} collective-permute-done((bf16[32,768]{1,0:T(8,128)(2,1)S(1)}, bf16[32,768]{1,0:T(8,128)(2,1)S(1)}, u32[]{:S(2)}, u32[]{:S(2)}) %collective-permute-start.4) | collective-permute-done | bytes 49184 | tf_op jit(solution)/shard_map/ppermute | solution.py:432
  26.0 3.2 %attend.1.rest_0_ = bf16[40,896]{1,0:T(8,128)(2,1)S(1)} custom-call(bf16[32,768]{1,0:T(8,128)(2,1)S(1)} %get-tuple-element.30.mine_ref, bf16[32,768]{1,0:T(8,128)(2,1)S(1)} %collective-permute-done.4.other_ref, bf16[192,32]{1,0:T(8,128)(2,1)S(1)} %get-tuple-element.31.pick_mine_ref, bf16[192,32]{1,0:T(8,128)(2,1)S(1)} %get-tuple-element.32.pick_other_ref, ...), custom_call_target="tpu_custom_call" | custom-call | tf_op jit(solution)/shard_map/attend/pallas_call | solution.py:519
  29.3 1.2 %collective-permute-start.6 = (bf16[40,896]{1,0:T(8,128)(2,1)S(1)}, bf16[40,896]{1,0:T(8,128)(2,1)S(1)}, u32[]{:S(2)}, u32[]{:S(2)}) collective-permute-start(bf16[40,896]{1,0:T(8,128)(2,1)S(1)} %attend.1.rest_0_), channel_id=1, source_target_pairs={{0,8},{4,12},{8,0},{12,4},{16,24},{20,28},{24,16},{28,20},{1,9},{5... | collective-permute-start | bytes 215048 | tf_op jit(solution)/shard_map/ppermute | solution.py:432
  30.5 1.6 %collective-permute-start.8 = (bf16[40,896]{1,0:T(8,128)(2,1)S(1)}, bf16[40,896]{1,0:T(8,128)(2,1)S(1)}, u32[]{:S(2)}, u32[]{:S(2)}) collective-permute-start(bf16[40,896]{1,0:T(8,128)(2,1)S(1)} %attend.1.rest_0_), channel_id=1, source_target_pairs={{0,16},{4,20},{8,24},{12,28},{16,0},{20,4},{24,8},{28,12},{1,17},{... | collective-permute-start | bytes 215048 | tf_op jit(solution)/shard_map/ppermute | solution.py:432
  32.0 1.7 %collective-permute-start.10 = (bf16[40,896]{1,0:T(8,128)(2,1)S(1)}, bf16[40,896]{1,0:T(8,128)(2,1)S(1)}, u32[]{:S(2)}, u32[]{:S(2)}) collective-permute-start(bf16[40,896]{1,0:T(8,128)(2,1)S(1)} %attend.1.rest_0_), channel_id=1, source_target_pairs={{0,24},{4,28},{8,16},{12,20},{16,8},{20,12},{24,0},{28,4},{1,25},{... | collective-permute-start | bytes 215048 | tf_op jit(solution)/shard_map/ppermute | solution.py:432
  33.7 1.5 %collective-permute-start.5 = (bf16[40,896]{1,0:T(8,128)(2,1)S(1)}, bf16[40,896]{1,0:T(8,128)(2,1)S(1)}, u32[]{:S(2)}, u32[]{:S(2)}) collective-permute-start(bf16[40,896]{1,0:T(8,128)(2,1)S(1)} %attend.1.rest_0_), channel_id=1, source_target_pairs={{0,4},{4,0},{8,12},{12,8},{16,20},{20,16},{24,28},{28,24},{1,5},{5... | collective-permute-start | bytes 215048 | tf_op jit(solution)/shard_map/ppermute | solution.py:432
  35.2 0.5 %collective-permute-start.7 = (bf16[40,896]{1,0:T(8,128)(2,1)S(1)}, bf16[40,896]{1,0:T(8,128)(2,1)S(1)}, u32[]{:S(2)}, u32[]{:S(2)}) collective-permute-start(bf16[40,896]{1,0:T(8,128)(2,1)S(1)} %collective-permute-done.6.rest_2_), channel_id=1, source_target_pairs={{0,4},{4,0},{8,12},{12,8},{16,20},{20,16},{24,28},{28,24},{1,5},{5... | collective-permute-start | bytes 215048 | tf_op jit(solution)/shard_map/ppermute | solution.py:432
  35.8 0.7 %collective-permute-done.8.rest_4_ = bf16[40,896]{1,0:T(8,128)(2,1)S(1)} collective-permute-done((bf16[40,896]{1,0:T(8,128)(2,1)S(1)}, bf16[40,896]{1,0:T(8,128)(2,1)S(1)}, u32[]{:S(2)}, u32[]{:S(2)}) %collective-permute-start.8) | collective-permute-done | bytes 71712 | tf_op jit(solution)/shard_map/ppermute | solution.py:432
  36.5 1.5 %collective-permute-start.9 = (bf16[40,896]{1,0:T(8,128)(2,1)S(1)}, bf16[40,896]{1,0:T(8,128)(2,1)S(1)}, u32[]{:S(2)}, u32[]{:S(2)}) collective-permute-start(bf16[40,896]{1,0:T(8,128)(2,1)S(1)} %collective-permute-done.8.rest_4_), channel_id=1, source_target_pairs={{0,4},{4,0},{8,12},{12,8},{16,20},{20,16},{24,28},{28,24},{1,5},{5... | collective-permute-start | bytes 215048 | tf_op jit(solution)/shard_map/ppermute | solution.py:432
  38.0 0.2 collective-permute-done.10.rest_6_
  38.1 1.5 %collective-permute-start.11 = (bf16[40,896]{1,0:T(8,128)(2,1)S(1)}, bf16[40,896]{1,0:T(8,128)(2,1)S(1)}, u32[]{:S(2)}, u32[]{:S(2)}) collective-permute-start(bf16[40,896]{1,0:T(8,128)(2,1)S(1)} %collective-permute-done.10.rest_6_), channel_id=1, source_target_pairs={{0,4},{4,0},{8,12},{12,8},{16,20},{20,16},{24,28},{28,24},{1,5},{5... | collective-permute-start | bytes 215048 | tf_op jit(solution)/shard_map/ppermute | solution.py:432
  39.7 1.1 %collective-permute-done.9.rest_5_ = bf16[40,896]{1,0:T(8,128)(2,1)S(1)} collective-permute-done((bf16[40,896]{1,0:T(8,128)(2,1)S(1)}, bf16[40,896]{1,0:T(8,128)(2,1)S(1)}, u32[]{:S(2)}, u32[]{:S(2)}) %collective-permute-start.9) | collective-permute-done | bytes 71712 | tf_op jit(solution)/shard_map/ppermute | solution.py:432
  40.8 1.7 %collective-permute-done.11.rest_7_ = bf16[40,896]{1,0:T(8,128)(2,1)S(1)} collective-permute-done((bf16[40,896]{1,0:T(8,128)(2,1)S(1)}, bf16[40,896]{1,0:T(8,128)(2,1)S(1)}, u32[]{:S(2)}, u32[]{:S(2)}) %collective-permute-start.11) | collective-permute-done | bytes 71712 | tf_op jit(solution)/shard_map/ppermute | solution.py:432
  42.5 1.5 %output.1 = (f32[16,384]{1,0:T(8,128)S(1)}, f32[16,384]{1,0:T(8,128)S(1)}, f32[16,384]{1,0:T(8,128)S(1)}, f32[16,384]{1,0:T(8,128)S(1)}) custom-call(s32[1]{0:T(128)} %bitcast.place_ref, bf16[40,896]{1,0:T(8,128)(2,1)S(1)} %attend.1.rest_0_, bf16[40,896]{1,0:T(8,128)(2,1)S(1)} %collective-permute-done.5.rest_1_, ...), custom_call_target="tpu_custom_call" | custom-call | tf_op jit(solution)/shard_map/output/pallas_call | solution.py:535
  44.1 1.6 %collective-permute-start.13 = (f32[16,384]{1,0:T(8,128)S(1)}, f32[16,384]{1,0:T(8,128)S(1)}, u32[]{:S(2)}, u32[]{:S(2)}) collective-permute-start(f32[16,384]{1,0:T(8,128)S(1)} %get-tuple-element.38), channel_id=1, source_target_pairs={{0,2},{1,3},{2,0},{3,1},{4,6},{5,7},{6,4},{7,5},{8,10},{9,11},{10,... | collective-permute-start | bytes 73736 | tf_op jit(solution)/shard_map/ppermute | solution.py:546
  45.7 0.3 collective-permute-start.12
  45.9 3.0 %patch.1 = bf16[24,2,64,768]{3,2,1,0:T(8,128)(2,1)} custom-call(s32[1]{0:T(128)} %bitcast.1.place_ref, s32[24]{0:T(128)S(1)} %copy-done.4, s32[24]{0:T(128)S(1)} %copy-done.5, s32[64]{0:T(128)S(1)} %copy-done.3, f32[16,384]{1,0:T(8,128)S(1)} %get-tuple-element.37.after_ref, bf16[40,896]{1,0:T(8,128)(2,1)S(1)} %attend.1.rest_0_, ...), custom_call_target="tpu_custom_call", output_to_operand_aliasing={{}: (14, {})} | custom-call | bytes 2359296 | tf_op jit(solution)/shard_map/patch/pallas_call | solution.py:547
  49.0 0.6 %add_convert_fusion = bf16[16,384]{1,0:T(8,128)(2,1)} fusion(f32[16,384]{1,0:T(8,128)S(1)} %collective-permute-done.14, f32[16,384]{1,0:T(8,128)S(1)} %collective-permute-done.13, f32[16,384]{1,0:T(8,128)S(1)} %get-tuple-element.36, f32[16,384]{1,0:T(8,128)S(1)} %collective-permute-done.12), kind=kLoop, calls=%fused_computation.2 | loop fusion | flops 24576 | bytes 110592 | tf_op jit(solution)/shard_map/convert_element_type | solution.py:563
  (23 shorter events, 0.2 us)
Async XLA Ops:
  3.3 7.3 %copy-start.1 = (f32[32,2432]{1,0:T(8,128)S(1)}, f32[32,2432]{1,0:T(8,128)}, u32[]{:S(2)}) copy-start(f32[32,2432]{1,0:T(8,128)} %get-tuple-element.22.kept_ref) | copy-start | bytes 933892
  3.3 7.3 %collective-permute-start = (bf16[32,2432]{1,0:T(8,128)(2,1)}, bf16[32,2432]{1,0:T(8,128)(2,1)S(1)}, u32[]{:S(2)}, u32[]{:S(2)}) collective-permute-start(bf16[32,2432]{1,0:T(8,128)(2,1)} %get-tuple-element.23), channel_id=1, source_target_pairs={{0,4},{4,0},{8,12},{12,8},{16,20},{20,16},{24,28},{28,24},{1,5},{5... | collective-permute-start | bytes 466952 | tf_op jit(solution)/shard_map/ppermute | solution.py:432
  10.7 7.4 %collective-permute-start.1 = (bf16[48,896]{1,0:T(8,128)(2,1)S(1)}, bf16[48,896]{1,0:T(8,128)(2,1)S(1)}, u32[]{:S(2)}, u32[]{:S(2)}) collective-permute-start(bf16[48,896]{1,0:T(8,128)(2,1)S(1)} %get-tuple-element.27), channel_id=1, source_target_pairs={{0,8},{4,12},{8,0},{12,4},{16,24},{20,28},{24,16},{28,20},{1,9},{5... | collective-permute-start | bytes 258056 | tf_op jit(solution)/shard_map/ppermute | solution.py:432
  12.5 7.7 %collective-permute-start.2 = (bf16[48,896]{1,0:T(8,128)(2,1)S(1)}, bf16[48,896]{1,0:T(8,128)(2,1)S(1)}, u32[]{:S(2)}, u32[]{:S(2)}) collective-permute-start(bf16[48,896]{1,0:T(8,128)(2,1)S(1)} %get-tuple-element.28), channel_id=1, source_target_pairs={{0,16},{4,20},{8,24},{12,28},{16,0},{20,4},{24,8},{28,12},{1,17},{... | collective-permute-start | bytes 258056 | tf_op jit(solution)/shard_map/ppermute | solution.py:432
  15.1 6.4 %collective-permute-start.3 = (bf16[48,896]{1,0:T(8,128)(2,1)S(1)}, bf16[48,896]{1,0:T(8,128)(2,1)S(1)}, u32[]{:S(2)}, u32[]{:S(2)}) collective-permute-start(bf16[48,896]{1,0:T(8,128)(2,1)S(1)} %get-tuple-element.29), channel_id=1, source_target_pairs={{0,24},{4,28},{8,16},{12,20},{16,8},{20,12},{24,0},{28,4},{1,25},{... | collective-permute-start | bytes 258056 | tf_op jit(solution)/shard_map/ppermute | solution.py:432
  18.1 5.4 %copy-start.3 = (s32[64]{0:T(128)S(1)}, s32[64]{0:T(128)}, u32[]{:S(2)}) copy-start(s32[64]{0:T(128)} %length_ref.3) | copy-start | bytes 772
  18.1 5.4 %copy-start.4 = (s32[24]{0:T(128)S(1)}, s32[24]{0:T(128)}, u32[]{:S(2)}) copy-start(s32[24]{0:T(128)} %owner_ref.3) | copy-start | bytes 292
  18.1 5.4 %copy-start.5 = (s32[24]{0:T(128)S(1)}, s32[24]{0:T(128)}, u32[]{:S(2)}) copy-start(s32[24]{0:T(128)} %index_ref.3) | copy-start | bytes 292
  21.9 20.6 %copy-start = (bf16[768,384]{1,0:T(8,128)(2,1)S(1)}, bf16[768,384]{1,0:T(8,128)(2,1)}, u32[]{:S(2)}) copy-start(bf16[768,384]{1,0:T(8,128)(2,1)} %rest_8_.2) | copy-start | bytes 1769476
  21.9 20.6 %copy-start.2 = (bf16[64,384]{1,0:T(8,128)(2,1)S(1)}, bf16[64,384]{1,0:T(8,128)(2,1)}, u32[]{:S(2)}) copy-start(bf16[64,384]{1,0:T(8,128)(2,1)} %rest_9_.1) | copy-start | bytes 147460
  21.9 4.2 %collective-permute-start.4 = (bf16[32,768]{1,0:T(8,128)(2,1)S(1)}, bf16[32,768]{1,0:T(8,128)(2,1)S(1)}, u32[]{:S(2)}, u32[]{:S(2)}) collective-permute-start(bf16[32,768]{1,0:T(8,128)(2,1)S(1)} %get-tuple-element.30.mine_ref), channel_id=1, source_target_pairs={{0,4},{4,0},{8,12},{12,8},{16,20},{20,16},{24,28},{28,24},{1,5},{5... | collective-permute-start | bytes 147464 | tf_op jit(solution)/shard_map/ppermute | solution.py:432
  29.3 6.0 %collective-permute-start.6 = (bf16[40,896]{1,0:T(8,128)(2,1)S(1)}, bf16[40,896]{1,0:T(8,128)(2,1)S(1)}, u32[]{:S(2)}, u32[]{:S(2)}) collective-permute-start(bf16[40,896]{1,0:T(8,128)(2,1)S(1)} %attend.1.rest_0_), channel_id=1, source_target_pairs={{0,8},{4,12},{8,0},{12,4},{16,24},{20,28},{24,16},{28,20},{1,9},{5... | collective-permute-start | bytes 215048 | tf_op jit(solution)/shard_map/ppermute | solution.py:432
  30.5 6.0 %collective-permute-start.8 = (bf16[40,896]{1,0:T(8,128)(2,1)S(1)}, bf16[40,896]{1,0:T(8,128)(2,1)S(1)}, u32[]{:S(2)}, u32[]{:S(2)}) collective-permute-start(bf16[40,896]{1,0:T(8,128)(2,1)S(1)} %attend.1.rest_0_), channel_id=1, source_target_pairs={{0,16},{4,20},{8,24},{12,28},{16,0},{20,4},{24,8},{28,12},{1,17},{... | collective-permute-start | bytes 215048 | tf_op jit(solution)/shard_map/ppermute | solution.py:432
  32.0 6.1 %collective-permute-start.10 = (bf16[40,896]{1,0:T(8,128)(2,1)S(1)}, bf16[40,896]{1,0:T(8,128)(2,1)S(1)}, u32[]{:S(2)}, u32[]{:S(2)}) collective-permute-start(bf16[40,896]{1,0:T(8,128)(2,1)S(1)} %attend.1.rest_0_), channel_id=1, source_target_pairs={{0,24},{4,28},{8,16},{12,20},{16,8},{20,12},{24,0},{28,4},{1,25},{... | collective-permute-start | bytes 215048 | tf_op jit(solution)/shard_map/ppermute | solution.py:432
  33.7 6.0 %collective-permute-start.5 = (bf16[40,896]{1,0:T(8,128)(2,1)S(1)}, bf16[40,896]{1,0:T(8,128)(2,1)S(1)}, u32[]{:S(2)}, u32[]{:S(2)}) collective-permute-start(bf16[40,896]{1,0:T(8,128)(2,1)S(1)} %attend.1.rest_0_), channel_id=1, source_target_pairs={{0,4},{4,0},{8,12},{12,8},{16,20},{20,16},{24,28},{28,24},{1,5},{5... | collective-permute-start | bytes 215048 | tf_op jit(solution)/shard_map/ppermute | solution.py:432
  35.2 4.4 %collective-permute-start.7 = (bf16[40,896]{1,0:T(8,128)(2,1)S(1)}, bf16[40,896]{1,0:T(8,128)(2,1)S(1)}, u32[]{:S(2)}, u32[]{:S(2)}) collective-permute-start(bf16[40,896]{1,0:T(8,128)(2,1)S(1)} %collective-permute-done.6.rest_2_), channel_id=1, source_target_pairs={{0,4},{4,0},{8,12},{12,8},{16,20},{20,16},{24,28},{28,24},{1,5},{5... | collective-permute-start | bytes 215048 | tf_op jit(solution)/shard_map/ppermute | solution.py:432
  36.5 4.3 %collective-permute-start.9 = (bf16[40,896]{1,0:T(8,128)(2,1)S(1)}, bf16[40,896]{1,0:T(8,128)(2,1)S(1)}, u32[]{:S(2)}, u32[]{:S(2)}) collective-permute-start(bf16[40,896]{1,0:T(8,128)(2,1)S(1)} %collective-permute-done.8.rest_4_), channel_id=1, source_target_pairs={{0,4},{4,0},{8,12},{12,8},{16,20},{20,16},{24,28},{28,24},{1,5},{5... | collective-permute-start | bytes 215048 | tf_op jit(solution)/shard_map/ppermute | solution.py:432
  38.1 4.3 %collective-permute-start.11 = (bf16[40,896]{1,0:T(8,128)(2,1)S(1)}, bf16[40,896]{1,0:T(8,128)(2,1)S(1)}, u32[]{:S(2)}, u32[]{:S(2)}) collective-permute-start(bf16[40,896]{1,0:T(8,128)(2,1)S(1)} %collective-permute-done.10.rest_6_), channel_id=1, source_target_pairs={{0,4},{4,0},{8,12},{12,8},{16,20},{20,16},{24,28},{28,24},{1,5},{5... | collective-permute-start | bytes 215048 | tf_op jit(solution)/shard_map/ppermute | solution.py:432
  44.0 5.0 %collective-permute-start.14 = (f32[16,384]{1,0:T(8,128)S(1)}, f32[16,384]{1,0:T(8,128)S(1)}, u32[]{:S(2)}, u32[]{:S(2)}) collective-permute-start(f32[16,384]{1,0:T(8,128)S(1)} %get-tuple-element.39), channel_id=1, source_target_pairs={{0,3},{1,2},{2,1},{3,0},{4,7},{5,6},{6,5},{7,4},{8,11},{9,10},{10,... | collective-permute-start | bytes 73736 | tf_op jit(solution)/shard_map/ppermute | solution.py:546
  44.1 4.9 %collective-permute-start.13 = (f32[16,384]{1,0:T(8,128)S(1)}, f32[16,384]{1,0:T(8,128)S(1)}, u32[]{:S(2)}, u32[]{:S(2)}) collective-permute-start(f32[16,384]{1,0:T(8,128)S(1)} %get-tuple-element.38), channel_id=1, source_target_pairs={{0,2},{1,3},{2,0},{3,1},{4,6},{5,7},{6,4},{7,5},{8,10},{9,11},{10,... | collective-permute-start | bytes 73736 | tf_op jit(solution)/shard_map/ppermute | solution.py:546
  45.7 3.3 %collective-permute-start.12 = (f32[16,384]{1,0:T(8,128)S(1)}, f32[16,384]{1,0:T(8,128)S(1)}, u32[]{:S(2)}, u32[]{:S(2)}) collective-permute-start(f32[16,384]{1,0:T(8,128)S(1)} %get-tuple-element.37.after_ref), channel_id=1, source_target_pairs={{0,1},{1,0},{2,3},{3,2},{4,5},{5,4},{6,7},{7,6},{8,9},{9,8},{10,11... | collective-permute-start | bytes 73736 | tf_op jit(solution)/shard_map/ppermute | solution.py:546

commit v4 on v3

--- a/solution.py
+++ b/solution.py
@@ -70,6 +70,11 @@
         kept_ref[:, here] = term[half:]
 
 
+def flat(value):
+    chunks = value.shape[1] // LANES
+    return [value[:, c * LANES : (c + 1) * LANES] for c in range(chunks)]
+
+
 def halve_kernel(place_ref, kept_ref, recv_ref, after_ref, *rest):
     sends, query_ref, fresh_ref, total = rest[:-3], rest[-3], rest[-2], rest[-1]
     columns = query_ref.shape[1] - LANES
@@ -77,37 +82,54 @@
     half = kept_ref.shape[0]
     total[...] = kept_ref[...] + recv_ref[...].astype(jnp.float32)
     squares = jnp.sum(total[:, 3 * columns :], axis=1, keepdims=True)
-    stat = lanes_of(split3(squares))
     query_ref[:, :columns] = total[:, :columns]
-    query_ref[:, columns:] = stat
-    query = total[:, :columns].astype(jnp.bfloat16)
-    stat = stat.astype(jnp.bfloat16)
+    query_ref[:, columns:] = lanes_of([squares])
+    query = jnp.concatenate(flat(total[:, :columns]), axis=0).astype(jnp.bfloat16)
+    pads = -half % LANES
+    stat = [jnp.pad(term, ((0, pads), (0, 0))) for term in split3(squares)]
+    lane = lax.broadcasted_iota(jnp.int32, (half + pads, half + pads), 1)
+    row = lax.broadcasted_iota(jnp.int32, (half + pads, half + pads), 0)
+    stat = [jnp.sum(jnp.where(lane == row, t, 0.0), axis=0, keepdims=True) for t in stat]
+    stat = jnp.concatenate(stat + [jnp.zeros((ROWS - 3, half + pads), jnp.float32)], axis=0)
+    stat = jnp.concatenate(flat(stat), axis=0).astype(jnp.bfloat16)
     line = place_ref[0] // 2
+    chunks = columns // LANES
 
     def rows_of(group):
         return total[pl.ds(pl.multiple_of(group * share, share), share), columns : 3 * columns]
 
     fresh_ref[...] = rows_of(line)
     for m, send in enumerate(sends, 1):
-        other = rows_of(line ^ m)
-        both = jnp.concatenate([other[:, :columns], other[:, columns:]], axis=0)
-        send[:half, :columns] = query
-        send[:half, columns:] = stat
-        send[half:, :columns] = both.astype(jnp.bfloat16)
-        send[half:, columns:] = jnp.zeros((2 * share, LANES), jnp.bfloat16)
+        other = jnp.concatenate(flat(rows_of(line ^ m)), axis=0)
+        send[: chunks * half, :] = query
+        send[chunks * half : chunks * (half + 2 * share), :] = other.astype(jnp.bfloat16)
+        send[chunks * (half + 2 * share) :, :] = stat
 
 
 def finish_kernel(width, place_ref, after_ref, query_ref, fresh_ref, cos_ref, sin_ref, *rest):
     received, out_ref, news_ref = rest[:-2], rest[-2], rest[-1]
     half, columns = out_ref.shape
     share = fresh_ref.shape[0]
-    total = query_ref[...]
-    fresh = fresh_ref[...]
+    chunks = columns // LANES
+    total = flat(query_ref[:, :columns])
+    squares = query_ref[:, columns : columns + 1]
+    fresh = flat(fresh_ref[...])
+    pads = -half % LANES
+    stat = jnp.zeros((ROWS * (half + pads) // LANES, LANES), jnp.float32)
     for piece in received:
-        total = total + piece[:half, :].astype(jnp.float32)
-        extra = piece[half:, :columns].astype(jnp.float32)
-        fresh = fresh + jnp.concatenate([extra[:share], extra[share:]], axis=1)
-    squares = jnp.sum(total[:, columns:], axis=1, keepdims=True)
+        for c in range(chunks):
+            total[c] = total[c] + piece[c * half : (c + 1) * half, :].astype(jnp.float32)
+        extra = piece[chunks * half : chunks * (half + 2 * share), :].astype(jnp.float32)
+        for c in range(2 * chunks):
+            fresh[c] = fresh[c] + extra[c * share : (c + 1) * share]
+        stat = stat + piece[chunks * (half + 2 * share) :, :].astype(jnp.float32)
+    total = jnp.concatenate(total, axis=1)
+    fresh = jnp.concatenate(fresh, axis=1)
+    stat = [jnp.sum(stat[r : r + ROWS], axis=0, keepdims=True) for r in range(0, stat.shape[0], ROWS)]
+    stat = jnp.concatenate(stat, axis=1)[:, :half] if len(stat) * LANES == half else stat[0]
+    lane = lax.broadcasted_iota(jnp.int32, (half, stat.shape[1]), 1)
+    row = lax.broadcasted_iota(jnp.int32, (half, stat.shape[1]), 0)
+    squares = squares + jnp.sum(jnp.where(lane == row, stat, 0.0), axis=1, keepdims=True)
     inverse = lax.rsqrt(squares * (1.0 / width) + EPSILON)
     span = HEAD_DIM // 2
 
@@ -150,44 +172,31 @@
     news_ref[:, columns:] = jnp.concatenate([stat, none], axis=0).astype(jnp.bfloat16)
 
 
+def stage(part, cache_ref, near_ref, updated_ref, loads, stores):
+    spans = [pl.ds(first, GROUP) for first in range(0, cache_ref.shape[0], GROUP)]
+    load = [
+        pltpu.make_async_copy(cache_ref.at[span, part], near_ref.at[span], loads.at[i])
+        for i, span in enumerate(spans)
+    ]
+    store = [
+        pltpu.make_async_copy(near_ref.at[span], updated_ref.at[span, part], stores.at[i])
+        for i, span in enumerate(spans)
+    ]
+    for copy in load:
+        copy.start()
+    for arriving, leaving in zip(load, store):
+        arriving.wait()
+        leaving.start()
+    for copy in store:
+        copy.wait()
+
+
 def stage_keys_kernel(cache_ref, keys_ref, updated_ref, loads, stores):
-    steps = cache_ref.shape[0] // GROUP
-
-    def load(step):
-        part = pl.ds(step * GROUP, GROUP)
-        return pltpu.make_async_copy(cache_ref.at[part, 0], keys_ref.at[part], loads.at[step])
-
-    def store(step):
-        part = pl.ds(step * GROUP, GROUP)
-        return pltpu.make_async_copy(keys_ref.at[part], updated_ref.at[part, 0], stores.at[step])
-
-    for step in range(steps):
-        load(step).start()
-    for step in range(steps):
-        load(step).wait()
-        store(step).start()
-    for step in range(steps):
-        store(step).wait()
-
-
-def stage_values_kernel(cache_ref, held_ref, updated_ref, near, loads, stores):
-    steps = cache_ref.shape[0] // GROUP
-
-    def load(step):
-        part = pl.ds(step * GROUP, GROUP)
-        return pltpu.make_async_copy(cache_ref.at[part, 1], near.at[part], loads.at[step])
-
-    def store(step):
-        part = pl.ds(step * GROUP, GROUP)
-        return pltpu.make_async_copy(near.at[part], updated_ref.at[part, 1], stores.at[step])
-
-    for step in range(steps):
-        load(step).start()
-    for step in range(steps):
-        load(step).wait()
-        store(step).start()
-    for step in range(steps):
-        store(step).wait()
+    stage(0, cache_ref, keys_ref, updated_ref, loads, stores)
+
+
+def stage_values_kernel(cache_ref, held_ref, values_ref, updated_ref, loads, stores):
+    stage(1, cache_ref, values_ref, updated_ref, loads, stores)
 
 
 def read_block(b, owner_ref, index_ref, length_ref, tokens):
@@ -236,24 +245,12 @@
     name_ref,
     news_ref,
     keys_ref,
-    cache_ref,
+    values_ref,
     out_ref,
-    near,
-    sems,
 ):
-    blocks, _, tokens, columns = cache_ref.shape
+    blocks, tokens, columns = keys_ref.shape
     extra = news_ref.shape[0]
     steps = blocks // GROUP
-    copies = [
-        pltpu.make_async_copy(
-            cache_ref.at[pl.ds(step * GROUP, GROUP), 1],
-            near.at[pl.ds(step * GROUP, GROUP)],
-            sems.at[step],
-        )
-        for step in range(steps)
-    ]
-    for copy in copies:
-        copy.start()
     out_ref[:extra, :] = news_ref[...]
 
     def iota(shape, dim):
@@ -288,8 +285,7 @@
     mass = jnp.sum(weights.astype(jnp.float32), axis=1, keepdims=True)
     parts = []
     for step in range(steps):
-        copies[step].wait()
-        values = near[step * GROUP : (step + 1) * GROUP].reshape(width, columns)
+        values = values_ref[step * GROUP : (step + 1) * GROUP].reshape(width, columns)
         parts.append(
             jnp.dot(
                 weights[step * size : (step + 1) * size],
@@ -313,54 +309,60 @@
     out_ref[extra:, columns:] = stat[:blocks].astype(jnp.bfloat16)
 
 
+def each_slot(tokens, owner_ref, index_ref, length_ref, do):
+    for b in range(owner_ref.shape[0]):
+        owner, _, slot = read_block(b, owner_ref, index_ref, length_ref, tokens)
+        first = pl.multiple_of(jnp.maximum(slot, 0) // ROWS * ROWS, ROWS)
+        pl.when(slot >= 0)(functools.partial(do, b, owner, slot, first))
+
+
+def fetch_kernel(owner_ref, index_ref, length_ref, after_ref, cache_ref, near_ref, loads):
+    tokens = cache_ref.shape[2]
+
+    def fetch(b, owner, slot, first):
+        return pltpu.make_async_copy(
+            cache_ref.at[b, :, pl.ds(first, ROWS), :], near_ref.at[b], loads.at[b]
+        )
+
+    each_slot(tokens, owner_ref, index_ref, length_ref, lambda *at: fetch(*at).start())
+    each_slot(tokens, owner_ref, index_ref, length_ref, lambda *at: fetch(*at).wait())
+
+
 def patch_kernel(count, place_ref, owner_ref, index_ref, length_ref, after_ref, *rest):
-    pieces, cache_ref, held_ref, updated_ref = rest[:count], rest[count], rest[count + 1], rest[count + 2]
-    fresh, patch, loads, stores = rest[count + 3 :]
-    blocks, _, tokens, columns = cache_ref.shape
+    pieces, near_ref, held_ref, updated_ref = rest[:count], rest[count], rest[count + 1], rest[count + 2]
+    fresh, patch, stores = rest[count + 3 :]
+    _, _, tokens, columns = updated_ref.shape
     requests = length_ref.shape[0]
     share = fresh.shape[1] // 2
     half = requests // 2
-
-    def each(do):
-        for b in range(blocks):
-            owner, _, slot = read_block(b, owner_ref, index_ref, length_ref, tokens)
-            first = pl.multiple_of(jnp.maximum(slot, 0) // ROWS * ROWS, ROWS)
-            pl.when(slot >= 0)(functools.partial(do, b, owner, slot, first))
-
-    def fetch(b, owner, slot, first):
-        return pltpu.make_async_copy(
-            cache_ref.at[b, :, pl.ds(first, ROWS), :], patch.at[b], loads.at[b]
-        )
 
     def store(b, owner, slot, first):
         return pltpu.make_async_copy(
             patch.at[b], updated_ref.at[b, :, pl.ds(first, ROWS), :], stores.at[b]
         )
 
-    each(lambda *at: fetch(*at).start())
     for m in range(count):
         fresh[m] = pieces[m][: 2 * share, :columns].astype(jnp.float32)
     row = lax.broadcasted_iota(jnp.int32, (ROWS, columns), 0)
 
     def change(b, owner, slot, first):
-        fetch(b, owner, slot, first).wait()
         request = jnp.minimum(owner, requests - 1)
         device = request % half // share * 2 + request // half
         piece = place_ref[0] ^ device
         line = request % share
         for c in range(2):
             new = fresh[piece, pl.ds(line + (1 - c) * share, 1), :]
-            old = patch[b, c].astype(jnp.float32)
+            old = near_ref[b, c].astype(jnp.float32)
             patch[b, c] = jnp.where(row == slot - first, new, old).astype(jnp.bfloat16)
         store(b, owner, slot, first).start()
 
-    each(change)
-    each(lambda *at: store(*at).wait())
+    each_slot(tokens, owner_ref, index_ref, length_ref, change)
+    each_slot(tokens, owner_ref, index_ref, length_ref, lambda *at: store(*at).wait())
 
 
 def output_kernel(count, place_ref, *rest):
-    pieces, w_ref, states_ref, own_ref = rest[:count], rest[count], rest[count + 1], rest[count + 2]
-    sends, product = rest[count + 3 : -1], rest[-1]
+    pieces, w_ref, states_ref, own_ref = rest[:count], rest[count], rest[count + 1], rest[count + 3]
+    sends, product = rest[count + 4 : -1], rest[-1]
     heads = HEADS
     blocks, wide = pieces[0].shape
     columns = wide - LANES
@@ -482,10 +484,11 @@
         name="stage_keys",
     )(cache)
 
+    message = columns // LANES * (half + 2 * share) + ROWS * pl.cdiv(half, LANES)
     *sends, query, fresh = pl.pallas_call(
         halve_kernel,
         out_shape=(
-            *(array(half + 2 * share, columns + LANES) for _ in range(1, lines)),
+            *(array(message, LANES) for _ in range(1, lines)),
             array(half, columns + LANES, dtype=jnp.float32),
             array(share, 2 * columns, dtype=jnp.float32),
         ),
@@ -494,72 +497,84 @@
         compiler_params=limit,
         name="halve",
     )(at, kept, received, keys)
-    received = [to_peer(send, 2 * m) for m, send in enumerate(sends, 1)]
-    updated = pl.pallas_call(
+    received = [to_peer(sends[m - 1], 2 * m) for m in sorted(range(1, lines), key=lambda m: m)]
+    values, updated = pl.pallas_call(
         stage_values_kernel,
-        out_shape=array(*cache.shape),
+        out_shape=(array(blocks, tokens, columns), array(*cache.shape)),
         in_specs=[in_hbm, in_hbm],
-        out_specs=in_hbm,
-        scratch_shapes=[pltpu.VMEM((blocks, tokens, columns), jnp.bfloat16)]
-        + [pltpu.SemaphoreType.DMA((steps,))] * 2,
-        input_output_aliases={1: 0},
-        compiler_params=most_room,
+        out_specs=(in_vmem, in_hbm),
+        scratch_shapes=[pltpu.SemaphoreType.DMA((steps,))] * 2,
+        input_output_aliases={1: 1},
+        compiler_params=pltpu.CompilerParams(vmem_limit_bytes=47 * 1024 * 1024),
         cost_estimate=moves(cache.size * 2),
         name="stage_values",
     )(cache, updated)
     mine, news = pl.pallas_call(
         functools.partial(finish_kernel, depth * peers),
         out_shape=(array(half, columns), array(2 * share, columns + LANES)),
-        in_specs=[in_smem, in_hbm] + [in_vmem] * (4 + len(received)),
-        compiler_params=most_room,
+        in_specs=[in_smem, anywhere] + [in_vmem] * (4 + len(received)),
+        compiler_params=pltpu.CompilerParams(vmem_limit_bytes=47 * 1024 * 1024),
         name="finish",
-    )(at, updated, query, fresh, jnp.cos(angles), jnp.sin(angles), *received)
+    )(at, values, query, fresh, jnp.cos(angles), jnp.sin(angles), *received)
     other = to_peer(mine, 1)
 
     piece = pl.pallas_call(
         attend_kernel,
         out_shape=array(2 * share + blocks, columns + LANES),
-        in_specs=[in_vmem] * 8 + [in_hbm],
-        scratch_shapes=[
-            pltpu.VMEM((blocks, tokens, columns), jnp.bfloat16),
-            pltpu.SemaphoreType.DMA((steps,)),
-        ],
+        in_specs=[in_vmem] * 9,
+        compiler_params=pltpu.CompilerParams(vmem_limit_bytes=47 * 1024 * 1024),
+        name="attend",
+    )(mine, other, *plan, news, keys, values)
+    pieces = [piece] * peers
+    far = sorted(range(1, lines), key=lambda m: m)
+    for m in far:
+        pieces[2 * m] = to_peer(piece, 2 * m)
+    for m in (*far, 0):
+        pieces[2 * m + 1] = to_peer(pieces[2 * m], 1)
+
+    near = pl.pallas_call(
+        fetch_kernel,
+        out_shape=array(blocks, 2, ROWS, columns),
+        in_specs=[in_smem] * 3 + [anywhere, in_hbm],
+        out_specs=in_vmem,
+        scratch_shapes=[pltpu.SemaphoreType.DMA((blocks,))],
         compiler_params=most_room,
-        name="attend",
-    )(mine, other, *plan, news, keys, cache)
-    column = [piece] + [to_peer(piece, 2 * m) for m in range(1, lines)]
-    pieces = [p for near in column for p in (near, to_peer(near, 1))]
-
+        cost_estimate=moves(blocks * ROWS * columns * 8),
+        name="fetch",
+    )(*table, piece, cache)
     rank = lax.axis_index("tp")
     kept_rows = requests // ranks
     own, *sends = pl.pallas_call(
         functools.partial(output_kernel, peers),
-        out_shape=tuple(array(kept_rows, out_columns, dtype=jnp.float32) for _ in range(ranks)),
-        in_specs=[in_smem] + [in_vmem] * (peers + 2),
+        out_shape=(
+            array(kept_rows, out_columns, dtype=jnp.float32),
+            *(array(kept_rows, out_columns, dtype=jnp.float32) for _ in range(1, ranks)),
+        ),
+        in_specs=[in_smem] + [in_vmem] * (peers + 2) + [anywhere],
         out_specs=(in_vmem,) * ranks,
         scratch_shapes=[pltpu.VMEM((requests, out_columns), jnp.float32)],
         compiler_params=limit,
         name="output",
-    )(rank.reshape(1).astype(jnp.int32), *pieces, w_out, states)
+    )(rank.reshape(1).astype(jnp.int32), *pieces, w_out, states, near)
     total = own
-    for m, send in enumerate(sends, 1):
-        total = total + lax.ppermute(send, "tp", [(i, i ^ m) for i in range(ranks)])
+    for m in range(1, ranks):
+        moved = lax.ppermute(sends[m - 1], "tp", [(i, i ^ m) for i in range(ranks)])
+        total = total + moved.astype(jnp.float32)
     updated = pl.pallas_call(
         functools.partial(patch_kernel, peers),
         out_shape=array(*cache.shape),
-        in_specs=[in_smem] * 4 + [anywhere] + [in_vmem] * peers + [in_hbm] * 2,
+        in_specs=[in_smem] * 4 + [anywhere] + [in_vmem] * (peers + 1) + [in_hbm],
         out_specs=in_hbm,
         scratch_shapes=[
             pltpu.VMEM((peers, 2 * share, columns), jnp.float32),
             pltpu.VMEM((blocks, 2, ROWS, columns), jnp.bfloat16),
             pltpu.SemaphoreType.DMA((blocks,)),
-            pltpu.SemaphoreType.DMA((blocks,)),
         ],
         input_output_aliases={6 + peers: 0},
         compiler_params=most_room,
-        cost_estimate=moves(cache.size),
+        cost_estimate=moves(blocks * ROWS * columns * 8),
         name="patch",
-    )(at, *table, sends[0], *pieces, cache, updated)
+    )(at, *table, sends[0], *pieces, near, updated)
     return (total.astype(jnp.bfloat16), updated)
 
 

time: 49.9 us -> 46.7 us (0.936)
  waiting for transfers between devices: 9.94 us -> 7.95 us
  Pallas kernels: 16.5 us -> 15.3 us
    ppermute x12, waiting for transfers between devices: 9.93 us -> 7.94 us  [to_peer(): return lax.ppermute(value, 'seq', [(i, i ^ m) for i in range(peers)])]
    pallas_call x1, Pallas kernels: 3.2 us -> 1.44 us  [shards(): pl.pallas_call(attend_kernel, out_shape=array(2 * share + blocks, columns...]
    pallas_call x3 -> x4, Pallas kernels: 4.13 us -> 5.42 us  [the longest x1 1.87 us: shards(): pl.pallas_call(stage_values_kernel, out_shape=(array(blocks, tokens, colu...]
    pallas_call x1, Pallas kernels: 3.03 us -> 2.05 us  [shards(): pl.pallas_call(functools.partial(patch_kernel, peers), out_shape=array(*c...]
  transfers between devices with their start and end apart: 15 -> 15, of which waited for: 8 -> 6; matrix products, arithmetic and copies ran while one was open for 2% -> 3% of each run, Pallas kernels for 18% -> 19%
where the time goes in v4:
time: 46.7 us; the launch traced here: 46.5 us
  starting transfers between devices  20.5 us (44%)
  Pallas kernels  15.3 us (33%)
  waiting for transfers between devices  7.95 us (17%)
  other arithmetic  1.77 us (4%)
  between operations  0.87 us (2%)
    ppermute x12, starting transfers between devices, to_peer(): return lax.ppermute(value, 'seq', [(i, i ^ m) for i in range(peers)])  18.6 us
    ppermute x12, waiting for transfers between devices, to_peer(): return lax.ppermute(value, 'seq', [(i, i ^ m) for i in range(peers)])  7.94 us
    pallas_call x1, Pallas kernels, shards(): pl.pallas_call(project_kernel, out_shape=(array(half, parts * columns + L...  2.7 us
    pallas_call x1, Pallas kernels, shards(): pl.pallas_call(stage_keys_kernel, out_shape=(array(blocks, tokens, column...  2.64 us
    pallas_call x1, Pallas kernels, shards(): pl.pallas_call(functools.partial(patch_kernel, peers), out_shape=array(*c...  2.05 us
    ppermute x3, starting transfers between devices, shards(): moved = lax.ppermute(sends[m - 1], 'tp', [(i, i ^ m) for i in range(ranks)])  1.92 us
    pallas_call x1, Pallas kernels, shards(): pl.pallas_call(stage_values_kernel, out_shape=(array(blocks, tokens, colu...  1.87 us
    pallas_call x1, Pallas kernels, shards(): pl.pallas_call(fetch_kernel, out_shape=array(blocks, 2, ROWS, columns), i...  1.83 us
  transfers between devices with their start and end apart: 15, of which 6 were waited for; matrix products, arithmetic and copies ran while one was open for 3% of the time, Pallas kernels for 19%

profile of v4, /device:TPU:0, one launch (start us, length us, event | category | flops | bytes accessed | tf_op | source)
XLA Modules:
  0.0 46.5 jit_solution(15160219284149035847)
XLA Ops:
  0.6 2.7 %project.1 = (bf16[32,2432]{1,0:T(8,128)(2,1)}, f32[32,2432]{1,0:T(8,128)}) custom-call(s32[1]{0:T(128)} %bitcast.1.place_ref, bf16[64,384]{1,0:T(8,128)(2,1)} %rest_9_.1, bf16[384]{0:T(512)(128)(2,1)} %gain_ref.1, bf16[3,384,768]{2,1,0:T(8,128)(2,1)} %w_ref.1), custom_call_target="tpu_custom_call" | custom-call | tf_op jit(solution)/shard_map/project/pallas_call | solution.py:439
  3.4 3.0 %collective-permute-start = (bf16[32,2432]{1,0:T(8,128)(2,1)}, bf16[32,2432]{1,0:T(8,128)(2,1)S(1)}, u32[]{:S(2)}, u32[]{:S(2)}) collective-permute-start(bf16[32,2432]{1,0:T(8,128)(2,1)} %get-tuple-element.26), channel_id=1, source_target_pairs={{0,4},{4,0},{8,12},{12,8},{16,20},{20,16},{24,28},{28,24},{1,5},{5... | collective-permute-start | bytes 466952 | tf_op jit(solution)/shard_map/ppermute | solution.py:434
  6.4 0.7 %add_convert_fusion.1 = f32[32]{0:T(128)S(1)} fusion(s32[64]{0:T(128)} %length_ref.5, s32[]{:T(128)S(6)} %select_n.21), kind=kLoop, calls=%fused_computation.12 | loop fusion | flops 64 | bytes 260 | tf_op jit(solution)/shard_map/convert_element_type | solution.py:461
  7.1 2.6 %stage_keys.1 = (bf16[24,64,768]{2,1,0:T(8,128)(2,1)S(1)}, bf16[24,2,64,768]{3,2,1,0:T(8,128)(2,1)}) custom-call(bf16[24,2,64,768]{3,2,1,0:T(8,128)(2,1)} %cache_ref.5), custom_call_target="tpu_custom_call" | custom-call | bytes 4718592 | tf_op jit(solution)/shard_map/stage_keys/pallas_call | solution.py:476
  9.8 0.8 %collective-permute-done.recv_ref = bf16[32,2432]{1,0:T(8,128)(2,1)S(1)} collective-permute-done((bf16[32,2432]{1,0:T(8,128)(2,1)}, bf16[32,2432]{1,0:T(8,128)(2,1)S(1)}, u32[]{:S(2)}, u32[]{:S(2)}) %collective-permute-start) | collective-permute-done | bytes 155680 | tf_op jit(solution)/shard_map/ppermute | solution.py:434
  10.6 0.2 halve.1
  10.8 1.9 %collective-permute-start.1 = (bf16[304,128]{1,0:T(8,128)(2,1)S(1)}, bf16[304,128]{1,0:T(8,128)(2,1)S(1)}, u32[]{:S(2)}, u32[]{:S(2)}) collective-permute-start(bf16[304,128]{1,0:T(8,128)(2,1)S(1)} %get-tuple-element.30), channel_id=1, source_target_pairs={{0,8},{4,12},{8,0},{12,4},{16,24},{20,28},{24,16},{28,20},{1,9},{5... | collective-permute-start | bytes 233480 | tf_op jit(solution)/shard_map/ppermute | solution.py:434
  12.7 2.6 %collective-permute-start.2 = (bf16[304,128]{1,0:T(8,128)(2,1)S(1)}, bf16[304,128]{1,0:T(8,128)(2,1)S(1)}, u32[]{:S(2)}, u32[]{:S(2)}) collective-permute-start(bf16[304,128]{1,0:T(8,128)(2,1)S(1)} %get-tuple-element.31), channel_id=1, source_target_pairs={{0,16},{4,20},{8,24},{12,28},{16,0},{20,4},{24,8},{28,12},{1,17},{... | collective-permute-start | bytes 233480 | tf_op jit(solution)/shard_map/ppermute | solution.py:434
  15.3 0.4 multiply_sine_fusion
  15.8 1.9 %stage_values.1 = (bf16[24,64,768]{2,1,0:T(8,128)(2,1)S(1)}, bf16[24,2,64,768]{3,2,1,0:T(8,128)(2,1)}) custom-call(bf16[24,2,64,768]{3,2,1,0:T(8,128)(2,1)S(1)} %bitcast.3, bf16[24,2,64,768]{3,2,1,0:T(8,128)(2,1)} %get-tuple-element.23.held_ref), custom_call_target="tpu_custom_call", output_to_operand_aliasing={{1}: (1, {})} | custom-call | bytes 4718592 | tf_op jit(solution)/shard_map/stage_values/pallas_call | solution.py:501
  17.6 2.2 %collective-permute-done.2.rest_1_ = bf16[304,128]{1,0:T(8,128)(2,1)S(1)} collective-permute-done((bf16[304,128]{1,0:T(8,128)(2,1)S(1)}, bf16[304,128]{1,0:T(8,128)(2,1)S(1)}, u32[]{:S(2)}, u32[]{:S(2)}) %collective-permute-start.2) | collective-permute-done | bytes 77856 | tf_op jit(solution)/shard_map/ppermute | solution.py:434
  19.9 1.7 %collective-permute-done.3.rest_2_ = bf16[304,128]{1,0:T(8,128)(2,1)S(1)} collective-permute-done((bf16[304,128]{1,0:T(8,128)(2,1)S(1)}, bf16[304,128]{1,0:T(8,128)(2,1)S(1)}, u32[]{:S(2)}, u32[]{:S(2)}) %collective-permute-start.3) | collective-permute-done | bytes 77856 | tf_op jit(solution)/shard_map/ppermute | solution.py:434
  21.5 0.4 finish.1
  22.0 1.6 %collective-permute-start.4 = (bf16[32,768]{1,0:T(8,128)(2,1)S(1)}, bf16[32,768]{1,0:T(8,128)(2,1)S(1)}, u32[]{:S(2)}, u32[]{:S(2)}) collective-permute-start(bf16[32,768]{1,0:T(8,128)(2,1)S(1)} %get-tuple-element.33.mine_ref), channel_id=1, source_target_pairs={{0,4},{4,0},{8,12},{12,8},{16,20},{20,16},{24,28},{28,24},{1,5},{5... | collective-permute-start | bytes 147464 | tf_op jit(solution)/shard_map/ppermute | solution.py:434
  23.5 0.7 %plan.1 = (bf16[192,32]{1,0:T(8,128)(2,1)S(1)}, bf16[192,32]{1,0:T(8,128)(2,1)S(1)}, s32[192,128]{1,0:T(8,128)S(1)}, f32[192,128]{1,0:T(8,128)S(1)}) custom-call(s32[1]{0:T(128)} %bitcast.1.place_ref, s32[24]{0:T(128)S(1)} %copy-done.4, s32[24]{0:T(128)S(1)} %copy-done.5, s32[64]{0:T(128)S(1)} %copy-done.3), custom_call_target="tpu_custom_call" | custom-call | tf_op jit(solution)/shard_map/plan/pallas_call | solution.py:464
  24.2 1.9 %collective-permute-done.4.other_ref = bf16[32,768]{1,0:T(8,128)(2,1)S(1)} collective-permute-done((bf16[32,768]{1,0:T(8,128)(2,1)S(1)}, bf16[32,768]{1,0:T(8,128)(2,1)S(1)}, u32[]{:S(2)}, u32[]{:S(2)}) %collective-permute-start.4) | collective-permute-done | bytes 49184 | tf_op jit(solution)/shard_map/ppermute | solution.py:434
  26.1 1.4 %attend.1.after_ref.rest_0_ = bf16[40,896]{1,0:T(8,128)(2,1)S(1)} custom-call(bf16[32,768]{1,0:T(8,128)(2,1)S(1)} %get-tuple-element.33.mine_ref, bf16[32,768]{1,0:T(8,128)(2,1)S(1)} %collective-permute-done.4.other_ref, bf16[192,32]{1,0:T(8,128)(2,1)S(1)} %get-tuple-element.34.pick_mine_ref, bf16[192,32]{1,0:T(8,128)(2,1)S(1)} %get-tuple-element.35.pick_other_ref, ...), custom_call_target="tpu_custom_call" | custom-call | tf_op jit(solution)/shard_map/attend/pallas_call | solution.py:521
  27.6 0.1 collective-permute-start.6
  27.6 2.2 %collective-permute-start.8 = (bf16[40,896]{1,0:T(8,128)(2,1)S(1)}, bf16[40,896]{1,0:T(8,128)(2,1)S(1)}, u32[]{:S(2)}, u32[]{:S(2)}) collective-permute-start(bf16[40,896]{1,0:T(8,128)(2,1)S(1)} %attend.1.after_ref.rest_0_), channel_id=1, source_target_pairs={{0,16},{4,20},{8,24},{12,28},{16,0},{20,4},{24,8},{28,12},{1,17},{... | collective-permute-start | bytes 215048 | tf_op jit(solution)/shard_map/ppermute | solution.py:434
  29.8 2.2 %collective-permute-start.10 = (bf16[40,896]{1,0:T(8,128)(2,1)S(1)}, bf16[40,896]{1,0:T(8,128)(2,1)S(1)}, u32[]{:S(2)}, u32[]{:S(2)}) collective-permute-start(bf16[40,896]{1,0:T(8,128)(2,1)S(1)} %attend.1.after_ref.rest_0_), channel_id=1, source_target_pairs={{0,24},{4,28},{8,16},{12,20},{16,8},{20,12},{24,0},{28,4},{1,25},{... | collective-permute-start | bytes 215048 | tf_op jit(solution)/shard_map/ppermute | solution.py:434
  32.0 1.5 %collective-permute-start.5 = (bf16[40,896]{1,0:T(8,128)(2,1)S(1)}, bf16[40,896]{1,0:T(8,128)(2,1)S(1)}, u32[]{:S(2)}, u32[]{:S(2)}) collective-permute-start(bf16[40,896]{1,0:T(8,128)(2,1)S(1)} %attend.1.after_ref.rest_0_), channel_id=1, source_target_pairs={{0,4},{4,0},{8,12},{12,8},{16,20},{20,16},{24,28},{28,24},{1,5},{5... | collective-permute-start | bytes 215048 | tf_op jit(solution)/shard_map/ppermute | solution.py:434
  33.5 0.5 %collective-permute-start.7 = (bf16[40,896]{1,0:T(8,128)(2,1)S(1)}, bf16[40,896]{1,0:T(8,128)(2,1)S(1)}, u32[]{:S(2)}, u32[]{:S(2)}) collective-permute-start(bf16[40,896]{1,0:T(8,128)(2,1)S(1)} %collective-permute-done.6.rest_2_), channel_id=1, source_target_pairs={{0,4},{4,0},{8,12},{12,8},{16,20},{20,16},{24,28},{28,24},{1,5},{5... | collective-permute-start | bytes 215048 | tf_op jit(solution)/shard_map/ppermute | solution.py:434
  34.0 1.5 %collective-permute-start.9 = (bf16[40,896]{1,0:T(8,128)(2,1)S(1)}, bf16[40,896]{1,0:T(8,128)(2,1)S(1)}, u32[]{:S(2)}, u32[]{:S(2)}) collective-permute-start(bf16[40,896]{1,0:T(8,128)(2,1)S(1)} %collective-permute-done.8.rest_4_), channel_id=1, source_target_pairs={{0,4},{4,0},{8,12},{12,8},{16,20},{20,16},{24,28},{28,24},{1,5},{5... | collective-permute-start | bytes 215048 | tf_op jit(solution)/shard_map/ppermute | solution.py:434
  35.6 0.4 collective-permute-done.10.rest_6_
  36.0 1.5 %collective-permute-start.11 = (bf16[40,896]{1,0:T(8,128)(2,1)S(1)}, bf16[40,896]{1,0:T(8,128)(2,1)S(1)}, u32[]{:S(2)}, u32[]{:S(2)}) collective-permute-start(bf16[40,896]{1,0:T(8,128)(2,1)S(1)} %collective-permute-done.10.rest_6_), channel_id=1, source_target_pairs={{0,4},{4,0},{8,12},{12,8},{16,20},{20,16},{24,28},{28,24},{1,5},{5... | collective-permute-start | bytes 215048 | tf_op jit(solution)/shard_map/ppermute | solution.py:434
  37.5 1.8 %fetch.1.rest_10_.rest_8_ = bf16[24,2,16,768]{3,2,1,0:T(8,128)(2,1)S(1)} custom-call(s32[24]{0:T(128)S(1)} %copy-done.4, s32[24]{0:T(128)S(1)} %copy-done.5, s32[64]{0:T(128)S(1)} %copy-done.3, bf16[40,896]{1,0:T(8,128)(2,1)S(1)} %attend.1.after_ref.rest_0_, bf16[24,2,64,768]{3,2,1,0:T(8,128)(2,1)} %cache_ref.5), custom_call_target="tpu_custom_call" | custom-call | bytes 2359296 | tf_op jit(solution)/shard_map/fetch/pallas_call | solution.py:535
  39.4 0.9 %collective-permute-done.11.rest_7_ = bf16[40,896]{1,0:T(8,128)(2,1)S(1)} collective-permute-done((bf16[40,896]{1,0:T(8,128)(2,1)S(1)}, bf16[40,896]{1,0:T(8,128)(2,1)S(1)}, u32[]{:S(2)}, u32[]{:S(2)}) %collective-permute-start.11) | collective-permute-done | bytes 71712 | tf_op jit(solution)/shard_map/ppermute | solution.py:434
  40.3 1.5 %output.1 = (f32[16,384]{1,0:T(8,128)S(1)}, f32[16,384]{1,0:T(8,128)S(1)}, f32[16,384]{1,0:T(8,128)S(1)}, f32[16,384]{1,0:T(8,128)S(1)}) custom-call(s32[1]{0:T(128)} %bitcast.place_ref, bf16[40,896]{1,0:T(8,128)(2,1)S(1)} %attend.1.after_ref.rest_0_, bf16[40,896]{1,0:T(8,128)(2,1)S(1)} %collective-permute-done.5.rest_1_, ...), custom_call_target="tpu_custom_call" | custom-call | tf_op jit(solution)/shard_map/output/pallas_call | solution.py:547
  41.9 1.5 %collective-permute-start.13 = (f32[16,384]{1,0:T(8,128)S(1)}, f32[16,384]{1,0:T(8,128)S(1)}, u32[]{:S(2)}, u32[]{:S(2)}) collective-permute-start(f32[16,384]{1,0:T(8,128)S(1)} %get-tuple-element.41), channel_id=1, source_target_pairs={{0,2},{1,3},{2,0},{3,1},{4,6},{5,7},{6,4},{7,5},{8,10},{9,11},{10,... | collective-permute-start | bytes 73736 | tf_op jit(solution)/shard_map/ppermute | solution.py:561
  43.5 0.3 collective-permute-start.12
  43.8 2.0 %patch.1 = bf16[24,2,64,768]{3,2,1,0:T(8,128)(2,1)} custom-call(s32[1]{0:T(128)} %bitcast.1.place_ref, s32[24]{0:T(128)S(1)} %copy-done.4, s32[24]{0:T(128)S(1)} %copy-done.5, s32[64]{0:T(128)S(1)} %copy-done.3, f32[16,384]{1,0:T(8,128)S(1)} %get-tuple-element.40.after_ref, ...), custom_call_target="tpu_custom_call", output_to_operand_aliasing={{}: (14, {})} | custom-call | bytes 2359296 | tf_op jit(solution)/shard_map/patch/pallas_call | solution.py:563
  45.9 0.6 %add_convert_fusion = bf16[16,384]{1,0:T(8,128)(2,1)} fusion(f32[16,384]{1,0:T(8,128)S(1)} %collective-permute-done.14, f32[16,384]{1,0:T(8,128)S(1)} %collective-permute-done.13, f32[16,384]{1,0:T(8,128)S(1)} %get-tuple-element.39, f32[16,384]{1,0:T(8,128)S(1)} %collective-permute-done.12), kind=kLoop, calls=%fused_computation.2 | loop fusion | flops 24576 | bytes 110592 | tf_op jit(solution)/shard_map/convert_element_type | solution.py:578
  (29 shorter events, 0.2 us)
Async XLA Ops:
  0.6 15.1 %slice-start = ((s8[4718592]{0:T(1024)(128)(4,1)}), s8[524288]{0:T(1024)(128)(4,1)S(1)}, s32[]{:S(2)}) async-start(s8[4718592]{0:T(1024)(128)(4,1)} %bitcast.2), calls=%async_computation | async-start | bytes 1048576
  3.4 7.3 %copy-start.1 = (f32[32,2432]{1,0:T(8,128)S(1)}, f32[32,2432]{1,0:T(8,128)}, u32[]{:S(2)}) copy-start(f32[32,2432]{1,0:T(8,128)} %get-tuple-element.25.kept_ref) | copy-start | bytes 933892
  3.4 7.3 %collective-permute-start = (bf16[32,2432]{1,0:T(8,128)(2,1)}, bf16[32,2432]{1,0:T(8,128)(2,1)S(1)}, u32[]{:S(2)}, u32[]{:S(2)}) collective-permute-start(bf16[32,2432]{1,0:T(8,128)(2,1)} %get-tuple-element.26), channel_id=1, source_target_pairs={{0,4},{4,0},{8,12},{12,8},{16,20},{20,16},{24,28},{28,24},{1,5},{5... | collective-permute-start | bytes 466952 | tf_op jit(solution)/shard_map/ppermute | solution.py:434
  7.1 8.6 %slice-start.1 = ((s8[4718592]{0:T(1024)(128)(4,1)}), s8[4194304]{0:T(1024)(128)(4,1)S(1)}, s32[]{:S(2)}) async-start(s8[4718592]{0:T(1024)(128)(4,1)} %bitcast.2), calls=%async_computation.1 | async-start | bytes 8388608
  10.8 6.8 %collective-permute-start.1 = (bf16[304,128]{1,0:T(8,128)(2,1)S(1)}, bf16[304,128]{1,0:T(8,128)(2,1)S(1)}, u32[]{:S(2)}, u32[]{:S(2)}) collective-permute-start(bf16[304,128]{1,0:T(8,128)(2,1)S(1)} %get-tuple-element.30), channel_id=1, source_target_pairs={{0,8},{4,12},{8,0},{12,4},{16,24},{20,28},{24,16},{28,20},{1,9},{5... | collective-permute-start | bytes 233480 | tf_op jit(solution)/shard_map/ppermute | solution.py:434
  12.7 7.2 %collective-permute-start.2 = (bf16[304,128]{1,0:T(8,128)(2,1)S(1)}, bf16[304,128]{1,0:T(8,128)(2,1)S(1)}, u32[]{:S(2)}, u32[]{:S(2)}) collective-permute-start(bf16[304,128]{1,0:T(8,128)(2,1)S(1)} %get-tuple-element.31), channel_id=1, source_target_pairs={{0,16},{4,20},{8,24},{12,28},{16,0},{20,4},{24,8},{28,12},{1,17},{... | collective-permute-start | bytes 233480 | tf_op jit(solution)/shard_map/ppermute | solution.py:434
  15.3 6.3 %collective-permute-start.3 = (bf16[304,128]{1,0:T(8,128)(2,1)S(1)}, bf16[304,128]{1,0:T(8,128)(2,1)S(1)}, u32[]{:S(2)}, u32[]{:S(2)}) collective-permute-start(bf16[304,128]{1,0:T(8,128)(2,1)S(1)} %get-tuple-element.32), channel_id=1, source_target_pairs={{0,24},{4,28},{8,16},{12,20},{16,8},{20,12},{24,0},{28,4},{1,25},{... | collective-permute-start | bytes 233480 | tf_op jit(solution)/shard_map/ppermute | solution.py:434
  15.7 7.8 %copy-start.3 = (s32[64]{0:T(128)S(1)}, s32[64]{0:T(128)}, u32[]{:S(2)}) copy-start(s32[64]{0:T(128)} %length_ref.5) | copy-start | bytes 772
  15.7 7.8 %copy-start.4 = (s32[24]{0:T(128)S(1)}, s32[24]{0:T(128)}, u32[]{:S(2)}) copy-start(s32[24]{0:T(128)} %owner_ref.5) | copy-start | bytes 292
  15.8 7.8 %copy-start.5 = (s32[24]{0:T(128)S(1)}, s32[24]{0:T(128)}, u32[]{:S(2)}) copy-start(s32[24]{0:T(128)} %index_ref.5) | copy-start | bytes 292
  22.0 4.2 %collective-permute-start.4 = (bf16[32,768]{1,0:T(8,128)(2,1)S(1)}, bf16[32,768]{1,0:T(8,128)(2,1)S(1)}, u32[]{:S(2)}, u32[]{:S(2)}) collective-permute-start(bf16[32,768]{1,0:T(8,128)(2,1)S(1)} %get-tuple-element.33.mine_ref), channel_id=1, source_target_pairs={{0,4},{4,0},{8,12},{12,8},{16,20},{20,16},{24,28},{28,24},{1,5},{5... | collective-permute-start | bytes 147464 | tf_op jit(solution)/shard_map/ppermute | solution.py:434
  26.1 14.2 %copy-start = (bf16[768,384]{1,0:T(8,128)(2,1)S(1)}, bf16[768,384]{1,0:T(8,128)(2,1)}, u32[]{:S(2)}) copy-start(bf16[768,384]{1,0:T(8,128)(2,1)} %rest_8_.1) | copy-start | bytes 1769476
  26.1 14.2 %copy-start.2 = (bf16[64,384]{1,0:T(8,128)(2,1)S(1)}, bf16[64,384]{1,0:T(8,128)(2,1)}, u32[]{:S(2)}) copy-start(bf16[64,384]{1,0:T(8,128)(2,1)} %rest_9_.1) | copy-start | bytes 147460
  27.6 6.0 %collective-permute-start.6 = (bf16[40,896]{1,0:T(8,128)(2,1)S(1)}, bf16[40,896]{1,0:T(8,128)(2,1)S(1)}, u32[]{:S(2)}, u32[]{:S(2)}) collective-permute-start(bf16[40,896]{1,0:T(8,128)(2,1)S(1)} %attend.1.after_ref.rest_0_), channel_id=1, source_target_pairs={{0,8},{4,12},{8,0},{12,4},{16,24},{20,28},{24,16},{28,20},{1,9},{5... | collective-permute-start | bytes 215048 | tf_op jit(solution)/shard_map/ppermute | solution.py:434
  27.6 6.4 %collective-permute-start.8 = (bf16[40,896]{1,0:T(8,128)(2,1)S(1)}, bf16[40,896]{1,0:T(8,128)(2,1)S(1)}, u32[]{:S(2)}, u32[]{:S(2)}) collective-permute-start(bf16[40,896]{1,0:T(8,128)(2,1)S(1)} %attend.1.after_ref.rest_0_), channel_id=1, source_target_pairs={{0,16},{4,20},{8,24},{12,28},{16,0},{20,4},{24,8},{28,12},{1,17},{... | collective-permute-start | bytes 215048 | tf_op jit(solution)/shard_map/ppermute | solution.py:434
  29.8 6.1 %collective-permute-start.10 = (bf16[40,896]{1,0:T(8,128)(2,1)S(1)}, bf16[40,896]{1,0:T(8,128)(2,1)S(1)}, u32[]{:S(2)}, u32[]{:S(2)}) collective-permute-start(bf16[40,896]{1,0:T(8,128)(2,1)S(1)} %attend.1.after_ref.rest_0_), channel_id=1, source_target_pairs={{0,24},{4,28},{8,16},{12,20},{16,8},{20,12},{24,0},{28,4},{1,25},{... | collective-permute-start | bytes 215048 | tf_op jit(solution)/shard_map/ppermute | solution.py:434
  32.0 7.3 %collective-permute-start.5 = (bf16[40,896]{1,0:T(8,128)(2,1)S(1)}, bf16[40,896]{1,0:T(8,128)(2,1)S(1)}, u32[]{:S(2)}, u32[]{:S(2)}) collective-permute-start(bf16[40,896]{1,0:T(8,128)(2,1)S(1)} %attend.1.after_ref.rest_0_), channel_id=1, source_target_pairs={{0,4},{4,0},{8,12},{12,8},{16,20},{20,16},{24,28},{28,24},{1,5},{5... | collective-permute-start | bytes 215048 | tf_op jit(solution)/shard_map/ppermute | solution.py:434
  33.5 5.8 %collective-permute-start.7 = (bf16[40,896]{1,0:T(8,128)(2,1)S(1)}, bf16[40,896]{1,0:T(8,128)(2,1)S(1)}, u32[]{:S(2)}, u32[]{:S(2)}) collective-permute-start(bf16[40,896]{1,0:T(8,128)(2,1)S(1)} %collective-permute-done.6.rest_2_), channel_id=1, source_target_pairs={{0,4},{4,0},{8,12},{12,8},{16,20},{20,16},{24,28},{28,24},{1,5},{5... | collective-permute-start | bytes 215048 | tf_op jit(solution)/shard_map/ppermute | solution.py:434
  34.0 5.3 %collective-permute-start.9 = (bf16[40,896]{1,0:T(8,128)(2,1)S(1)}, bf16[40,896]{1,0:T(8,128)(2,1)S(1)}, u32[]{:S(2)}, u32[]{:S(2)}) collective-permute-start(bf16[40,896]{1,0:T(8,128)(2,1)S(1)} %collective-permute-done.8.rest_4_), channel_id=1, source_target_pairs={{0,4},{4,0},{8,12},{12,8},{16,20},{20,16},{24,28},{28,24},{1,5},{5... | collective-permute-start | bytes 215048 | tf_op jit(solution)/shard_map/ppermute | solution.py:434
  36.0 4.3 %collective-permute-start.11 = (bf16[40,896]{1,0:T(8,128)(2,1)S(1)}, bf16[40,896]{1,0:T(8,128)(2,1)S(1)}, u32[]{:S(2)}, u32[]{:S(2)}) collective-permute-start(bf16[40,896]{1,0:T(8,128)(2,1)S(1)} %collective-permute-done.10.rest_6_), channel_id=1, source_target_pairs={{0,4},{4,0},{8,12},{12,8},{16,20},{20,16},{24,28},{28,24},{1,5},{5... | collective-permute-start | bytes 215048 | tf_op jit(solution)/shard_map/ppermute | solution.py:434
  41.8 4.0 %collective-permute-start.14 = (f32[16,384]{1,0:T(8,128)S(1)}, f32[16,384]{1,0:T(8,128)S(1)}, u32[]{:S(2)}, u32[]{:S(2)}) collective-permute-start(f32[16,384]{1,0:T(8,128)S(1)} %get-tuple-element.42), channel_id=1, source_target_pairs={{0,3},{1,2},{2,1},{3,0},{4,7},{5,6},{6,5},{7,4},{8,11},{9,10},{10,... | collective-permute-start | bytes 73736 | tf_op jit(solution)/shard_map/ppermute | solution.py:561
  41.9 3.9 %collective-permute-start.13 = (f32[16,384]{1,0:T(8,128)S(1)}, f32[16,384]{1,0:T(8,128)S(1)}, u32[]{:S(2)}, u32[]{:S(2)}) collective-permute-start(f32[16,384]{1,0:T(8,128)S(1)} %get-tuple-element.41), channel_id=1, source_target_pairs={{0,2},{1,3},{2,0},{3,1},{4,6},{5,7},{6,4},{7,5},{8,10},{9,11},{10,... | collective-permute-start | bytes 73736 | tf_op jit(solution)/shard_map/ppermute | solution.py:561
  43.5 2.4 %collective-permute-start.12 = (f32[16,384]{1,0:T(8,128)S(1)}, f32[16,384]{1,0:T(8,128)S(1)}, u32[]{:S(2)}, u32[]{:S(2)}) collective-permute-start(f32[16,384]{1,0:T(8,128)S(1)} %get-tuple-element.40.after_ref), channel_id=1, source_target_pairs={{0,1},{1,0},{2,3},{3,2},{4,5},{5,4},{6,7},{7,6},{8,9},{9,8},{10,11... | collective-permute-start | bytes 73736 | tf_op jit(solution)/shard_map/ppermute | solution.py:561

commit v5 on v4

--- a/solution.py
+++ b/solution.py
@@ -385,14 +385,17 @@
     request = lax.broadcasted_iota(jnp.int32, (requests, total_blocks), 0).astype(jnp.float32)
     member = owner == request
     lane_head = lax.broadcasted_iota(jnp.int32, (requests, columns), 1) // HEAD_DIM
-    attended = jnp.zeros((requests, columns), jnp.float32)
+    factors = []
     for h in range(heads):
         top = jnp.where(member, stat[h : h + 1], NEG_FLOOR)
         highest = jnp.max(top, axis=1, keepdims=True)
         factor = jnp.where(member, jnp.exp(top - highest) * stat[heads + h : heads + h + 1], 0.0)
-        factor = factor / jnp.sum(factor, axis=1, keepdims=True)
-        joined = jnp.dot(factor.astype(jnp.bfloat16), parts, preferred_element_type=jnp.float32)
-        attended = jnp.where(lane_head == h, joined, attended)
+        factors.append(factor / jnp.sum(factor, axis=1, keepdims=True))
+    factors = jnp.concatenate(factors, axis=0).astype(jnp.bfloat16)
+    joined = jnp.dot(factors, parts, preferred_element_type=jnp.float32)
+    attended = joined[:requests]
+    for h in range(1, heads):
+        attended = jnp.where(lane_head == h, joined[h * requests : (h + 1) * requests], attended)
     product[...] = jnp.dot(
         attended.astype(jnp.bfloat16), w_ref[...], preferred_element_type=jnp.float32
     )
@@ -497,7 +500,7 @@
         compiler_params=limit,
         name="halve",
     )(at, kept, received, keys)
-    received = [to_peer(sends[m - 1], 2 * m) for m in sorted(range(1, lines), key=lambda m: m)]
+    received = [to_peer(sends[m - 1], 2 * m) for m in sorted(range(1, lines), key=lambda m: (m == 1, m))]
     values, updated = pl.pallas_call(
         stage_values_kernel,
         out_shape=(array(blocks, tokens, columns), array(*cache.shape)),
@@ -548,7 +551,7 @@
         functools.partial(output_kernel, peers),
         out_shape=(
             array(kept_rows, out_columns, dtype=jnp.float32),
-            *(array(kept_rows, out_columns, dtype=jnp.float32) for _ in range(1, ranks)),
+            *(array(kept_rows, out_columns, dtype=jnp.bfloat16) for _ in range(1, ranks)),
         ),
         in_specs=[in_smem] + [in_vmem] * (peers + 2) + [anywhere],
         out_specs=(in_vmem,) * ranks,

time: 46.7 us -> 46 us (0.985)
  transfers between devices with their start and end apart: 15 -> 15, of which waited for: 6 -> 7; matrix products, arithmetic and copies ran while one was open for 3% -> 3% of each run, Pallas kernels for 19% -> 20%
where the time goes in v5:
time: 46 us; the launch traced here: 45.8 us
  starting transfers between devices  20.5 us (45%)
  Pallas kernels  14.9 us (32%)
  waiting for transfers between devices  7.68 us (17%)
  other arithmetic  1.78 us (4%)
  between operations  0.86 us (2%)
    ppermute x12, starting transfers between devices, to_peer(): return lax.ppermute(value, 'seq', [(i, i ^ m) for i in range(peers)])  18.6 us
    ppermute x12, waiting for transfers between devices, to_peer(): return lax.ppermute(value, 'seq', [(i, i ^ m) for i in range(peers)])  7.67 us
    pallas_call x1, Pallas kernels, shards(): pl.pallas_call(project_kernel, out_shape=(array(half, parts * columns + L...  2.7 us
    pallas_call x1, Pallas kernels, shards(): pl.pallas_call(stage_keys_kernel, out_shape=(array(blocks, tokens, column...  2.64 us
    pallas_call x1, Pallas kernels, shards(): pl.pallas_call(functools.partial(patch_kernel, peers), out_shape=array(*c...  1.99 us
    ppermute x3, starting transfers between devices, shards(): moved = lax.ppermute(sends[m - 1], 'tp', [(i, i ^ m) for i in range(ranks)])  1.92 us
    pallas_call x1, Pallas kernels, shards(): pl.pallas_call(stage_values_kernel, out_shape=(array(blocks, tokens, colu...  1.87 us
    pallas_call x1, Pallas kernels, shards(): pl.pallas_call(fetch_kernel, out_shape=array(blocks, 2, ROWS, columns), i...  1.81 us
  transfers between devices with their start and end apart: 15, of which 7 were waited for; matrix products, arithmetic and copies ran while one was open for 3% of the time, Pallas kernels for 20%

profile of v5, /device:TPU:0, one launch (start us, length us, event | category | flops | bytes accessed | tf_op | source)
XLA Modules:
  0.0 45.8 jit_solution(12270695842050088441)
XLA Ops:
  0.6 2.7 %project.1 = (bf16[32,2432]{1,0:T(8,128)(2,1)}, f32[32,2432]{1,0:T(8,128)}) custom-call(s32[1]{0:T(128)} %bitcast.1.place_ref, bf16[64,384]{1,0:T(8,128)(2,1)} %rest_9_.1, bf16[384]{0:T(512)(128)(2,1)} %gain_ref.1, bf16[3,384,768]{2,1,0:T(8,128)(2,1)} %w_ref.1), custom_call_target="tpu_custom_call" | custom-call | tf_op jit(solution)/shard_map/project/pallas_call | solution.py:442
  3.4 3.0 %collective-permute-start = (bf16[32,2432]{1,0:T(8,128)(2,1)}, bf16[32,2432]{1,0:T(8,128)(2,1)S(1)}, u32[]{:S(2)}, u32[]{:S(2)}) collective-permute-start(bf16[32,2432]{1,0:T(8,128)(2,1)} %get-tuple-element.26), channel_id=1, source_target_pairs={{0,4},{4,0},{8,12},{12,8},{16,20},{20,16},{24,28},{28,24},{1,5},{5... | collective-permute-start | bytes 466952 | tf_op jit(solution)/shard_map/ppermute | solution.py:437
  6.4 0.7 %add_convert_fusion.1 = f32[32]{0:T(128)S(1)} fusion(s32[64]{0:T(128)} %length_ref.5, s32[]{:T(128)S(6)} %select_n.21), kind=kLoop, calls=%fused_computation.12 | loop fusion | flops 64 | bytes 260 | tf_op jit(solution)/shard_map/convert_element_type | solution.py:464
  7.1 2.6 %stage_keys.1 = (bf16[24,64,768]{2,1,0:T(8,128)(2,1)S(1)}, bf16[24,2,64,768]{3,2,1,0:T(8,128)(2,1)}) custom-call(bf16[24,2,64,768]{3,2,1,0:T(8,128)(2,1)} %cache_ref.5), custom_call_target="tpu_custom_call" | custom-call | bytes 4718592 | tf_op jit(solution)/shard_map/stage_keys/pallas_call | solution.py:479
  9.8 0.8 %collective-permute-done.recv_ref = bf16[32,2432]{1,0:T(8,128)(2,1)S(1)} collective-permute-done((bf16[32,2432]{1,0:T(8,128)(2,1)}, bf16[32,2432]{1,0:T(8,128)(2,1)S(1)}, u32[]{:S(2)}, u32[]{:S(2)}) %collective-permute-start) | collective-permute-done | bytes 155680 | tf_op jit(solution)/shard_map/ppermute | solution.py:437
  10.6 0.2 halve.1
  10.8 2.9 %collective-permute-start.1 = (bf16[304,128]{1,0:T(8,128)(2,1)S(1)}, bf16[304,128]{1,0:T(8,128)(2,1)S(1)}, u32[]{:S(2)}, u32[]{:S(2)}) collective-permute-start(bf16[304,128]{1,0:T(8,128)(2,1)S(1)} %get-tuple-element.30), channel_id=1, source_target_pairs={{0,16},{4,20},{8,24},{12,28},{16,0},{20,4},{24,8},{28,12},{1,17},{... | collective-permute-start | bytes 233480 | tf_op jit(solution)/shard_map/ppermute | solution.py:437
  13.7 1.3 %collective-permute-start.2 = (bf16[304,128]{1,0:T(8,128)(2,1)S(1)}, bf16[304,128]{1,0:T(8,128)(2,1)S(1)}, u32[]{:S(2)}, u32[]{:S(2)}) collective-permute-start(bf16[304,128]{1,0:T(8,128)(2,1)S(1)} %get-tuple-element.31), channel_id=1, source_target_pairs={{0,24},{4,28},{8,16},{12,20},{16,8},{20,12},{24,0},{28,4},{1,25},{... | collective-permute-start | bytes 233480 | tf_op jit(solution)/shard_map/ppermute | solution.py:437
  15.0 0.2 collective-permute-start.3
  15.3 0.4 multiply_sine_fusion
  15.8 1.9 %stage_values.1 = (bf16[24,64,768]{2,1,0:T(8,128)(2,1)S(1)}, bf16[24,2,64,768]{3,2,1,0:T(8,128)(2,1)}) custom-call(bf16[24,2,64,768]{3,2,1,0:T(8,128)(2,1)S(1)} %bitcast.3, bf16[24,2,64,768]{3,2,1,0:T(8,128)(2,1)} %get-tuple-element.23.held_ref), custom_call_target="tpu_custom_call", output_to_operand_aliasing={{1}: (1, {})} | custom-call | bytes 4718592 | tf_op jit(solution)/shard_map/stage_values/pallas_call | solution.py:504
  17.6 2.5 %collective-permute-done.2.rest_1_ = bf16[304,128]{1,0:T(8,128)(2,1)S(1)} collective-permute-done((bf16[304,128]{1,0:T(8,128)(2,1)S(1)}, bf16[304,128]{1,0:T(8,128)(2,1)S(1)}, u32[]{:S(2)}, u32[]{:S(2)}) %collective-permute-start.2) | collective-permute-done | bytes 77856 | tf_op jit(solution)/shard_map/ppermute | solution.py:437
  20.3 0.4 finish.1
  20.7 1.6 %collective-permute-start.4 = (bf16[32,768]{1,0:T(8,128)(2,1)S(1)}, bf16[32,768]{1,0:T(8,128)(2,1)S(1)}, u32[]{:S(2)}, u32[]{:S(2)}) collective-permute-start(bf16[32,768]{1,0:T(8,128)(2,1)S(1)} %get-tuple-element.33.mine_ref), channel_id=1, source_target_pairs={{0,4},{4,0},{8,12},{12,8},{16,20},{20,16},{24,28},{28,24},{1,5},{5... | collective-permute-start | bytes 147464 | tf_op jit(solution)/shard_map/ppermute | solution.py:437
  22.3 0.7 %plan.1 = (bf16[192,32]{1,0:T(8,128)(2,1)S(1)}, bf16[192,32]{1,0:T(8,128)(2,1)S(1)}, s32[192,128]{1,0:T(8,128)S(1)}, f32[192,128]{1,0:T(8,128)S(1)}) custom-call(s32[1]{0:T(128)} %bitcast.1.place_ref, s32[24]{0:T(128)S(1)} %copy-done.4, s32[24]{0:T(128)S(1)} %copy-done.5, s32[64]{0:T(128)S(1)} %copy-done.3), custom_call_target="tpu_custom_call" | custom-call | tf_op jit(solution)/shard_map/plan/pallas_call | solution.py:467
  23.0 1.9 %collective-permute-done.4.other_ref = bf16[32,768]{1,0:T(8,128)(2,1)S(1)} collective-permute-done((bf16[32,768]{1,0:T(8,128)(2,1)S(1)}, bf16[32,768]{1,0:T(8,128)(2,1)S(1)}, u32[]{:S(2)}, u32[]{:S(2)}) %collective-permute-start.4) | collective-permute-done | bytes 49184 | tf_op jit(solution)/shard_map/ppermute | solution.py:437
  24.9 1.4 %attend.1.after_ref.rest_0_ = bf16[40,896]{1,0:T(8,128)(2,1)S(1)} custom-call(bf16[32,768]{1,0:T(8,128)(2,1)S(1)} %get-tuple-element.33.mine_ref, bf16[32,768]{1,0:T(8,128)(2,1)S(1)} %collective-permute-done.4.other_ref, bf16[192,32]{1,0:T(8,128)(2,1)S(1)} %get-tuple-element.34.pick_mine_ref, bf16[192,32]{1,0:T(8,128)(2,1)S(1)} %get-tuple-element.35.pick_other_ref, ...), custom_call_target="tpu_custom_call" | custom-call | tf_op jit(solution)/shard_map/attend/pallas_call | solution.py:524
  26.3 0.8 %collective-permute-start.6 = (bf16[40,896]{1,0:T(8,128)(2,1)S(1)}, bf16[40,896]{1,0:T(8,128)(2,1)S(1)}, u32[]{:S(2)}, u32[]{:S(2)}) collective-permute-start(bf16[40,896]{1,0:T(8,128)(2,1)S(1)} %attend.1.after_ref.rest_0_), channel_id=1, source_target_pairs={{0,8},{4,12},{8,0},{12,4},{16,24},{20,28},{24,16},{28,20},{1,9},{5... | collective-permute-start | bytes 215048 | tf_op jit(solution)/shard_map/ppermute | solution.py:437
  27.1 2.5 %collective-permute-start.8 = (bf16[40,896]{1,0:T(8,128)(2,1)S(1)}, bf16[40,896]{1,0:T(8,128)(2,1)S(1)}, u32[]{:S(2)}, u32[]{:S(2)}) collective-permute-start(bf16[40,896]{1,0:T(8,128)(2,1)S(1)} %attend.1.after_ref.rest_0_), channel_id=1, source_target_pairs={{0,16},{4,20},{8,24},{12,28},{16,0},{20,4},{24,8},{28,12},{1,17},{... | collective-permute-start | bytes 215048 | tf_op jit(solution)/shard_map/ppermute | solution.py:437
  29.5 1.2 %collective-permute-start.10 = (bf16[40,896]{1,0:T(8,128)(2,1)S(1)}, bf16[40,896]{1,0:T(8,128)(2,1)S(1)}, u32[]{:S(2)}, u32[]{:S(2)}) collective-permute-start(bf16[40,896]{1,0:T(8,128)(2,1)S(1)} %attend.1.after_ref.rest_0_), channel_id=1, source_target_pairs={{0,24},{4,28},{8,16},{12,20},{16,8},{20,12},{24,0},{28,4},{1,25},{... | collective-permute-start | bytes 215048 | tf_op jit(solution)/shard_map/ppermute | solution.py:437
  30.8 1.5 %collective-permute-start.5 = (bf16[40,896]{1,0:T(8,128)(2,1)S(1)}, bf16[40,896]{1,0:T(8,128)(2,1)S(1)}, u32[]{:S(2)}, u32[]{:S(2)}) collective-permute-start(bf16[40,896]{1,0:T(8,128)(2,1)S(1)} %attend.1.after_ref.rest_0_), channel_id=1, source_target_pairs={{0,4},{4,0},{8,12},{12,8},{16,20},{20,16},{24,28},{28,24},{1,5},{5... | collective-permute-start | bytes 215048 | tf_op jit(solution)/shard_map/ppermute | solution.py:437
  32.3 0.5 %collective-permute-start.7 = (bf16[40,896]{1,0:T(8,128)(2,1)S(1)}, bf16[40,896]{1,0:T(8,128)(2,1)S(1)}, u32[]{:S(2)}, u32[]{:S(2)}) collective-permute-start(bf16[40,896]{1,0:T(8,128)(2,1)S(1)} %collective-permute-done.6.rest_2_), channel_id=1, source_target_pairs={{0,4},{4,0},{8,12},{12,8},{16,20},{20,16},{24,28},{28,24},{1,5},{5... | collective-permute-start | bytes 215048 | tf_op jit(solution)/shard_map/ppermute | solution.py:437
  32.8 1.3 %collective-permute-done.8.rest_4_ = bf16[40,896]{1,0:T(8,128)(2,1)S(1)} collective-permute-done((bf16[40,896]{1,0:T(8,128)(2,1)S(1)}, bf16[40,896]{1,0:T(8,128)(2,1)S(1)}, u32[]{:S(2)}, u32[]{:S(2)}) %collective-permute-start.8) | collective-permute-done | bytes 71712 | tf_op jit(solution)/shard_map/ppermute | solution.py:437
  34.1 1.5 %collective-permute-start.9 = (bf16[40,896]{1,0:T(8,128)(2,1)S(1)}, bf16[40,896]{1,0:T(8,128)(2,1)S(1)}, u32[]{:S(2)}, u32[]{:S(2)}) collective-permute-start(bf16[40,896]{1,0:T(8,128)(2,1)S(1)} %collective-permute-done.8.rest_4_), channel_id=1, source_target_pairs={{0,4},{4,0},{8,12},{12,8},{16,20},{20,16},{24,28},{28,24},{1,5},{5... | collective-permute-start | bytes 215048 | tf_op jit(solution)/shard_map/ppermute | solution.py:437
  35.7 1.5 %collective-permute-start.11 = (bf16[40,896]{1,0:T(8,128)(2,1)S(1)}, bf16[40,896]{1,0:T(8,128)(2,1)S(1)}, u32[]{:S(2)}, u32[]{:S(2)}) collective-permute-start(bf16[40,896]{1,0:T(8,128)(2,1)S(1)} %collective-permute-done.10.rest_6_), channel_id=1, source_target_pairs={{0,4},{4,0},{8,12},{12,8},{16,20},{20,16},{24,28},{28,24},{1,5},{5... | collective-permute-start | bytes 215048 | tf_op jit(solution)/shard_map/ppermute | solution.py:437
  37.2 1.8 %fetch.1.rest_10_.rest_8_ = bf16[24,2,16,768]{3,2,1,0:T(8,128)(2,1)S(1)} custom-call(s32[24]{0:T(128)S(1)} %copy-done.4, s32[24]{0:T(128)S(1)} %copy-done.5, s32[64]{0:T(128)S(1)} %copy-done.3, bf16[40,896]{1,0:T(8,128)(2,1)S(1)} %attend.1.after_ref.rest_0_, bf16[24,2,64,768]{3,2,1,0:T(8,128)(2,1)} %cache_ref.5), custom_call_target="tpu_custom_call" | custom-call | bytes 2359296 | tf_op jit(solution)/shard_map/fetch/pallas_call | solution.py:538
  39.0 1.0 %collective-permute-done.11.rest_7_ = bf16[40,896]{1,0:T(8,128)(2,1)S(1)} collective-permute-done((bf16[40,896]{1,0:T(8,128)(2,1)S(1)}, bf16[40,896]{1,0:T(8,128)(2,1)S(1)}, u32[]{:S(2)}, u32[]{:S(2)}) %collective-permute-start.11) | collective-permute-done | bytes 71712 | tf_op jit(solution)/shard_map/ppermute | solution.py:437
  40.0 1.2 %output.1 = (f32[16,384]{1,0:T(8,128)S(1)}, bf16[16,384]{1,0:T(8,128)(2,1)S(1)}, bf16[16,384]{1,0:T(8,128)(2,1)S(1)}, bf16[16,384]{1,0:T(8,128)(2,1)S(1)}) custom-call(s32[1]{0:T(128)} %bitcast.place_ref, bf16[40,896]{1,0:T(8,128)(2,1)S(1)} %attend.1.after_ref.rest_0_, bf16[40,896]{1,0:T(8,128)(2,1)S(1)} %collective-permute-done.5.rest_1_, ...), custom_call_target="tpu_custom_call" | custom-call | tf_op jit(solution)/shard_map/output/pallas_call | solution.py:550
  41.3 1.6 %collective-permute-start.13 = (bf16[16,384]{1,0:T(8,128)(2,1)S(1)}, bf16[16,384]{1,0:T(8,128)(2,1)S(1)}, u32[]{:S(2)}, u32[]{:S(2)}) collective-permute-start(bf16[16,384]{1,0:T(8,128)(2,1)S(1)} %get-tuple-element.41), channel_id=1, source_target_pairs={{0,2},{1,3},{2,0},{3,1},{4,6},{5,7},{6,4},{7,5},{8,10},{9,11},{10,... | collective-permute-start | bytes 36872 | tf_op jit(solution)/shard_map/ppermute | solution.py:564
  42.9 0.3 collective-permute-start.12
  43.2 2.0 %patch.1 = bf16[24,2,64,768]{3,2,1,0:T(8,128)(2,1)} custom-call(s32[1]{0:T(128)} %bitcast.1.place_ref, s32[24]{0:T(128)S(1)} %copy-done.4, s32[24]{0:T(128)S(1)} %copy-done.5, s32[64]{0:T(128)S(1)} %copy-done.3, bf16[16,384]{1,0:T(8,128)(2,1)S(1)} %get-tuple-element.40.after_ref, ...), custom_call_target="tpu_custom_call", output_to_operand_aliasing={{}: (14, {})} | custom-call | bytes 2359296 | tf_op jit(solution)/shard_map/patch/pallas_call | solution.py:566
  45.2 0.6 %add_convert_fusion = bf16[16,384]{1,0:T(8,128)(2,1)} fusion(bf16[16,384]{1,0:T(8,128)(2,1)S(1)} %collective-permute-done.14, bf16[16,384]{1,0:T(8,128)(2,1)S(1)} %collective-permute-done.13, f32[16,384]{1,0:T(8,128)S(1)} %get-tuple-element.39, bf16[16,384]{1,0:T(8,128)(2,1)S(1)} %collective-permute-done.12), kind=kLoop, calls=%fused_computation.2 | loop fusion | flops 43008 | bytes 73728 | tf_op jit(solution)/shard_map/convert_element_type | solution.py:581
  (29 shorter events, 0.4 us)
Async XLA Ops:
  0.6 15.1 %slice-start = ((s8[4718592]{0:T(1024)(128)(4,1)}), s8[524288]{0:T(1024)(128)(4,1)S(1)}, s32[]{:S(2)}) async-start(s8[4718592]{0:T(1024)(128)(4,1)} %bitcast.2), calls=%async_computation | async-start | bytes 1048576
  3.4 7.3 %copy-start.1 = (f32[32,2432]{1,0:T(8,128)S(1)}, f32[32,2432]{1,0:T(8,128)}, u32[]{:S(2)}) copy-start(f32[32,2432]{1,0:T(8,128)} %get-tuple-element.25.kept_ref) | copy-start | bytes 933892
  3.4 7.3 %collective-permute-start = (bf16[32,2432]{1,0:T(8,128)(2,1)}, bf16[32,2432]{1,0:T(8,128)(2,1)S(1)}, u32[]{:S(2)}, u32[]{:S(2)}) collective-permute-start(bf16[32,2432]{1,0:T(8,128)(2,1)} %get-tuple-element.26), channel_id=1, source_target_pairs={{0,4},{4,0},{8,12},{12,8},{16,20},{20,16},{24,28},{28,24},{1,5},{5... | collective-permute-start | bytes 466952 | tf_op jit(solution)/shard_map/ppermute | solution.py:437
  7.1 8.6 %slice-start.1 = ((s8[4718592]{0:T(1024)(128)(4,1)}), s8[4194304]{0:T(1024)(128)(4,1)S(1)}, s32[]{:S(2)}) async-start(s8[4718592]{0:T(1024)(128)(4,1)} %bitcast.2), calls=%async_computation.1 | async-start | bytes 8388608
  10.8 6.8 %collective-permute-start.1 = (bf16[304,128]{1,0:T(8,128)(2,1)S(1)}, bf16[304,128]{1,0:T(8,128)(2,1)S(1)}, u32[]{:S(2)}, u32[]{:S(2)}) collective-permute-start(bf16[304,128]{1,0:T(8,128)(2,1)S(1)} %get-tuple-element.30), channel_id=1, source_target_pairs={{0,16},{4,20},{8,24},{12,28},{16,0},{20,4},{24,8},{28,12},{1,17},{... | collective-permute-start | bytes 233480 | tf_op jit(solution)/shard_map/ppermute | solution.py:437
  13.7 6.4 %collective-permute-start.2 = (bf16[304,128]{1,0:T(8,128)(2,1)S(1)}, bf16[304,128]{1,0:T(8,128)(2,1)S(1)}, u32[]{:S(2)}, u32[]{:S(2)}) collective-permute-start(bf16[304,128]{1,0:T(8,128)(2,1)S(1)} %get-tuple-element.31), channel_id=1, source_target_pairs={{0,24},{4,28},{8,16},{12,20},{16,8},{20,12},{24,0},{28,4},{1,25},{... | collective-permute-start | bytes 233480 | tf_op jit(solution)/shard_map/ppermute | solution.py:437
  15.0 5.2 %collective-permute-start.3 = (bf16[304,128]{1,0:T(8,128)(2,1)S(1)}, bf16[304,128]{1,0:T(8,128)(2,1)S(1)}, u32[]{:S(2)}, u32[]{:S(2)}) collective-permute-start(bf16[304,128]{1,0:T(8,128)(2,1)S(1)} %get-tuple-element.32), channel_id=1, source_target_pairs={{0,8},{4,12},{8,0},{12,4},{16,24},{20,28},{24,16},{28,20},{1,9},{5... | collective-permute-start | bytes 233480 | tf_op jit(solution)/shard_map/ppermute | solution.py:437
  15.7 6.6 %copy-start.3 = (s32[64]{0:T(128)S(1)}, s32[64]{0:T(128)}, u32[]{:S(2)}) copy-start(s32[64]{0:T(128)} %length_ref.5) | copy-start | bytes 772
  15.7 6.5 %copy-start.4 = (s32[24]{0:T(128)S(1)}, s32[24]{0:T(128)}, u32[]{:S(2)}) copy-start(s32[24]{0:T(128)} %owner_ref.5) | copy-start | bytes 292
  15.8 6.5 %copy-start.5 = (s32[24]{0:T(128)S(1)}, s32[24]{0:T(128)}, u32[]{:S(2)}) copy-start(s32[24]{0:T(128)} %index_ref.5) | copy-start | bytes 292
  20.7 4.2 %collective-permute-start.4 = (bf16[32,768]{1,0:T(8,128)(2,1)S(1)}, bf16[32,768]{1,0:T(8,128)(2,1)S(1)}, u32[]{:S(2)}, u32[]{:S(2)}) collective-permute-start(bf16[32,768]{1,0:T(8,128)(2,1)S(1)} %get-tuple-element.33.mine_ref), channel_id=1, source_target_pairs={{0,4},{4,0},{8,12},{12,8},{16,20},{20,16},{24,28},{28,24},{1,5},{5... | collective-permute-start | bytes 147464 | tf_op jit(solution)/shard_map/ppermute | solution.py:437
  24.9 15.2 %copy-start = (bf16[768,384]{1,0:T(8,128)(2,1)S(1)}, bf16[768,384]{1,0:T(8,128)(2,1)}, u32[]{:S(2)}) copy-start(bf16[768,384]{1,0:T(8,128)(2,1)} %rest_8_.1) | copy-start | bytes 1769476
  24.9 15.2 %copy-start.2 = (bf16[64,384]{1,0:T(8,128)(2,1)S(1)}, bf16[64,384]{1,0:T(8,128)(2,1)}, u32[]{:S(2)}) copy-start(bf16[64,384]{1,0:T(8,128)(2,1)} %rest_9_.1) | copy-start | bytes 147460
  26.3 6.0 %collective-permute-start.6 = (bf16[40,896]{1,0:T(8,128)(2,1)S(1)}, bf16[40,896]{1,0:T(8,128)(2,1)S(1)}, u32[]{:S(2)}, u32[]{:S(2)}) collective-permute-start(bf16[40,896]{1,0:T(8,128)(2,1)S(1)} %attend.1.after_ref.rest_0_), channel_id=1, source_target_pairs={{0,8},{4,12},{8,0},{12,4},{16,24},{20,28},{24,16},{28,20},{1,9},{5... | collective-permute-start | bytes 215048 | tf_op jit(solution)/shard_map/ppermute | solution.py:437
  27.1 7.0 %collective-permute-start.8 = (bf16[40,896]{1,0:T(8,128)(2,1)S(1)}, bf16[40,896]{1,0:T(8,128)(2,1)S(1)}, u32[]{:S(2)}, u32[]{:S(2)}) collective-permute-start(bf16[40,896]{1,0:T(8,128)(2,1)S(1)} %attend.1.after_ref.rest_0_), channel_id=1, source_target_pairs={{0,16},{4,20},{8,24},{12,28},{16,0},{20,4},{24,8},{28,12},{1,17},{... | collective-permute-start | bytes 215048 | tf_op jit(solution)/shard_map/ppermute | solution.py:437
  29.5 6.1 %collective-permute-start.10 = (bf16[40,896]{1,0:T(8,128)(2,1)S(1)}, bf16[40,896]{1,0:T(8,128)(2,1)S(1)}, u32[]{:S(2)}, u32[]{:S(2)}) collective-permute-start(bf16[40,896]{1,0:T(8,128)(2,1)S(1)} %attend.1.after_ref.rest_0_), channel_id=1, source_target_pairs={{0,24},{4,28},{8,16},{12,20},{16,8},{20,12},{24,0},{28,4},{1,25},{... | collective-permute-start | bytes 215048 | tf_op jit(solution)/shard_map/ppermute | solution.py:437
  30.8 8.3 %collective-permute-start.5 = (bf16[40,896]{1,0:T(8,128)(2,1)S(1)}, bf16[40,896]{1,0:T(8,128)(2,1)S(1)}, u32[]{:S(2)}, u32[]{:S(2)}) collective-permute-start(bf16[40,896]{1,0:T(8,128)(2,1)S(1)} %attend.1.after_ref.rest_0_), channel_id=1, source_target_pairs={{0,4},{4,0},{8,12},{12,8},{16,20},{20,16},{24,28},{28,24},{1,5},{5... | collective-permute-start | bytes 215048 | tf_op jit(solution)/shard_map/ppermute | solution.py:437
  32.3 6.8 %collective-permute-start.7 = (bf16[40,896]{1,0:T(8,128)(2,1)S(1)}, bf16[40,896]{1,0:T(8,128)(2,1)S(1)}, u32[]{:S(2)}, u32[]{:S(2)}) collective-permute-start(bf16[40,896]{1,0:T(8,128)(2,1)S(1)} %collective-permute-done.6.rest_2_), channel_id=1, source_target_pairs={{0,4},{4,0},{8,12},{12,8},{16,20},{20,16},{24,28},{28,24},{1,5},{5... | collective-permute-start | bytes 215048 | tf_op jit(solution)/shard_map/ppermute | solution.py:437
  34.1 5.0 %collective-permute-start.9 = (bf16[40,896]{1,0:T(8,128)(2,1)S(1)}, bf16[40,896]{1,0:T(8,128)(2,1)S(1)}, u32[]{:S(2)}, u32[]{:S(2)}) collective-permute-start(bf16[40,896]{1,0:T(8,128)(2,1)S(1)} %collective-permute-done.8.rest_4_), channel_id=1, source_target_pairs={{0,4},{4,0},{8,12},{12,8},{16,20},{20,16},{24,28},{28,24},{1,5},{5... | collective-permute-start | bytes 215048 | tf_op jit(solution)/shard_map/ppermute | solution.py:437
  35.7 4.3 %collective-permute-start.11 = (bf16[40,896]{1,0:T(8,128)(2,1)S(1)}, bf16[40,896]{1,0:T(8,128)(2,1)S(1)}, u32[]{:S(2)}, u32[]{:S(2)}) collective-permute-start(bf16[40,896]{1,0:T(8,128)(2,1)S(1)} %collective-permute-done.10.rest_6_), channel_id=1, source_target_pairs={{0,4},{4,0},{8,12},{12,8},{16,20},{20,16},{24,28},{28,24},{1,5},{5... | collective-permute-start | bytes 215048 | tf_op jit(solution)/shard_map/ppermute | solution.py:437
  41.2 3.9 %collective-permute-start.14 = (bf16[16,384]{1,0:T(8,128)(2,1)S(1)}, bf16[16,384]{1,0:T(8,128)(2,1)S(1)}, u32[]{:S(2)}, u32[]{:S(2)}) collective-permute-start(bf16[16,384]{1,0:T(8,128)(2,1)S(1)} %get-tuple-element.42), channel_id=1, source_target_pairs={{0,3},{1,2},{2,1},{3,0},{4,7},{5,6},{6,5},{7,4},{8,11},{9,10},{10,... | collective-permute-start | bytes 36872 | tf_op jit(solution)/shard_map/ppermute | solution.py:564
  41.3 3.9 %collective-permute-start.13 = (bf16[16,384]{1,0:T(8,128)(2,1)S(1)}, bf16[16,384]{1,0:T(8,128)(2,1)S(1)}, u32[]{:S(2)}, u32[]{:S(2)}) collective-permute-start(bf16[16,384]{1,0:T(8,128)(2,1)S(1)} %get-tuple-element.41), channel_id=1, source_target_pairs={{0,2},{1,3},{2,0},{3,1},{4,6},{5,7},{6,4},{7,5},{8,10},{9,11},{10,... | collective-permute-start | bytes 36872 | tf_op jit(solution)/shard_map/ppermute | solution.py:564
  42.9 2.3 %collective-permute-start.12 = (bf16[16,384]{1,0:T(8,128)(2,1)S(1)}, bf16[16,384]{1,0:T(8,128)(2,1)S(1)}, u32[]{:S(2)}, u32[]{:S(2)}) collective-permute-start(bf16[16,384]{1,0:T(8,128)(2,1)S(1)} %get-tuple-element.40.after_ref), channel_id=1, source_target_pairs={{0,1},{1,0},{2,3},{3,2},{4,5},{5,4},{6,7},{7,6},{8,9},{9,8},{10,11... | collective-permute-start | bytes 36872 | tf_op jit(solution)/shard_map/ppermute | solution.py:564

commit v6 on v5

--- a/solution.py
+++ b/solution.py
@@ -18,6 +18,7 @@
 SMEM = pltpu.MemorySpace.SMEM
 HEADS = 8
 ROWS = 16
+JOINS = 2
 
 
 def split3(value):
@@ -37,7 +38,18 @@
 
 
 def project_kernel(
-    place_ref, states_ref, gain_ref, w_ref, sent_ref, kept_ref, states_buf, gain_buf, w_buf, sems
+    place_ref,
+    states_ref,
+    gain_ref,
+    w_ref,
+    sent_ref,
+    kept_ref,
+    sent_fresh_ref,
+    kept_fresh_ref,
+    states_buf,
+    gain_buf,
+    w_buf,
+    sems,
 ):
     parts, _, columns = w_ref.shape
     half = sent_ref.shape[0]
@@ -58,16 +70,17 @@
     wide = jnp.concatenate(rows, axis=0)
     gain = gain_buf[...].astype(jnp.float32)
     scaled = (wide * gain.reshape(1, wide.shape[1])).astype(jnp.bfloat16)
-    squares = jnp.sum(wide * wide, axis=1, keepdims=True)
-    stat = lanes_of(split3(squares))
-    sent_ref[:, parts * columns :] = stat[:half].astype(jnp.bfloat16)
-    kept_ref[:, parts * columns :] = stat[half:]
-    for c in range(parts):
+    stat = lanes_of(split3(jnp.sum(wide * wide, axis=1, keepdims=True)))
+    sent_ref[:, columns:] = stat[:half].astype(jnp.bfloat16)
+    kept_ref[:, columns:] = stat[half:]
+    places = [(sent_ref, kept_ref, 0), (sent_fresh_ref, kept_fresh_ref, 0)]
+    places.append((sent_fresh_ref, kept_fresh_ref, columns))
+    for c, (sent, kept, first) in enumerate(places):
         copies[c].wait()
         term = jnp.dot(scaled, w_buf[c], preferred_element_type=jnp.float32)
-        here = slice(c * columns, (c + 1) * columns)
-        sent_ref[:, here] = term[:half].astype(jnp.bfloat16)
-        kept_ref[:, here] = term[half:]
+        here = slice(first, first + columns)
+        sent[:, here] = term[:half].astype(jnp.bfloat16)
+        kept[:, here] = term[half:]
 
 
 def flat(value):
@@ -75,87 +88,114 @@
     return [value[:, c * LANES : (c + 1) * LANES] for c in range(chunks)]
 
 
-def halve_kernel(place_ref, kept_ref, recv_ref, after_ref, *rest):
-    sends, query_ref, fresh_ref, total = rest[:-3], rest[-3], rest[-2], rest[-1]
+def sum_plan(lines):
+    masks = [1 << k for k in range(lines.bit_length() - 1)]
+    steps = []
+    for k, mask in enumerate(masks):
+        kept = [0]
+        for later in masks[k + 1 :]:
+            kept = kept + [offset ^ later for offset in kept]
+        steps.append((mask, [mask ^ offset for offset in kept], kept))
+    return steps
+
+
+def halve_query_kernel(kept_ref, recv_ref, after_ref, planned_ref, send, query_ref):
     columns = query_ref.shape[1] - LANES
-    share = fresh_ref.shape[0]
     half = kept_ref.shape[0]
-    total[...] = kept_ref[...] + recv_ref[...].astype(jnp.float32)
-    squares = jnp.sum(total[:, 3 * columns :], axis=1, keepdims=True)
+    total = kept_ref[...] + recv_ref[...].astype(jnp.float32)
+    squares = jnp.sum(total[:, columns:], axis=1, keepdims=True)
     query_ref[:, :columns] = total[:, :columns]
     query_ref[:, columns:] = lanes_of([squares])
-    query = jnp.concatenate(flat(total[:, :columns]), axis=0).astype(jnp.bfloat16)
     pads = -half % LANES
     stat = [jnp.pad(term, ((0, pads), (0, 0))) for term in split3(squares)]
     lane = lax.broadcasted_iota(jnp.int32, (half + pads, half + pads), 1)
     row = lax.broadcasted_iota(jnp.int32, (half + pads, half + pads), 0)
     stat = [jnp.sum(jnp.where(lane == row, t, 0.0), axis=0, keepdims=True) for t in stat]
     stat = jnp.concatenate(stat + [jnp.zeros((ROWS - 3, half + pads), jnp.float32)], axis=0)
-    stat = jnp.concatenate(flat(stat), axis=0).astype(jnp.bfloat16)
+    chunks = columns // LANES
+    send[: chunks * half, :] = jnp.concatenate(flat(total[:, :columns]), axis=0).astype(jnp.bfloat16)
+    send[chunks * half :, :] = jnp.concatenate(flat(stat), axis=0).astype(jnp.bfloat16)
+
+
+def halve_fresh_kernel(sent, held, place_ref, kept_ref, recv_ref, send_ref, fresh_ref, total):
+    share = fresh_ref.shape[0] // len(held)
+    total[...] = kept_ref[...] + recv_ref[...].astype(jnp.float32)
     line = place_ref[0] // 2
-    chunks = columns // LANES
-
-    def rows_of(group):
-        return total[pl.ds(pl.multiple_of(group * share, share), share), columns : 3 * columns]
-
-    fresh_ref[...] = rows_of(line)
-    for m, send in enumerate(sends, 1):
-        other = jnp.concatenate(flat(rows_of(line ^ m)), axis=0)
-        send[: chunks * half, :] = query
-        send[chunks * half : chunks * (half + 2 * share), :] = other.astype(jnp.bfloat16)
-        send[chunks * (half + 2 * share) :, :] = stat
-
-
-def finish_kernel(width, place_ref, after_ref, query_ref, fresh_ref, cos_ref, sin_ref, *rest):
-    received, out_ref, news_ref = rest[:-2], rest[-2], rest[-1]
+
+    def rows_of(offsets):
+        rows = [
+            total[pl.ds(pl.multiple_of((line ^ offset) * share, share), share), :]
+            for offset in offsets
+        ]
+        return jnp.concatenate(rows, axis=0)
+
+    fresh_ref[...] = rows_of(held)
+    send_ref[...] = rows_of(sent).astype(jnp.bfloat16)
+
+
+def fold_kernel(offsets, sent, held, fresh_in, recv_ref, send_ref, fresh_ref):
+    share = fresh_ref.shape[0] // len(held)
+    fresh = fresh_in[...] + recv_ref[...].astype(jnp.float32)
+
+    def rows_of(wanted):
+        at = [offsets.index(offset) * share for offset in wanted]
+        return jnp.concatenate([fresh[first : first + share] for first in at], axis=0)
+
+    fresh_ref[...] = rows_of(held)
+    send_ref[...] = rows_of(sent).astype(jnp.bfloat16)
+
+
+def rotated(x, cosine, sine):
+    columns = x.shape[1]
+    span = HEAD_DIM // 2
+    front = lax.broadcasted_iota(jnp.int32, x.shape, 1) % HEAD_DIM < span
+    other = jnp.where(front, -pltpu.roll(x, columns - span, 1), pltpu.roll(x, span, 1))
+    return x * cosine + other * sine
+
+
+def query_kernel(width, after_ref, query_ref, cos_ref, sin_ref, *rest):
+    received, out_ref, scale_ref = rest[:-2], rest[-2], rest[-1]
     half, columns = out_ref.shape
-    share = fresh_ref.shape[0]
     chunks = columns // LANES
     total = flat(query_ref[:, :columns])
     squares = query_ref[:, columns : columns + 1]
-    fresh = flat(fresh_ref[...])
-    pads = -half % LANES
-    stat = jnp.zeros((ROWS * (half + pads) // LANES, LANES), jnp.float32)
+    stat = jnp.zeros((received[0].shape[0] - chunks * half, LANES), jnp.float32)
     for piece in received:
         for c in range(chunks):
             total[c] = total[c] + piece[c * half : (c + 1) * half, :].astype(jnp.float32)
-        extra = piece[chunks * half : chunks * (half + 2 * share), :].astype(jnp.float32)
-        for c in range(2 * chunks):
-            fresh[c] = fresh[c] + extra[c * share : (c + 1) * share]
-        stat = stat + piece[chunks * (half + 2 * share) :, :].astype(jnp.float32)
-    total = jnp.concatenate(total, axis=1)
-    fresh = jnp.concatenate(fresh, axis=1)
+        stat = stat + piece[chunks * half :, :].astype(jnp.float32)
     stat = [jnp.sum(stat[r : r + ROWS], axis=0, keepdims=True) for r in range(0, stat.shape[0], ROWS)]
-    stat = jnp.concatenate(stat, axis=1)[:, :half] if len(stat) * LANES == half else stat[0]
+    stat = jnp.concatenate(stat, axis=1)
     lane = lax.broadcasted_iota(jnp.int32, (half, stat.shape[1]), 1)
     row = lax.broadcasted_iota(jnp.int32, (half, stat.shape[1]), 0)
     squares = squares + jnp.sum(jnp.where(lane == row, stat, 0.0), axis=1, keepdims=True)
     inverse = lax.rsqrt(squares * (1.0 / width) + EPSILON)
-    span = HEAD_DIM // 2
-
-    def rotated(x, cosine, sine):
-        front = lax.broadcasted_iota(jnp.int32, x.shape, 1) % HEAD_DIM < span
-        other = jnp.where(front, -pltpu.roll(x, columns - span, 1), pltpu.roll(x, span, 1))
-        return x * cosine + other * sine
-
-    query = rotated(total[:, :columns] * inverse, cos_ref[...], sin_ref[...])
-    query = (query * HEAD_DIM ** (-0.5)).astype(jnp.bfloat16)
-    out_ref[...] = query
+    query = rotated(jnp.concatenate(total, axis=1) * inverse, cos_ref[...], sin_ref[...])
+    out_ref[...] = (query * HEAD_DIM ** (-0.5)).astype(jnp.bfloat16)
+    scale_ref[...] = jnp.broadcast_to(inverse, scale_ref.shape)
+
+
+def news_kernel(
+    place_ref,
+    query_ref,
+    scale_ref,
+    cos_ref,
+    sin_ref,
+    fresh_ref,
+    recv_ref,
+    part_ref,
+    stat_ref,
+    out_ref,
+    wide,
+):
+    half, columns = query_ref.shape
+    share = fresh_ref.shape[0]
     line = place_ref[0] // 2
-    groups = half // share
-    mine = jnp.zeros((share, columns), jnp.float32)
-    scale = jnp.zeros((share, 1), jnp.float32)
-    cosine, sine = mine, mine
-    wide = query.astype(jnp.float32)
-    for group in range(groups):
-        here = slice(group * share, (group + 1) * share)
-        mine = jnp.where(line == group, wide[here], mine)
-        scale = jnp.where(line == group, inverse[here], scale)
-        cosine = jnp.where(line == group, cos_ref[here, :], cosine)
-        sine = jnp.where(line == group, sin_ref[here, :], sine)
-    key = rotated(fresh[:, :columns] * scale, cosine, sine).astype(jnp.bfloat16)
-    value = (fresh[:, columns:] * scale).astype(jnp.bfloat16)
-    product = mine * key.astype(jnp.float32)
+    here = pl.ds(pl.multiple_of(line * share, share), share)
+    wide[...] = query_ref[...].astype(jnp.float32)
+    fresh = (fresh_ref[...] + recv_ref[...].astype(jnp.float32)) * scale_ref[here, 0:1]
+    key = rotated(fresh[:, :columns], cos_ref[here, :], sin_ref[here, :])
+    product = wide[here, :] * key.astype(jnp.bfloat16).astype(jnp.float32)
     lane_head = lax.broadcasted_iota(jnp.int32, product.shape, 1) // HEAD_DIM
     lane = lax.broadcasted_iota(jnp.int32, (share, LANES), 1)
     first = (place_ref[0] % 2) * half + line * share
@@ -166,10 +206,14 @@
         for j, term in enumerate(split3(score)):
             stat = jnp.where(lane == j * HEADS + h, term, stat)
         stat = jnp.where(lane == 3 * HEADS + h, 1.0, stat)
-    none = jnp.where(lane == 6 * HEADS, -1.0, 0.0)
-    both = jnp.concatenate([value.astype(jnp.float32), key.astype(jnp.float32)], axis=0)
-    news_ref[:, :columns] = both.astype(jnp.bfloat16)
-    news_ref[:, columns:] = jnp.concatenate([stat, none], axis=0).astype(jnp.bfloat16)
+    part = part_ref[...]
+    part = jnp.concatenate([fresh[:, columns:], part[share:]], axis=0)
+    stat = jnp.concatenate([stat_ref[:share, :] + stat, stat_ref[share:, :]], axis=0)
+    first = 0
+    for value in (part[:ROWS], part[ROWS:], key, stat):
+        value = jnp.concatenate(flat(value), axis=0).astype(jnp.bfloat16)
+        out_ref[first : first + value.shape[0], :] = value
+        first += value.shape[0]
 
 
 def stage(part, cache_ref, near_ref, updated_ref, loads, stores):
@@ -195,8 +239,17 @@
     stage(0, cache_ref, keys_ref, updated_ref, loads, stores)
 
 
-def stage_values_kernel(cache_ref, held_ref, values_ref, updated_ref, loads, stores):
-    stage(1, cache_ref, values_ref, updated_ref, loads, stores)
+def stage_values_kernel(cache_ref, values_ref, loads):
+    copies = [
+        pltpu.make_async_copy(
+            cache_ref.at[pl.ds(first, GROUP), 1], values_ref.at[pl.ds(first, GROUP)], loads.at[i]
+        )
+        for i, first in enumerate(range(0, cache_ref.shape[0], GROUP))
+    ]
+    for copy in copies:
+        copy.start()
+    for copy in copies:
+        copy.wait()
 
 
 def read_block(b, owner_ref, index_ref, length_ref, tokens):
@@ -243,15 +296,13 @@
     pick_other_ref,
     seen_ref,
     name_ref,
-    news_ref,
     keys_ref,
     values_ref,
-    out_ref,
+    part_ref,
+    stat_ref,
 ):
     blocks, tokens, columns = keys_ref.shape
-    extra = news_ref.shape[0]
     steps = blocks // GROUP
-    out_ref[:extra, :] = news_ref[...]
 
     def iota(shape, dim):
         return lax.broadcasted_iota(jnp.int32, shape, dim)
@@ -295,42 +346,103 @@
         )
     part = jnp.concatenate(parts, axis=0) * jnp.where(mass > 0.0, 1.0 / mass, 0.0)
     part = jnp.where(head_mask, part, 0.0).astype(jnp.bfloat16)
+    fresh = part_ref.shape[0] - blocks
     lane = iota((rows, LANES), 1)
     head = iota((rows, LANES), 0) % HEADS
+    spot = iota((rows, LANES), 0) // HEADS + fresh
+    lane = lane - spot // ROWS * (LANES // 2)
     stat = jnp.where((lane == 6 * HEADS) & (head == 0), name_ref[...], 0.0)
     for j, term in enumerate(split3(top) + split3(mass)):
         stat = jnp.where(lane == head + j * HEADS, term, stat)
-    padded = blocks + -blocks % 16
-    fold = iota((padded, rows), 1) // HEADS == iota((padded, rows), 0)
-    fold = fold.astype(jnp.float32).astype(jnp.bfloat16)
-    part = jnp.dot(fold, part, preferred_element_type=jnp.float32)
-    stat = jnp.dot(fold, stat.astype(jnp.bfloat16), preferred_element_type=jnp.float32)
-    out_ref[extra:, :columns] = part[:blocks].astype(jnp.bfloat16)
-    out_ref[extra:, columns:] = stat[:blocks].astype(jnp.bfloat16)
-
-
-def each_slot(tokens, owner_ref, index_ref, length_ref, do):
+    spot = iota((2 * ROWS, rows), 1) // HEADS + fresh
+    fold = (spot == iota((2 * ROWS, rows), 0)).astype(jnp.float32).astype(jnp.bfloat16)
+    part_ref[...] = jnp.dot(fold, part, preferred_element_type=jnp.float32)
+    spot = iota((ROWS, rows), 1) // HEADS + fresh
+    fold = (spot % ROWS == iota((ROWS, rows), 0)).astype(jnp.float32).astype(jnp.bfloat16)
+    stat_ref[...] = jnp.dot(fold, stat.astype(jnp.bfloat16), preferred_element_type=jnp.float32)
+
+
+def slots(tokens, owner_ref, index_ref, length_ref):
+    found = []
     for b in range(owner_ref.shape[0]):
         owner, _, slot = read_block(b, owner_ref, index_ref, length_ref, tokens)
         first = pl.multiple_of(jnp.maximum(slot, 0) // ROWS * ROWS, ROWS)
-        pl.when(slot >= 0)(functools.partial(do, b, owner, slot, first))
-
-
-def fetch_kernel(owner_ref, index_ref, length_ref, after_ref, cache_ref, near_ref, loads):
-    tokens = cache_ref.shape[2]
+        found.append((b, owner, slot, first))
+    return found
+
+
+def each(found, do):
+    for spot in found:
+        pl.when(spot[2] >= 0)(functools.partial(do, *spot))
+
+
+def fetch_kernel(
+    owner_ref,
+    index_ref,
+    length_ref,
+    after_ref,
+    cache_ref,
+    held_ref,
+    updated_ref,
+    near_ref,
+    values,
+    loads,
+    stores,
+    fetches,
+):
+    found = slots(cache_ref.shape[2], owner_ref, index_ref, length_ref)
 
     def fetch(b, owner, slot, first):
         return pltpu.make_async_copy(
-            cache_ref.at[b, :, pl.ds(first, ROWS), :], near_ref.at[b], loads.at[b]
+            cache_ref.at[b, :, pl.ds(first, ROWS), :], near_ref.at[b], fetches.at[b]
         )
 
-    each_slot(tokens, owner_ref, index_ref, length_ref, lambda *at: fetch(*at).start())
-    each_slot(tokens, owner_ref, index_ref, length_ref, lambda *at: fetch(*at).wait())
+    spans = [pl.ds(first, GROUP) for first in range(0, cache_ref.shape[0], GROUP)]
+    load = [
+        pltpu.make_async_copy(cache_ref.at[span, 1], values.at[span], loads.at[i])
+        for i, span in enumerate(spans)
+    ]
+    store = [
+        pltpu.make_async_copy(values.at[span], updated_ref.at[span, 1], stores.at[i])
+        for i, span in enumerate(spans)
+    ]
+    for copy in load:
+        copy.start()
+    each(found, lambda *at: fetch(*at).start())
+    for arriving, leaving in zip(load, store):
+        arriving.wait()
+        leaving.start()
+    each(found, lambda *at: fetch(*at).wait())
+    for copy in store:
+        copy.wait()
+
+
+def join_kernel(*refs):
+    out_ref = refs[-1]
+    rows = refs[0].shape[0]
+    for i, ref in enumerate(refs[:-1]):
+        out_ref[i * rows : (i + 1) * rows, :] = ref[...]
+
+
+def line_order(lines):
+    return [0, *range(lines - 1, 0, -1)]
+
+
+def pieces_of(column, crossed):
+    rows = column[0].shape[0]
+    each = len(column) // len(crossed)
+    pieces = [None] * (2 * len(column))
+    for i, m in enumerate(line_order(len(column))):
+        first = i % each * rows
+        pieces[2 * m] = column[i]
+        pieces[2 * m + 1] = crossed[i // each].at[first : first + rows]
+    return pieces
 
 
 def patch_kernel(count, place_ref, owner_ref, index_ref, length_ref, after_ref, *rest):
-    pieces, near_ref, held_ref, updated_ref = rest[:count], rest[count], rest[count + 1], rest[count + 2]
-    fresh, patch, stores = rest[count + 3 :]
+    lines = count // 2
+    pieces = pieces_of(rest[:lines], rest[lines : lines + JOINS])
+    near_ref, held_ref, updated_ref, fresh, patch, stores = rest[lines + JOINS :]
     _, _, tokens, columns = updated_ref.shape
     requests = length_ref.shape[0]
     share = fresh.shape[1] // 2
@@ -342,7 +454,11 @@
         )
 
     for m in range(count):
-        fresh[m] = pieces[m][: 2 * share, :columns].astype(jnp.float32)
+        for c in range(columns // LANES):
+            here = slice(c * LANES, (c + 1) * LANES)
+            keys = 2 * columns // LANES * ROWS + c * share
+            fresh[m, :share, here] = pieces[m][c * ROWS : c * ROWS + share, :].astype(jnp.float32)
+            fresh[m, share:, here] = pieces[m][keys : keys + share, :].astype(jnp.float32)
     row = lax.broadcasted_iota(jnp.int32, (ROWS, columns), 0)
 
     def change(b, owner, slot, first):
@@ -356,31 +472,47 @@
             patch[b, c] = jnp.where(row == slot - first, new, old).astype(jnp.bfloat16)
         store(b, owner, slot, first).start()
 
-    each_slot(tokens, owner_ref, index_ref, length_ref, change)
-    each_slot(tokens, owner_ref, index_ref, length_ref, lambda *at: store(*at).wait())
+    found = slots(tokens, owner_ref, index_ref, length_ref)
+    each(found, change)
+    each(found, lambda *at: store(*at).wait())
 
 
 def output_kernel(count, place_ref, *rest):
-    pieces, w_ref, states_ref, own_ref = rest[:count], rest[count], rest[count + 1], rest[count + 3]
-    sends, product = rest[count + 4 : -1], rest[-1]
+    lines = count // 2
+    pieces = pieces_of(rest[:lines], rest[lines : lines + JOINS])
+    w_ref, states_ref, after_ref, own_ref, *sends, product = rest[lines + JOINS :]
     heads = HEADS
-    blocks, wide = pieces[0].shape
-    columns = wide - LANES
+    columns = w_ref.shape[0]
+    chunks = columns // LANES
     requests = states_ref.shape[0]
-    total_blocks = count * blocks
-    both = [piece[...].astype(jnp.float32) for piece in pieces]
-    both = jnp.concatenate(both, axis=0).astype(jnp.bfloat16)
-    parts, stat = both[:, :columns], both[:, columns:]
+    total_blocks = count * 2 * ROWS
+
+    def rows_of(first):
+        rows = [
+            jnp.concatenate(
+                [piece[first + c * ROWS : first + (c + 1) * ROWS, :] for c in range(chunks)], axis=1
+            )
+            for piece in pieces
+        ]
+        return jnp.concatenate(rows, axis=0)
+
+    parts = jnp.concatenate([rows_of(0), rows_of(chunks * ROWS)], axis=0)
+    stat = jnp.concatenate([piece[-ROWS:, :] for piece in pieces], axis=0)
     row = lax.broadcasted_iota(jnp.int32, (3 * heads, LANES), 0)
     lane = lax.broadcasted_iota(jnp.int32, (3 * heads, LANES), 1)
-    wanted = (row // heads == lane // (3 * heads)) & (row % heads == lane % heads)
-    wanted = (wanted & (row < 2 * heads)) | ((row >= 2 * heads) & (lane == 6 * heads))
-    stat = lax.dot_general(
-        wanted.astype(jnp.float32).astype(jnp.bfloat16),
-        stat,
-        (((1,), (1,)), ((), ())),
-        preferred_element_type=jnp.float32,
-    )
+
+    def terms(first):
+        at = lane - first
+        wanted = (row // heads == at // (3 * heads)) & (row % heads == at % heads) & (at >= 0)
+        wanted = (wanted & (row < 2 * heads)) | ((row >= 2 * heads) & (at == 6 * heads))
+        return lax.dot_general(
+            wanted.astype(jnp.float32).astype(jnp.bfloat16),
+            stat,
+            (((1,), (1,)), ((), ())),
+            preferred_element_type=jnp.float32,
+        )
+
+    stat = jnp.concatenate([terms(0), terms(LANES // 2)], axis=1)
     owner = stat[2 * heads : 2 * heads + 1]
     request = lax.broadcasted_iota(jnp.int32, (requests, total_blocks), 0).astype(jnp.float32)
     member = owner == request
@@ -439,14 +571,16 @@
     def moves(size):
         return pl.CostEstimate(flops=0, bytes_accessed=size, transcendentals=0)
 
-    sent, kept = pl.pallas_call(
+    sent, kept, sent_fresh, kept_fresh = pl.pallas_call(
         project_kernel,
         out_shape=(
-            array(half, parts * columns + LANES),
-            array(half, parts * columns + LANES, dtype=jnp.float32),
+            array(half, columns + LANES),
+            array(half, columns + LANES, dtype=jnp.float32),
+            array(half, 2 * columns),
+            array(half, 2 * columns, dtype=jnp.float32),
         ),
         in_specs=[in_smem] + [in_hbm] * 3,
-        out_specs=(in_vmem, in_vmem),
+        out_specs=(in_vmem,) * 4,
         scratch_shapes=[
             pltpu.VMEM(states.shape, jnp.bfloat16),
             pltpu.VMEM(norm_gain.shape, jnp.bfloat16),
@@ -457,6 +591,7 @@
         name="project",
     )(at, states, norm_gain, w_qkv)
     received = to_peer(sent, 1)
+    fresh_received = to_peer(sent_fresh, 1)
 
     positions = lax.dynamic_slice_in_dim(context_len, place % 2 * half, half) - 1
     pair = (jnp.arange(columns, dtype=jnp.int32) % (HEAD_DIM // 2)).astype(jnp.float32)
@@ -487,64 +622,105 @@
         name="stage_keys",
     )(cache)
 
-    message = columns // LANES * (half + 2 * share) + ROWS * pl.cdiv(half, LANES)
-    *sends, query, fresh = pl.pallas_call(
-        halve_kernel,
+    values = pl.pallas_call(
+        stage_values_kernel,
+        out_shape=array(blocks, tokens, columns),
+        in_specs=[in_hbm],
+        out_specs=in_vmem,
+        scratch_shapes=[pltpu.SemaphoreType.DMA((steps,))],
+        compiler_params=most_room,
+        cost_estimate=moves(cache.size),
+        name="stage_values",
+    )(cache)
+    message = columns // LANES * half + ROWS * pl.cdiv(half, LANES)
+    send, query = pl.pallas_call(
+        halve_query_kernel,
+        out_shape=(array(message, LANES), array(half, columns + LANES, dtype=jnp.float32)),
+        in_specs=[in_vmem, in_vmem, anywhere, anywhere],
+        compiler_params=pltpu.CompilerParams(vmem_limit_bytes=47 * 1024 * 1024),
+        name="halve_query",
+    )(kept, received, values, plan[0])
+    received = [to_peer(send, 2 * m) for m in line_order(lines)[1:]]
+    (mask, sent_to, held), *later = sum_plan(lines)
+    fresh_send, fresh = pl.pallas_call(
+        functools.partial(halve_fresh_kernel, sent_to, held),
         out_shape=(
-            *(array(message, LANES) for _ in range(1, lines)),
-            array(half, columns + LANES, dtype=jnp.float32),
-            array(share, 2 * columns, dtype=jnp.float32),
+            array(share * len(sent_to), 2 * columns),
+            array(share * len(held), 2 * columns, dtype=jnp.float32),
         ),
-        in_specs=[in_smem, in_vmem, in_vmem, anywhere],
-        scratch_shapes=[pltpu.VMEM((half, parts * columns + LANES), jnp.float32)],
+        in_specs=[in_smem, in_vmem, in_vmem],
+        scratch_shapes=[pltpu.VMEM((half, 2 * columns), jnp.float32)],
         compiler_params=limit,
-        name="halve",
-    )(at, kept, received, keys)
-    received = [to_peer(sends[m - 1], 2 * m) for m in sorted(range(1, lines), key=lambda m: (m == 1, m))]
-    values, updated = pl.pallas_call(
-        stage_values_kernel,
-        out_shape=(array(blocks, tokens, columns), array(*cache.shape)),
-        in_specs=[in_hbm, in_hbm],
-        out_specs=(in_vmem, in_hbm),
-        scratch_shapes=[pltpu.SemaphoreType.DMA((steps,))] * 2,
-        input_output_aliases={1: 1},
+        name="halve_fresh",
+    )(at, kept_fresh, fresh_received)
+    fresh_received = to_peer(fresh_send, 2 * mask)
+    for mask, sent_to, still in later:
+        fresh_send, fresh = pl.pallas_call(
+            functools.partial(fold_kernel, held, sent_to, still),
+            out_shape=(
+                array(share * len(sent_to), 2 * columns),
+                array(share * len(still), 2 * columns, dtype=jnp.float32),
+            ),
+            compiler_params=limit,
+            name="fold",
+        )(fresh, fresh_received)
+        held = still
+        fresh_received = to_peer(fresh_send, 2 * mask)
+    cosine, sine = jnp.cos(angles), jnp.sin(angles)
+    mine, scale = pl.pallas_call(
+        functools.partial(query_kernel, depth * peers),
+        out_shape=(array(half, columns), array(half, LANES, dtype=jnp.float32)),
+        in_specs=[anywhere] + [in_vmem] * (3 + len(received)),
         compiler_params=pltpu.CompilerParams(vmem_limit_bytes=47 * 1024 * 1024),
-        cost_estimate=moves(cache.size * 2),
-        name="stage_values",
-    )(cache, updated)
-    mine, news = pl.pallas_call(
-        functools.partial(finish_kernel, depth * peers),
-        out_shape=(array(half, columns), array(2 * share, columns + LANES)),
-        in_specs=[in_smem, anywhere] + [in_vmem] * (4 + len(received)),
-        compiler_params=pltpu.CompilerParams(vmem_limit_bytes=47 * 1024 * 1024),
-        name="finish",
-    )(at, values, query, fresh, jnp.cos(angles), jnp.sin(angles), *received)
+        name="query",
+    )(keys, query, cosine, sine, *received)
     other = to_peer(mine, 1)
 
-    piece = pl.pallas_call(
+    part, stat = pl.pallas_call(
         attend_kernel,
-        out_shape=array(2 * share + blocks, columns + LANES),
-        in_specs=[in_vmem] * 9,
+        out_shape=(
+            array(2 * ROWS, columns, dtype=jnp.float32),
+            array(ROWS, LANES, dtype=jnp.float32),
+        ),
+        in_specs=[in_vmem] * 8,
         compiler_params=pltpu.CompilerParams(vmem_limit_bytes=47 * 1024 * 1024),
         name="attend",
-    )(mine, other, *plan, news, keys, values)
-    pieces = [piece] * peers
-    far = sorted(range(1, lines), key=lambda m: m)
-    for m in far:
-        pieces[2 * m] = to_peer(piece, 2 * m)
-    for m in (*far, 0):
-        pieces[2 * m + 1] = to_peer(pieces[2 * m], 1)
-
-    near = pl.pallas_call(
+    )(mine, other, *plan, keys, values)
+    piece = pl.pallas_call(
+        news_kernel,
+        out_shape=array(columns // LANES * (2 * ROWS + share) + ROWS, LANES),
+        in_specs=[in_smem] + [in_vmem] * 8,
+        scratch_shapes=[pltpu.VMEM((half, columns), jnp.float32)],
+        compiler_params=limit,
+        name="news",
+    )(at, mine, scale, cosine, sine, fresh, fresh_received, part, stat)
+    column = [to_peer(piece, 2 * m) if m else piece for m in line_order(lines)]
+    each = lines // JOINS
+    pieces = list(column)
+    for first in range(0, lines, each):
+        joined = pl.pallas_call(
+            join_kernel,
+            out_shape=array(each * piece.shape[0], LANES),
+            compiler_params=limit,
+            name="join",
+        )(*column[first : first + each])
+        pieces.append(to_peer(joined, 1))
+    updated, near = pl.pallas_call(
         fetch_kernel,
-        out_shape=array(blocks, 2, ROWS, columns),
-        in_specs=[in_smem] * 3 + [anywhere, in_hbm],
-        out_specs=in_vmem,
-        scratch_shapes=[pltpu.SemaphoreType.DMA((blocks,))],
+        out_shape=(array(*cache.shape), array(blocks, 2, ROWS, columns)),
+        in_specs=[in_smem] * 3 + [anywhere, in_hbm, in_hbm],
+        out_specs=(in_hbm, in_vmem),
+        scratch_shapes=[
+            pltpu.VMEM((blocks, tokens, columns), jnp.bfloat16),
+            pltpu.SemaphoreType.DMA((steps,)),
+            pltpu.SemaphoreType.DMA((steps,)),
+            pltpu.SemaphoreType.DMA((blocks,)),
+        ],
+        input_output_aliases={5: 0},
         compiler_params=most_room,
-        cost_estimate=moves(blocks * ROWS * columns * 8),
+        cost_estimate=moves(cache.size * 2),
         name="fetch",
-    )(*table, piece, cache)
+    )(*table, piece, cache, updated)
     rank = lax.axis_index("tp")
     kept_rows = requests // ranks
     own, *sends = pl.pallas_call(
@@ -553,7 +729,7 @@
             array(kept_rows, out_columns, dtype=jnp.float32),
             *(array(kept_rows, out_columns, dtype=jnp.bfloat16) for _ in range(1, ranks)),
         ),
-        in_specs=[in_smem] + [in_vmem] * (peers + 2) + [anywhere],
+        in_specs=[in_smem] + [in_vmem] * (len(pieces) + 2) + [anywhere],
         out_specs=(in_vmem,) * ranks,
         scratch_shapes=[pltpu.VMEM((requests, out_columns), jnp.float32)],
         compiler_params=limit,
@@ -566,14 +742,14 @@
     updated = pl.pallas_call(
         functools.partial(patch_kernel, peers),
         out_shape=array(*cache.shape),
-        in_specs=[in_smem] * 4 + [anywhere] + [in_vmem] * (peers + 1) + [in_hbm],
+        in_specs=[in_smem] * 4 + [anywhere] + [in_vmem] * (len(pieces) + 1) + [in_hbm],
         out_specs=in_hbm,
         scratch_shapes=[
             pltpu.VMEM((peers, 2 * share, columns), jnp.float32),
             pltpu.VMEM((blocks, 2, ROWS, columns), jnp.bfloat16),
             pltpu.SemaphoreType.DMA((blocks,)),
         ],
-        input_output_aliases={6 + peers: 0},
+        input_output_aliases={6 + len(pieces): 0},
         compiler_params=most_room,
         cost_estimate=moves(blocks * ROWS * columns * 8),
         name="patch",

time: 46 us -> 44.6 us (0.970)
  waiting for transfers between devices: 7.68 us -> 4.2 us
  starting transfers between devices: 20.5 us -> 22 us
  Pallas kernels: 14.9 us -> 16.1 us
  other arithmetic: 1.78 us -> 1.13 us
    ppermute x12 -> x13, waiting for transfers between devices: 7.67 us -> 4.19 us  [to_peer(): return lax.ppermute(value, 'seq', [(i, i ^ m) for i in range(peers)])]
    pallas_call x6 -> x11, Pallas kernels: 8.41 us -> 10 us  [the longest x1 3.48 us: shards(): pl.pallas_call(fetch_kernel, out_shape=(array(*cache.shape), array(blocks...]
    ppermute x12 -> x13, starting transfers between devices: 18.6 us -> 20.1 us  [to_peer(): return lax.ppermute(value, 'seq', [(i, i ^ m) for i in range(peers)])]
    convert_element_type x1, other arithmetic: 0.73 us -> 0.08 us  [shards(): angles = positions.astype(jnp.float32)[:, None] * frequency[None, :]]
  transfers between devices with their start and end apart: 15 -> 16, of which waited for: 7 -> 6; matrix products, arithmetic and copies ran while one was open for 3% -> 1% of each run, Pallas kernels for 20% -> 28%
where the time goes in v6:
time: 44.6 us; the launch traced here: 44.4 us
  starting transfers between devices  22 us (49%)
  Pallas kernels  16.1 us (36%)
  waiting for transfers between devices  4.2 us (9%)
  other arithmetic  1.13 us (3%)
  between operations  0.87 us (2%)
    ppermute x13, starting transfers between devices, to_peer(): return lax.ppermute(value, 'seq', [(i, i ^ m) for i in range(peers)])  20.1 us
    ppermute x13, waiting for transfers between devices, to_peer(): return lax.ppermute(value, 'seq', [(i, i ^ m) for i in range(peers)])  4.19 us
    pallas_call x1, Pallas kernels, shards(): pl.pallas_call(fetch_kernel, out_shape=(array(*cache.shape), array(blocks...  3.48 us
    pallas_call x1, Pallas kernels, shards(): pl.pallas_call(project_kernel, out_shape=(array(half, columns + LANES), a...  2.59 us
    pallas_call x1, Pallas kernels, shards(): pl.pallas_call(stage_keys_kernel, out_shape=(array(blocks, tokens, column...  2.49 us
    pallas_call x1, Pallas kernels, shards(): pl.pallas_call(functools.partial(patch_kernel, peers), out_shape=array(*c...  1.97 us
    ppermute x3, starting transfers between devices, shards(): moved = lax.ppermute(sends[m - 1], 'tp', [(i, i ^ m) for i in range(ranks)])  1.92 us
    pallas_call x1, Pallas kernels, shards(): pl.pallas_call(stage_values_kernel, out_shape=array(blocks, tokens, colum...  1.68 us
  transfers between devices with their start and end apart: 16, of which 6 were waited for; matrix products, arithmetic and copies ran while one was open for 1% of the time, Pallas kernels for 28%

profile of v6, /device:TPU:0, one launch (start us, length us, event | category | flops | bytes accessed | tf_op | source)
XLA Modules:
  0.0 44.4 jit_solution(3944735574187912132)
XLA Ops:
  0.7 2.6 %project.1 = (bf16[32,896]{1,0:T(8,128)(2,1)}, f32[32,896]{1,0:T(8,128)}, bf16[32,1536]{1,0:T(8,128)(2,1)}, f32[32,1536]{1,0:T(8,128)}) custom-call(s32[1]{0:T(128)} %bitcast.1.place_ref, bf16[64,384]{1,0:T(8,128)(2,1)} %rest_7_.1, bf16[384]{0:T(512)(128)(2,1)} %gain_ref.1, bf16[3,384,768]{2,1,0:T(8,128)(2,1)} %w_ref.1), custom_call_target="tpu_custom_call" | custom-call | tf_op jit(solution)/shard_map/project/pallas_call | solution.py:574
  3.3 3.0 %collective-permute-start = (bf16[32,896]{1,0:T(8,128)(2,1)}, bf16[32,896]{1,0:T(8,128)(2,1)S(1)}, u32[]{:S(2)}, u32[]{:S(2)}) collective-permute-start(bf16[32,896]{1,0:T(8,128)(2,1)} %get-tuple-element.30), channel_id=1, source_target_pairs={{0,4},{4,0},{8,12},{12,8},{16,20},{20,16},{24,28},{28,24},{1,5},{5... | collective-permute-start | bytes 172040 | tf_op jit(solution)/shard_map/ppermute | solution.py:569
  6.4 1.7 %stage_values.1.after_ref.values_ref = bf16[24,64,768]{2,1,0:T(8,128)(2,1)S(1)} custom-call(bf16[24,2,64,768]{3,2,1,0:T(8,128)(2,1)} %cache_ref.5), custom_call_target="tpu_custom_call" | custom-call | bytes 2359296 | tf_op jit(solution)/shard_map/stage_values/pallas_call | solution.py:625
  8.1 0.7 %plan.1 = (bf16[192,32]{1,0:T(8,128)(2,1)S(1)}, bf16[192,32]{1,0:T(8,128)(2,1)S(1)}, s32[192,128]{1,0:T(8,128)S(1)}, f32[192,128]{1,0:T(8,128)S(1)}) custom-call(s32[1]{0:T(128)} %bitcast.1.place_ref, s32[24]{0:T(128)S(1)} %copy-done.4, s32[24]{0:T(128)S(1)} %copy-done.5, s32[64]{0:T(128)S(1)} %copy-done.6), custom_call_target="tpu_custom_call" | custom-call | tf_op jit(solution)/shard_map/plan/pallas_call | solution.py:602
  8.9 0.2 halve_query.1
  9.1 4.4 %collective-permute-start.1 = (bf16[208,128]{1,0:T(8,128)(2,1)S(1)}, bf16[208,128]{1,0:T(8,128)(2,1)S(1)}, u32[]{:S(2)}, u32[]{:S(2)}) collective-permute-start(bf16[208,128]{1,0:T(8,128)(2,1)S(1)} %get-tuple-element.33), channel_id=1, source_target_pairs={{0,24},{4,28},{8,16},{12,20},{16,8},{20,12},{24,0},{28,4},{1,25},{... | collective-permute-start | bytes 159752 | tf_op jit(solution)/shard_map/ppermute | solution.py:569
  13.5 0.6 %collective-permute-start.3 = (bf16[208,128]{1,0:T(8,128)(2,1)S(1)}, bf16[208,128]{1,0:T(8,128)(2,1)S(1)}, u32[]{:S(2)}, u32[]{:S(2)}) collective-permute-start(bf16[208,128]{1,0:T(8,128)(2,1)S(1)} %get-tuple-element.33), channel_id=1, source_target_pairs={{0,8},{4,12},{8,0},{12,4},{16,24},{20,28},{24,16},{28,20},{1,9},{5... | collective-permute-start | bytes 159752 | tf_op jit(solution)/shard_map/ppermute | solution.py:569
  14.2 1.5 %collective-permute-start.5 = (bf16[16,1536]{1,0:T(8,128)(2,1)S(1)}, bf16[16,1536]{1,0:T(8,128)(2,1)S(1)}, u32[]{:S(2)}, u32[]{:S(2)}) collective-permute-start(bf16[16,1536]{1,0:T(8,128)(2,1)S(1)} %get-tuple-element.39), channel_id=1, source_target_pairs={{0,8},{4,12},{8,0},{12,4},{16,24},{20,28},{24,16},{28,20},{1,9},{5... | collective-permute-start | bytes 147464 | tf_op jit(solution)/shard_map/ppermute | solution.py:569
  15.7 0.4 multiply_sine_fusion
  16.1 2.5 %stage_keys.1 = (bf16[24,64,768]{2,1,0:T(8,128)(2,1)S(1)}, bf16[24,2,64,768]{3,2,1,0:T(8,128)(2,1)}) custom-call(bf16[24,2,64,768]{3,2,1,0:T(8,128)(2,1)} %cache_ref.5), custom_call_target="tpu_custom_call" | custom-call | bytes 4718592 | tf_op jit(solution)/shard_map/stage_keys/pallas_call | solution.py:614
  18.6 0.1 collective-permute-done.2.rest_1_
  18.7 0.3 query.1
  19.1 1.6 %collective-permute-start.7 = (bf16[32,768]{1,0:T(8,128)(2,1)S(1)}, bf16[32,768]{1,0:T(8,128)(2,1)S(1)}, u32[]{:S(2)}, u32[]{:S(2)}) collective-permute-start(bf16[32,768]{1,0:T(8,128)(2,1)S(1)} %get-tuple-element.34.mine_ref.query_ref), channel_id=1, source_target_pairs={{0,4},{4,0},{8,12},{12,8},{16,20},{20,16},{24,28},{28,24},{1,5},{5... | collective-permute-start | bytes 147464 | tf_op jit(solution)/shard_map/ppermute | solution.py:569
  20.7 2.9 %collective-permute-start.6 = (bf16[8,1536]{1,0:T(8,128)(2,1)S(1)}, bf16[8,1536]{1,0:T(8,128)(2,1)S(1)}, u32[]{:S(2)}, u32[]{:S(2)}) collective-permute-start(bf16[8,1536]{1,0:T(8,128)(2,1)S(1)} %get-tuple-element.41), channel_id=1, source_target_pairs={{0,16},{4,20},{8,24},{12,28},{16,0},{20,4},{24,8},{28,12},{1,17},{... | collective-permute-start | bytes 73736 | tf_op jit(solution)/shard_map/ppermute | solution.py:569
  23.6 1.4 %attend.1 = (f32[32,768]{1,0:T(8,128)S(1)}, f32[16,128]{1,0:T(8,128)S(1)}) custom-call(bf16[32,768]{1,0:T(8,128)(2,1)S(1)} %get-tuple-element.34.mine_ref.query_ref, bf16[32,768]{1,0:T(8,128)(2,1)S(1)} %collective-permute-done.7.other_ref, bf16[192,32]{1,0:T(8,128)(2,1)S(1)} %get-tuple-element.31.planned_ref.pick_mine_ref, ...), custom_call_target="tpu_custom_call" | custom-call | tf_op jit(solution)/shard_map/attend/pallas_call | solution.py:679
  25.0 0.7 %collective-permute-done.6.recv_ref = bf16[8,1536]{1,0:T(8,128)(2,1)S(1)} collective-permute-done((bf16[8,1536]{1,0:T(8,128)(2,1)S(1)}, bf16[8,1536]{1,0:T(8,128)(2,1)S(1)}, u32[]{:S(2)}, u32[]{:S(2)}) %collective-permute-start.6) | collective-permute-done | bytes 24608 | tf_op jit(solution)/shard_map/ppermute | solution.py:569
  25.7 0.3 news.1.refs_0_.after_ref.rest_0_
  26.0 2.1 %collective-permute-start.8 = (bf16[256,128]{1,0:T(8,128)(2,1)S(1)}, bf16[256,128]{1,0:T(8,128)(2,1)S(1)}, u32[]{:S(2)}, u32[]{:S(2)}) collective-permute-start(bf16[256,128]{1,0:T(8,128)(2,1)S(1)} %news.1.refs_0_.after_ref.rest_0_), channel_id=1, source_target_pairs={{0,24},{4,28},{8,16},{12,20},{16,8},{20,12},{24,0},{28,4},{1,25},{... | collective-permute-start | bytes 196616 | tf_op jit(solution)/shard_map/ppermute | solution.py:569
  28.1 0.7 %collective-permute-start.9 = (bf16[256,128]{1,0:T(8,128)(2,1)S(1)}, bf16[256,128]{1,0:T(8,128)(2,1)S(1)}, u32[]{:S(2)}, u32[]{:S(2)}) collective-permute-start(bf16[256,128]{1,0:T(8,128)(2,1)S(1)} %news.1.refs_0_.after_ref.rest_0_), channel_id=1, source_target_pairs={{0,16},{4,20},{8,24},{12,28},{16,0},{20,4},{24,8},{28,12},{1,17},{... | collective-permute-start | bytes 196616 | tf_op jit(solution)/shard_map/ppermute | solution.py:569
  28.8 1.7 %collective-permute-start.10 = (bf16[256,128]{1,0:T(8,128)(2,1)S(1)}, bf16[256,128]{1,0:T(8,128)(2,1)S(1)}, u32[]{:S(2)}, u32[]{:S(2)}) collective-permute-start(bf16[256,128]{1,0:T(8,128)(2,1)S(1)} %news.1.refs_0_.after_ref.rest_0_), channel_id=1, source_target_pairs={{0,8},{4,12},{8,0},{12,4},{16,24},{20,28},{24,16},{28,20},{1,9},{5... | collective-permute-start | bytes 196616 | tf_op jit(solution)/shard_map/ppermute | solution.py:569
  30.5 1.7 %collective-permute-done.8.refs_1_.rest_1_ = bf16[256,128]{1,0:T(8,128)(2,1)S(1)} collective-permute-done((bf16[256,128]{1,0:T(8,128)(2,1)S(1)}, bf16[256,128]{1,0:T(8,128)(2,1)S(1)}, u32[]{:S(2)}, u32[]{:S(2)}) %collective-permute-start.8) | collective-permute-done | bytes 65568 | tf_op jit(solution)/shard_map/ppermute | solution.py:569
  32.1 0.5 %collective-permute-start.11 = (bf16[512,128]{1,0:T(8,128)(2,1)S(1)}, bf16[512,128]{1,0:T(8,128)(2,1)S(1)}, u32[]{:S(2)}, u32[]{:S(2)}) collective-permute-start(bf16[512,128]{1,0:T(8,128)(2,1)S(1)} %join.2), channel_id=1, source_target_pairs={{0,4},{4,0},{8,12},{12,8},{16,20},{20,16},{24,28},{28,24},{1,5},{5... | collective-permute-start | bytes 393224 | tf_op jit(solution)/shard_map/ppermute | solution.py:569
  32.7 0.7 %collective-permute-done.9.refs_0_.rest_2_ = bf16[256,128]{1,0:T(8,128)(2,1)S(1)} collective-permute-done((bf16[256,128]{1,0:T(8,128)(2,1)S(1)}, bf16[256,128]{1,0:T(8,128)(2,1)S(1)}, u32[]{:S(2)}, u32[]{:S(2)}) %collective-permute-start.9) | collective-permute-done | bytes 65568 | tf_op jit(solution)/shard_map/ppermute | solution.py:569
  33.4 0.4 collective-permute-done.10.refs_1_.rest_3_
  33.8 1.0 %collective-permute-start.12 = (bf16[512,128]{1,0:T(8,128)(2,1)S(1)}, bf16[512,128]{1,0:T(8,128)(2,1)S(1)}, u32[]{:S(2)}, u32[]{:S(2)}) collective-permute-start(bf16[512,128]{1,0:T(8,128)(2,1)S(1)} %join.3), channel_id=1, source_target_pairs={{0,4},{4,0},{8,12},{12,8},{16,20},{20,16},{24,28},{28,24},{1,5},{5... | collective-permute-start | bytes 393224 | tf_op jit(solution)/shard_map/ppermute | solution.py:569
  34.8 3.5 %fetch.1 = (bf16[24,2,64,768]{3,2,1,0:T(8,128)(2,1)}, bf16[24,2,16,768]{3,2,1,0:T(8,128)(2,1)S(1)}) custom-call(s32[24]{0:T(128)S(1)} %copy-done.4, s32[24]{0:T(128)S(1)} %copy-done.5, s32[64]{0:T(128)S(1)} %copy-done.6, bf16[256,128]{1,0:T(8,128)(2,1)S(1)} %news.1.refs_0_.after_ref.rest_0_, ...), custom_call_target="tpu_custom_call", output_to_operand_aliasing={{0}: (5, {})} | custom-call | bytes 4718592 | tf_op jit(solution)/shard_map/fetch/pallas_call | solution.py:708
  38.3 0.5 %collective-permute-done.12.rest_5_ = bf16[512,128]{1,0:T(8,128)(2,1)S(1)} collective-permute-done((bf16[512,128]{1,0:T(8,128)(2,1)S(1)}, bf16[512,128]{1,0:T(8,128)(2,1)S(1)}, u32[]{:S(2)}, u32[]{:S(2)}) %collective-permute-start.12) | collective-permute-done | bytes 131104 | tf_op jit(solution)/shard_map/ppermute | solution.py:569
  38.8 1.0 %output.1 = (f32[16,384]{1,0:T(8,128)S(1)}, bf16[16,384]{1,0:T(8,128)(2,1)S(1)}, bf16[16,384]{1,0:T(8,128)(2,1)S(1)}, bf16[16,384]{1,0:T(8,128)(2,1)S(1)}) custom-call(s32[1]{0:T(128)} %bitcast.place_ref, bf16[256,128]{1,0:T(8,128)(2,1)S(1)} %news.1.refs_0_.after_ref.rest_0_, bf16[256,128]{1,0:T(8,128)(2,1)S(1)} %collective-permute-done.8.refs_1_.rest_1_, ...), custom_call_target="tpu_custom_call" | custom-call | tf_op jit(solution)/shard_map/output/pallas_call | solution.py:726
  39.9 1.6 %collective-permute-start.14 = (bf16[16,384]{1,0:T(8,128)(2,1)S(1)}, bf16[16,384]{1,0:T(8,128)(2,1)S(1)}, u32[]{:S(2)}, u32[]{:S(2)}) collective-permute-start(bf16[16,384]{1,0:T(8,128)(2,1)S(1)} %get-tuple-element.51), channel_id=1, source_target_pairs={{0,2},{1,3},{2,0},{3,1},{4,6},{5,7},{6,4},{7,5},{8,10},{9,11},{10,... | collective-permute-start | bytes 36872 | tf_op jit(solution)/shard_map/ppermute | solution.py:740
  41.5 0.3 collective-permute-start.13
  41.8 2.0 %patch.1 = bf16[24,2,64,768]{3,2,1,0:T(8,128)(2,1)} custom-call(s32[1]{0:T(128)} %bitcast.1.place_ref, s32[24]{0:T(128)S(1)} %copy-done.4, s32[24]{0:T(128)S(1)} %copy-done.5, s32[64]{0:T(128)S(1)} %copy-done.6, bf16[16,384]{1,0:T(8,128)(2,1)S(1)} %get-tuple-element.50.after_ref, ...), custom_call_target="tpu_custom_call", output_to_operand_aliasing={{}: (12, {})} | custom-call | bytes 2359296 | tf_op jit(solution)/shard_map/patch/pallas_call | solution.py:742
  43.8 0.6 %add_convert_fusion = bf16[16,384]{1,0:T(8,128)(2,1)} fusion(bf16[16,384]{1,0:T(8,128)(2,1)S(1)} %collective-permute-done.15, bf16[16,384]{1,0:T(8,128)(2,1)S(1)} %collective-permute-done.14, f32[16,384]{1,0:T(8,128)S(1)} %get-tuple-element.49, bf16[16,384]{1,0:T(8,128)(2,1)S(1)} %collective-permute-done.13), kind=kLoop, calls=%fused_computation.2 | loop fusion | flops 43008 | bytes 73728 | tf_op jit(solution)/shard_map/convert_element_type | solution.py:757
  (33 shorter events, 0.4 us)
Async XLA Ops:
  0.6 7.5 %copy-start.4 = (s32[24]{0:T(128)S(1)}, s32[24]{0:T(128)}, u32[]{:S(2)}) copy-start(s32[24]{0:T(128)} %owner_ref.5) | copy-start | bytes 292
  0.6 7.5 %copy-start.5 = (s32[24]{0:T(128)S(1)}, s32[24]{0:T(128)}, u32[]{:S(2)}) copy-start(s32[24]{0:T(128)} %index_ref.5) | copy-start | bytes 292
  0.7 7.5 %copy-start.6 = (s32[64]{0:T(128)S(1)}, s32[64]{0:T(128)}, u32[]{:S(2)}) copy-start(s32[64]{0:T(128)} %length_ref.5) | copy-start | bytes 772
  3.3 5.7 %copy-start.3 = (f32[32,896]{1,0:T(8,128)S(1)}, f32[32,896]{1,0:T(8,128)}, u32[]{:S(2)}) copy-start(f32[32,896]{1,0:T(8,128)} %get-tuple-element.29.kept_ref) | copy-start | bytes 344068
  3.3 5.7 %collective-permute-start = (bf16[32,896]{1,0:T(8,128)(2,1)}, bf16[32,896]{1,0:T(8,128)(2,1)S(1)}, u32[]{:S(2)}, u32[]{:S(2)}) collective-permute-start(bf16[32,896]{1,0:T(8,128)(2,1)} %get-tuple-element.30), channel_id=1, source_target_pairs={{0,4},{4,0},{8,12},{12,8},{16,20},{20,16},{24,28},{28,24},{1,5},{5... | collective-permute-start | bytes 172040 | tf_op jit(solution)/shard_map/ppermute | solution.py:569
  6.3 7.9 %collective-permute-start.4 = (bf16[32,1536]{1,0:T(8,128)(2,1)}, bf16[32,1536]{1,0:T(8,128)(2,1)S(1)}, u32[]{:S(2)}, u32[]{:S(2)}) collective-permute-start(bf16[32,1536]{1,0:T(8,128)(2,1)} %get-tuple-element.37), channel_id=1, source_target_pairs={{0,4},{4,0},{8,12},{12,8},{16,20},{20,16},{24,28},{28,24},{1,5},{5... | collective-permute-start | bytes 294920 | tf_op jit(solution)/shard_map/ppermute | solution.py:569
  6.4 7.8 %copy-start.1 = (f32[32,1536]{1,0:T(8,128)S(1)}, f32[32,1536]{1,0:T(8,128)}, u32[]{:S(2)}) copy-start(f32[32,1536]{1,0:T(8,128)} %get-tuple-element.36.kept_ref) | copy-start | bytes 589828
  9.1 9.5 %collective-permute-start.1 = (bf16[208,128]{1,0:T(8,128)(2,1)S(1)}, bf16[208,128]{1,0:T(8,128)(2,1)S(1)}, u32[]{:S(2)}, u32[]{:S(2)}) collective-permute-start(bf16[208,128]{1,0:T(8,128)(2,1)S(1)} %get-tuple-element.33), channel_id=1, source_target_pairs={{0,24},{4,28},{8,16},{12,20},{16,8},{20,12},{24,0},{28,4},{1,25},{... | collective-permute-start | bytes 159752 | tf_op jit(solution)/shard_map/ppermute | solution.py:569
  13.5 5.2 %collective-permute-start.2 = (bf16[208,128]{1,0:T(8,128)(2,1)S(1)}, bf16[208,128]{1,0:T(8,128)(2,1)S(1)}, u32[]{:S(2)}, u32[]{:S(2)}) collective-permute-start(bf16[208,128]{1,0:T(8,128)(2,1)S(1)} %get-tuple-element.33), channel_id=1, source_target_pairs={{0,16},{4,20},{8,24},{12,28},{16,0},{20,4},{24,8},{28,12},{1,17},{... | collective-permute-start | bytes 159752 | tf_op jit(solution)/shard_map/ppermute | solution.py:569
  13.5 5.2 %collective-permute-start.3 = (bf16[208,128]{1,0:T(8,128)(2,1)S(1)}, bf16[208,128]{1,0:T(8,128)(2,1)S(1)}, u32[]{:S(2)}, u32[]{:S(2)}) collective-permute-start(bf16[208,128]{1,0:T(8,128)(2,1)S(1)} %get-tuple-element.33), channel_id=1, source_target_pairs={{0,8},{4,12},{8,0},{12,4},{16,24},{20,28},{24,16},{28,20},{1,9},{5... | collective-permute-start | bytes 159752 | tf_op jit(solution)/shard_map/ppermute | solution.py:569
  14.2 6.4 %collective-permute-start.5 = (bf16[16,1536]{1,0:T(8,128)(2,1)S(1)}, bf16[16,1536]{1,0:T(8,128)(2,1)S(1)}, u32[]{:S(2)}, u32[]{:S(2)}) collective-permute-start(bf16[16,1536]{1,0:T(8,128)(2,1)S(1)} %get-tuple-element.39), channel_id=1, source_target_pairs={{0,8},{4,12},{8,0},{12,4},{16,24},{20,28},{24,16},{28,20},{1,9},{5... | collective-permute-start | bytes 147464 | tf_op jit(solution)/shard_map/ppermute | solution.py:569
  19.1 4.5 %collective-permute-start.7 = (bf16[32,768]{1,0:T(8,128)(2,1)S(1)}, bf16[32,768]{1,0:T(8,128)(2,1)S(1)}, u32[]{:S(2)}, u32[]{:S(2)}) collective-permute-start(bf16[32,768]{1,0:T(8,128)(2,1)S(1)} %get-tuple-element.34.mine_ref.query_ref), channel_id=1, source_target_pairs={{0,4},{4,0},{8,12},{12,8},{16,20},{20,16},{24,28},{28,24},{1,5},{5... | collective-permute-start | bytes 147464 | tf_op jit(solution)/shard_map/ppermute | solution.py:569
  20.7 5.1 %collective-permute-start.6 = (bf16[8,1536]{1,0:T(8,128)(2,1)S(1)}, bf16[8,1536]{1,0:T(8,128)(2,1)S(1)}, u32[]{:S(2)}, u32[]{:S(2)}) collective-permute-start(bf16[8,1536]{1,0:T(8,128)(2,1)S(1)} %get-tuple-element.41), channel_id=1, source_target_pairs={{0,16},{4,20},{8,24},{12,28},{16,0},{20,4},{24,8},{28,12},{1,17},{... | collective-permute-start | bytes 73736 | tf_op jit(solution)/shard_map/ppermute | solution.py:569
  26.0 6.1 %collective-permute-start.8 = (bf16[256,128]{1,0:T(8,128)(2,1)S(1)}, bf16[256,128]{1,0:T(8,128)(2,1)S(1)}, u32[]{:S(2)}, u32[]{:S(2)}) collective-permute-start(bf16[256,128]{1,0:T(8,128)(2,1)S(1)} %news.1.refs_0_.after_ref.rest_0_), channel_id=1, source_target_pairs={{0,24},{4,28},{8,16},{12,20},{16,8},{20,12},{24,0},{28,4},{1,25},{... | collective-permute-start | bytes 196616 | tf_op jit(solution)/shard_map/ppermute | solution.py:569
  28.1 5.3 %collective-permute-start.9 = (bf16[256,128]{1,0:T(8,128)(2,1)S(1)}, bf16[256,128]{1,0:T(8,128)(2,1)S(1)}, u32[]{:S(2)}, u32[]{:S(2)}) collective-permute-start(bf16[256,128]{1,0:T(8,128)(2,1)S(1)} %news.1.refs_0_.after_ref.rest_0_), channel_id=1, source_target_pairs={{0,16},{4,20},{8,24},{12,28},{16,0},{20,4},{24,8},{28,12},{1,17},{... | collective-permute-start | bytes 196616 | tf_op jit(solution)/shard_map/ppermute | solution.py:569
  28.8 5.0 %collective-permute-start.10 = (bf16[256,128]{1,0:T(8,128)(2,1)S(1)}, bf16[256,128]{1,0:T(8,128)(2,1)S(1)}, u32[]{:S(2)}, u32[]{:S(2)}) collective-permute-start(bf16[256,128]{1,0:T(8,128)(2,1)S(1)} %news.1.refs_0_.after_ref.rest_0_), channel_id=1, source_target_pairs={{0,8},{4,12},{8,0},{12,4},{16,24},{20,28},{24,16},{28,20},{1,9},{5... | collective-permute-start | bytes 196616 | tf_op jit(solution)/shard_map/ppermute | solution.py:569
  32.1 6.1 %collective-permute-start.11 = (bf16[512,128]{1,0:T(8,128)(2,1)S(1)}, bf16[512,128]{1,0:T(8,128)(2,1)S(1)}, u32[]{:S(2)}, u32[]{:S(2)}) collective-permute-start(bf16[512,128]{1,0:T(8,128)(2,1)S(1)} %join.2), channel_id=1, source_target_pairs={{0,4},{4,0},{8,12},{12,8},{16,20},{20,16},{24,28},{28,24},{1,5},{5... | collective-permute-start | bytes 393224 | tf_op jit(solution)/shard_map/ppermute | solution.py:569
  33.8 5.0 %collective-permute-start.12 = (bf16[512,128]{1,0:T(8,128)(2,1)S(1)}, bf16[512,128]{1,0:T(8,128)(2,1)S(1)}, u32[]{:S(2)}, u32[]{:S(2)}) collective-permute-start(bf16[512,128]{1,0:T(8,128)(2,1)S(1)} %join.3), channel_id=1, source_target_pairs={{0,4},{4,0},{8,12},{12,8},{16,20},{20,16},{24,28},{28,24},{1,5},{5... | collective-permute-start | bytes 393224 | tf_op jit(solution)/shard_map/ppermute | solution.py:569
  34.8 4.1 %copy-start = (bf16[768,384]{1,0:T(8,128)(2,1)S(1)}, bf16[768,384]{1,0:T(8,128)(2,1)}, u32[]{:S(2)}) copy-start(bf16[768,384]{1,0:T(8,128)(2,1)} %rest_6_.1) | copy-start | bytes 1769476
  34.8 4.1 %copy-start.2 = (bf16[64,384]{1,0:T(8,128)(2,1)S(1)}, bf16[64,384]{1,0:T(8,128)(2,1)}, u32[]{:S(2)}) copy-start(bf16[64,384]{1,0:T(8,128)(2,1)} %rest_7_.1) | copy-start | bytes 147460
  39.8 3.9 %collective-permute-start.15 = (bf16[16,384]{1,0:T(8,128)(2,1)S(1)}, bf16[16,384]{1,0:T(8,128)(2,1)S(1)}, u32[]{:S(2)}, u32[]{:S(2)}) collective-permute-start(bf16[16,384]{1,0:T(8,128)(2,1)S(1)} %get-tuple-element.52), channel_id=1, source_target_pairs={{0,3},{1,2},{2,1},{3,0},{4,7},{5,6},{6,5},{7,4},{8,11},{9,10},{10,... | collective-permute-start | bytes 36872 | tf_op jit(solution)/shard_map/ppermute | solution.py:740
  39.9 3.8 %collective-permute-start.14 = (bf16[16,384]{1,0:T(8,128)(2,1)S(1)}, bf16[16,384]{1,0:T(8,128)(2,1)S(1)}, u32[]{:S(2)}, u32[]{:S(2)}) collective-permute-start(bf16[16,384]{1,0:T(8,128)(2,1)S(1)} %get-tuple-element.51), channel_id=1, source_target_pairs={{0,2},{1,3},{2,0},{3,1},{4,6},{5,7},{6,4},{7,5},{8,10},{9,11},{10,... | collective-permute-start | bytes 36872 | tf_op jit(solution)/shard_map/ppermute | solution.py:740
  41.5 2.3 %collective-permute-start.13 = (bf16[16,384]{1,0:T(8,128)(2,1)S(1)}, bf16[16,384]{1,0:T(8,128)(2,1)S(1)}, u32[]{:S(2)}, u32[]{:S(2)}) collective-permute-start(bf16[16,384]{1,0:T(8,128)(2,1)S(1)} %get-tuple-element.50.after_ref), channel_id=1, source_target_pairs={{0,1},{1,0},{2,3},{3,2},{4,5},{5,4},{6,7},{7,6},{8,9},{9,8},{10,11... | collective-permute-start | bytes 36872 | tf_op jit(solution)/shard_map/ppermute | solution.py:740

commit v7 on v6

--- a/solution.py
+++ b/solution.py
@@ -18,7 +18,6 @@
 SMEM = pltpu.MemorySpace.SMEM
 HEADS = 8
 ROWS = 16
-JOINS = 2
 
 
 def split3(value):
@@ -216,33 +215,10 @@
         first += value.shape[0]
 
 
-def stage(part, cache_ref, near_ref, updated_ref, loads, stores):
-    spans = [pl.ds(first, GROUP) for first in range(0, cache_ref.shape[0], GROUP)]
-    load = [
-        pltpu.make_async_copy(cache_ref.at[span, part], near_ref.at[span], loads.at[i])
-        for i, span in enumerate(spans)
-    ]
-    store = [
-        pltpu.make_async_copy(near_ref.at[span], updated_ref.at[span, part], stores.at[i])
-        for i, span in enumerate(spans)
-    ]
-    for copy in load:
-        copy.start()
-    for arriving, leaving in zip(load, store):
-        arriving.wait()
-        leaving.start()
-    for copy in store:
-        copy.wait()
-
-
-def stage_keys_kernel(cache_ref, keys_ref, updated_ref, loads, stores):
-    stage(0, cache_ref, keys_ref, updated_ref, loads, stores)
-
-
-def stage_values_kernel(cache_ref, values_ref, loads):
+def stage_kernel(part, cache_ref, near_ref, sems):
     copies = [
         pltpu.make_async_copy(
-            cache_ref.at[pl.ds(first, GROUP), 1], values_ref.at[pl.ds(first, GROUP)], loads.at[i]
+            cache_ref.at[pl.ds(first, GROUP), part], near_ref.at[pl.ds(first, GROUP)], sems.at[i]
         )
         for i, first in enumerate(range(0, cache_ref.shape[0], GROUP))
     ]
@@ -250,6 +226,28 @@
         copy.start()
     for copy in copies:
         copy.wait()
+
+
+def store(part, near_ref, updated_ref, token_ref, sems):
+    copies = [
+        pltpu.make_async_copy(
+            near_ref.at[pl.ds(first, GROUP)], updated_ref.at[pl.ds(first, GROUP), part], sems.at[i]
+        )
+        for i, first in enumerate(range(0, near_ref.shape[0], GROUP))
+    ]
+    for copy in copies:
+        copy.start()
+    token_ref[...] = jnp.zeros_like(token_ref)
+    for copy in copies:
+        copy.wait()
+
+
+def store_keys_kernel(after_ref, keys_ref, updated_ref, token_ref, sems):
+    store(0, keys_ref, updated_ref, token_ref, sems)
+
+
+def store_values_kernel(after_ref, values_ref, held_ref, updated_ref, token_ref, sems):
+    store(1, values_ref, updated_ref, token_ref, sems)
 
 
 def read_block(b, owner_ref, index_ref, length_ref, tokens):
@@ -298,6 +296,7 @@
     name_ref,
     keys_ref,
     values_ref,
+    after_ref,
     part_ref,
     stat_ref,
 ):
@@ -376,48 +375,19 @@
         pl.when(spot[2] >= 0)(functools.partial(do, *spot))
 
 
-def fetch_kernel(
-    owner_ref,
-    index_ref,
-    length_ref,
-    after_ref,
-    cache_ref,
-    held_ref,
-    updated_ref,
-    near_ref,
-    values,
-    loads,
-    stores,
-    fetches,
-):
+def fetch_kernel(owner_ref, index_ref, length_ref, after_ref, cache_ref, near_ref, sems):
     found = slots(cache_ref.shape[2], owner_ref, index_ref, length_ref)
 
     def fetch(b, owner, slot, first):
         return pltpu.make_async_copy(
-            cache_ref.at[b, :, pl.ds(first, ROWS), :], near_ref.at[b], fetches.at[b]
+            cache_ref.at[b, :, pl.ds(first, ROWS), :], near_ref.at[b], sems.at[b]
         )
 
-    spans = [pl.ds(first, GROUP) for first in range(0, cache_ref.shape[0], GROUP)]
-    load = [
-        pltpu.make_async_copy(cache_ref.at[span, 1], values.at[span], loads.at[i])
-        for i, span in enumerate(spans)
-    ]
-    store = [
-        pltpu.make_async_copy(values.at[span], updated_ref.at[span, 1], stores.at[i])
-        for i, span in enumerate(spans)
-    ]
-    for copy in load:
-        copy.start()
     each(found, lambda *at: fetch(*at).start())
-    for arriving, leaving in zip(load, store):
-        arriving.wait()
-        leaving.start()
     each(found, lambda *at: fetch(*at).wait())
-    for copy in store:
-        copy.wait()
-
-
-def join_kernel(*refs):
+
+
+def join_kernel(after_ref, *refs):
     out_ref = refs[-1]
     rows = refs[0].shape[0]
     for i, ref in enumerate(refs[:-1]):
@@ -428,21 +398,25 @@
     return [0, *range(lines - 1, 0, -1)]
 
 
+def line_groups(lines):
+    return [[0, 1], *([i] for i in range(2, lines))]
+
+
 def pieces_of(column, crossed):
     rows = column[0].shape[0]
-    each = len(column) // len(crossed)
+    order = line_order(len(column))
     pieces = [None] * (2 * len(column))
-    for i, m in enumerate(line_order(len(column))):
-        first = i % each * rows
-        pieces[2 * m] = column[i]
-        pieces[2 * m + 1] = crossed[i // each].at[first : first + rows]
+    for ref, group in zip(crossed, line_groups(len(column))):
+        for k, i in enumerate(group):
+            pieces[2 * order[i]] = column[i]
+            pieces[2 * order[i] + 1] = ref.at[k * rows : (k + 1) * rows]
     return pieces
 
 
 def patch_kernel(count, place_ref, owner_ref, index_ref, length_ref, after_ref, *rest):
     lines = count // 2
-    pieces = pieces_of(rest[:lines], rest[lines : lines + JOINS])
-    near_ref, held_ref, updated_ref, fresh, patch, stores = rest[lines + JOINS :]
+    pieces = pieces_of(rest[:lines], rest[lines : lines + len(line_groups(lines))])
+    near_ref, held_ref, updated_ref, fresh, patch, stores = rest[lines + len(line_groups(lines)) :]
     _, _, tokens, columns = updated_ref.shape
     requests = length_ref.shape[0]
     share = fresh.shape[1] // 2
@@ -479,8 +453,8 @@
 
 def output_kernel(count, place_ref, *rest):
     lines = count // 2
-    pieces = pieces_of(rest[:lines], rest[lines : lines + JOINS])
-    w_ref, states_ref, after_ref, own_ref, *sends, product = rest[lines + JOINS :]
+    pieces = pieces_of(rest[:lines], rest[lines : lines + len(line_groups(lines))])
+    w_ref, states_ref, after_ref, own_ref, *sends, product = rest[lines + len(line_groups(lines)) :]
     heads = HEADS
     columns = w_ref.shape[0]
     chunks = columns // LANES
@@ -611,27 +585,19 @@
         compiler_params=limit,
         name="plan",
     )(at, *table)
-    keys, updated = pl.pallas_call(
-        stage_keys_kernel,
-        out_shape=(array(blocks, tokens, columns), array(*cache.shape)),
-        in_specs=[in_hbm],
-        out_specs=(in_vmem, in_hbm),
-        scratch_shapes=[pltpu.SemaphoreType.DMA((steps,))] * 2,
-        compiler_params=most_room,
-        cost_estimate=moves(cache.size * 2),
-        name="stage_keys",
-    )(cache)
-
-    values = pl.pallas_call(
-        stage_values_kernel,
-        out_shape=array(blocks, tokens, columns),
-        in_specs=[in_hbm],
-        out_specs=in_vmem,
-        scratch_shapes=[pltpu.SemaphoreType.DMA((steps,))],
-        compiler_params=most_room,
-        cost_estimate=moves(cache.size),
-        name="stage_values",
-    )(cache)
+    def stage(part, name):
+        return pl.pallas_call(
+            functools.partial(stage_kernel, part),
+            out_shape=array(blocks, tokens, columns),
+            in_specs=[in_hbm],
+            out_specs=in_vmem,
+            scratch_shapes=[pltpu.SemaphoreType.DMA((steps,))],
+            compiler_params=most_room,
+            cost_estimate=moves(cache.size),
+            name=name,
+        )(cache)
+
+    keys, values = stage(0, "stage_keys"), stage(1, "stage_values")
     message = columns // LANES * half + ROWS * pl.cdiv(half, LANES)
     send, query = pl.pallas_call(
         halve_query_kernel,
@@ -640,7 +606,7 @@
         compiler_params=pltpu.CompilerParams(vmem_limit_bytes=47 * 1024 * 1024),
         name="halve_query",
     )(kept, received, values, plan[0])
-    received = [to_peer(send, 2 * m) for m in line_order(lines)[1:]]
+    received = [to_peer(send, 2 * m) for m in (1, *range(lines - 1, 1, -1))]
     (mask, sent_to, held), *later = sum_plan(lines)
     fresh_send, fresh = pl.pallas_call(
         functools.partial(halve_fresh_kernel, sent_to, held),
@@ -675,6 +641,16 @@
         name="query",
     )(keys, query, cosine, sine, *received)
     other = to_peer(mine, 1)
+    updated, token = pl.pallas_call(
+        store_keys_kernel,
+        out_shape=(array(*cache.shape), array(8, LANES, dtype=jnp.float32)),
+        in_specs=[anywhere, in_vmem],
+        out_specs=(in_hbm, in_vmem),
+        scratch_shapes=[pltpu.SemaphoreType.DMA((steps,))],
+        compiler_params=most_room,
+        cost_estimate=moves(cache.size),
+        name="store_keys",
+    )(mine, keys)
 
     part, stat = pl.pallas_call(
         attend_kernel,
@@ -682,10 +658,10 @@
             array(2 * ROWS, columns, dtype=jnp.float32),
             array(ROWS, LANES, dtype=jnp.float32),
         ),
-        in_specs=[in_vmem] * 8,
+        in_specs=[in_vmem] * 8 + [anywhere],
         compiler_params=pltpu.CompilerParams(vmem_limit_bytes=47 * 1024 * 1024),
         name="attend",
-    )(mine, other, *plan, keys, values)
+    )(mine, other, *plan, keys, values, token)
     piece = pl.pallas_call(
         news_kernel,
         out_shape=array(columns // LANES * (2 * ROWS + share) + ROWS, LANES),
@@ -694,33 +670,40 @@
         compiler_params=limit,
         name="news",
     )(at, mine, scale, cosine, sine, fresh, fresh_received, part, stat)
+    updated, token = pl.pallas_call(
+        store_values_kernel,
+        out_shape=(array(*cache.shape), array(8, LANES, dtype=jnp.float32)),
+        in_specs=[anywhere, in_vmem, in_hbm],
+        out_specs=(in_hbm, in_vmem),
+        scratch_shapes=[pltpu.SemaphoreType.DMA((steps,))],
+        input_output_aliases={2: 0},
+        compiler_params=most_room,
+        cost_estimate=moves(cache.size),
+        name="store_values",
+    )(piece, values, updated)
     column = [to_peer(piece, 2 * m) if m else piece for m in line_order(lines)]
-    each = lines // JOINS
     pieces = list(column)
-    for first in range(0, lines, each):
-        joined = pl.pallas_call(
-            join_kernel,
-            out_shape=array(each * piece.shape[0], LANES),
-            compiler_params=limit,
-            name="join",
-        )(*column[first : first + each])
+    for group in line_groups(lines):
+        joined = column[group[0]]
+        if len(group) > 1:
+            joined = pl.pallas_call(
+                join_kernel,
+                out_shape=array(len(group) * piece.shape[0], LANES),
+                in_specs=[anywhere] + [in_vmem] * len(group),
+                compiler_params=limit,
+                name="join",
+            )(token, *[column[i] for i in group])
         pieces.append(to_peer(joined, 1))
-    updated, near = pl.pallas_call(
+    near = pl.pallas_call(
         fetch_kernel,
-        out_shape=(array(*cache.shape), array(blocks, 2, ROWS, columns)),
-        in_specs=[in_smem] * 3 + [anywhere, in_hbm, in_hbm],
-        out_specs=(in_hbm, in_vmem),
-        scratch_shapes=[
-            pltpu.VMEM((blocks, tokens, columns), jnp.bfloat16),
-            pltpu.SemaphoreType.DMA((steps,)),
-            pltpu.SemaphoreType.DMA((steps,)),
-            pltpu.SemaphoreType.DMA((blocks,)),
-        ],
-        input_output_aliases={5: 0},
+        out_shape=array(blocks, 2, ROWS, columns),
+        in_specs=[in_smem] * 3 + [anywhere, in_hbm],
+        out_specs=in_vmem,
+        scratch_shapes=[pltpu.SemaphoreType.DMA((blocks,))],
         compiler_params=most_room,
-        cost_estimate=moves(cache.size * 2),
+        cost_estimate=moves(blocks * ROWS * columns * 8),
         name="fetch",
-    )(*table, piece, cache, updated)
+    )(*table, piece, cache)
     rank = lax.axis_index("tp")
     kept_rows = requests // ranks
     own, *sends = pl.pallas_call(
@@ -736,7 +719,7 @@
         name="output",
     )(rank.reshape(1).astype(jnp.int32), *pieces, w_out, states, near)
     total = own
-    for m in range(1, ranks):
+    for m in range(ranks - 1, 0, -1):
         moved = lax.ppermute(sends[m - 1], "tp", [(i, i ^ m) for i in range(ranks)])
         total = total + moved.astype(jnp.float32)
     updated = pl.pallas_call(

time: 44.6 us -> 44 us (0.987)
  waiting for transfers between devices: 4.2 us -> 3.05 us
    ppermute x13 -> x14, waiting for transfers between devices: 4.19 us -> 3.04 us  [to_peer(): return lax.ppermute(value, 'seq', [(i, i ^ m) for i in range(peers)])]
    pallas_call x5 -> x6, Pallas kernels: 7.67 us -> 8.05 us  [the longest x2 3.32 us: stage(): pl.pallas_call(functools.partial(stage_kernel, part), out_shape=array(blo...]
    ppermute x13 -> x14, starting transfers between devices: 20.1 us -> 20.2 us  [to_peer(): return lax.ppermute(value, 'seq', [(i, i ^ m) for i in range(peers)])]
  transfers between devices with their start and end apart: 16 -> 17, of which waited for: 6 -> 5; matrix products, arithmetic and copies ran while one was open for 1% -> 1% of each run, Pallas kernels for 28% -> 29%
where the time goes in v7:
time: 44 us; the launch traced here: 43.8 us
  starting transfers between devices  22.1 us (50%)
  Pallas kernels  16.5 us (38%)
  waiting for transfers between devices  3.05 us (7%)
  other arithmetic  1.13 us (3%)
  between operations  0.9 us (2%)
    ppermute x14, starting transfers between devices, to_peer(): return lax.ppermute(value, 'seq', [(i, i ^ m) for i in range(peers)])  20.2 us
    pallas_call x2, Pallas kernels, stage(): pl.pallas_call(functools.partial(stage_kernel, part), out_shape=array(blo...  3.32 us
    ppermute x14, waiting for transfers between devices, to_peer(): return lax.ppermute(value, 'seq', [(i, i ^ m) for i in range(peers)])  3.04 us
    pallas_call x1, Pallas kernels, shards(): pl.pallas_call(project_kernel, out_shape=(array(half, columns + LANES), a...  2.59 us
    pallas_call x1, Pallas kernels, shards(): pl.pallas_call(functools.partial(patch_kernel, peers), out_shape=array(*c...  1.96 us
    ppermute x3, starting transfers between devices, shards(): moved = lax.ppermute(sends[m - 1], 'tp', [(i, i ^ m) for i in range(ranks)])  1.92 us
    pallas_call x1, Pallas kernels, shards(): pl.pallas_call(fetch_kernel, out_shape=array(blocks, 2, ROWS, columns), i...  1.84 us
    pallas_call x1, Pallas kernels, shards(): pl.pallas_call(store_keys_kernel, out_shape=(array(*cache.shape), array(8...  1.44 us
  transfers between devices with their start and end apart: 17, of which 5 were waited for; matrix products, arithmetic and copies ran while one was open for 1% of the time, Pallas kernels for 29%

profile of v7, /device:TPU:0, one launch (start us, length us, event | category | flops | bytes accessed | tf_op | source)
XLA Modules:
  0.0 43.8 jit_solution(5711207048753898548)
XLA Ops:
  0.7 2.6 %project.1 = (bf16[32,896]{1,0:T(8,128)(2,1)}, f32[32,896]{1,0:T(8,128)}, bf16[32,1536]{1,0:T(8,128)(2,1)}, f32[32,1536]{1,0:T(8,128)}) custom-call(s32[1]{0:T(128)} %bitcast.1.place_ref, bf16[64,384]{1,0:T(8,128)(2,1)} %rest_8_.1, bf16[384]{0:T(512)(128)(2,1)} %gain_ref.1, bf16[3,384,768]{2,1,0:T(8,128)(2,1)} %w_ref.1), custom_call_target="tpu_custom_call" | custom-call | tf_op jit(solution)/shard_map/project/pallas_call | solution.py:548
  3.3 3.0 %collective-permute-start = (bf16[32,896]{1,0:T(8,128)(2,1)}, bf16[32,896]{1,0:T(8,128)(2,1)S(1)}, u32[]{:S(2)}, u32[]{:S(2)}) collective-permute-start(bf16[32,896]{1,0:T(8,128)(2,1)} %get-tuple-element.29), channel_id=1, source_target_pairs={{0,4},{4,0},{8,12},{12,8},{16,20},{20,16},{24,28},{28,24},{1,5},{5... | collective-permute-start | bytes 172040 | tf_op jit(solution)/shard_map/ppermute | solution.py:543
  6.4 1.7 %stage_values.1.after_ref.values_ref = bf16[24,64,768]{2,1,0:T(8,128)(2,1)S(1)} custom-call(bf16[24,2,64,768]{3,2,1,0:T(8,128)(2,1)} %cache_ref.5), custom_call_target="tpu_custom_call" | custom-call | bytes 2359296 | tf_op jit(solution)/shard_map/stage_values/pallas_call | solution.py:589
  8.1 0.7 %plan.1 = (bf16[192,32]{1,0:T(8,128)(2,1)S(1)}, bf16[192,32]{1,0:T(8,128)(2,1)S(1)}, s32[192,128]{1,0:T(8,128)S(1)}, f32[192,128]{1,0:T(8,128)S(1)}) custom-call(s32[1]{0:T(128)} %bitcast.1.place_ref, s32[24]{0:T(128)S(1)} %copy-done.4, s32[24]{0:T(128)S(1)} %copy-done.5, s32[64]{0:T(128)S(1)} %copy-done.6), custom_call_target="tpu_custom_call" | custom-call | tf_op jit(solution)/shard_map/plan/pallas_call | solution.py:576
  9.1 3.4 %collective-permute-start.3 = (bf16[208,128]{1,0:T(8,128)(2,1)S(1)}, bf16[208,128]{1,0:T(8,128)(2,1)S(1)}, u32[]{:S(2)}, u32[]{:S(2)}) collective-permute-start(bf16[208,128]{1,0:T(8,128)(2,1)S(1)} %get-tuple-element.32), channel_id=1, source_target_pairs={{0,16},{4,20},{8,24},{12,28},{16,0},{20,4},{24,8},{28,12},{1,17},{... | collective-permute-start | bytes 159752 | tf_op jit(solution)/shard_map/ppermute | solution.py:543
  12.5 1.3 %collective-permute-start.2 = (bf16[208,128]{1,0:T(8,128)(2,1)S(1)}, bf16[208,128]{1,0:T(8,128)(2,1)S(1)}, u32[]{:S(2)}, u32[]{:S(2)}) collective-permute-start(bf16[208,128]{1,0:T(8,128)(2,1)S(1)} %get-tuple-element.32), channel_id=1, source_target_pairs={{0,24},{4,28},{8,16},{12,20},{16,8},{20,12},{24,0},{28,4},{1,25},{... | collective-permute-start | bytes 159752 | tf_op jit(solution)/shard_map/ppermute | solution.py:543
  13.9 0.2 collective-permute-start.1
  14.1 1.9 %collective-permute-start.5 = (bf16[16,1536]{1,0:T(8,128)(2,1)S(1)}, bf16[16,1536]{1,0:T(8,128)(2,1)S(1)}, u32[]{:S(2)}, u32[]{:S(2)}) collective-permute-start(bf16[16,1536]{1,0:T(8,128)(2,1)S(1)} %get-tuple-element.38), channel_id=1, source_target_pairs={{0,8},{4,12},{8,0},{12,4},{16,24},{20,28},{24,16},{28,20},{1,9},{5... | collective-permute-start | bytes 147464 | tf_op jit(solution)/shard_map/ppermute | solution.py:543
  16.0 0.4 multiply_sine_fusion
  16.4 1.6 %stage_keys.1.after_ref.keys_ref = bf16[24,64,768]{2,1,0:T(8,128)(2,1)S(1)} custom-call(bf16[24,2,64,768]{3,2,1,0:T(8,128)(2,1)} %cache_ref.5), custom_call_target="tpu_custom_call" | custom-call | bytes 2359296 | tf_op jit(solution)/shard_map/stage_keys/pallas_call | solution.py:589
  18.1 0.5 %collective-permute-done.2.rest_1_ = bf16[208,128]{1,0:T(8,128)(2,1)S(1)} collective-permute-done((bf16[208,128]{1,0:T(8,128)(2,1)S(1)}, bf16[208,128]{1,0:T(8,128)(2,1)S(1)}, u32[]{:S(2)}, u32[]{:S(2)}) %collective-permute-start.2) | collective-permute-done | bytes 53280 | tf_op jit(solution)/shard_map/ppermute | solution.py:543
  18.6 0.3 query.1
  18.9 1.6 %collective-permute-start.7 = (bf16[32,768]{1,0:T(8,128)(2,1)S(1)}, bf16[32,768]{1,0:T(8,128)(2,1)S(1)}, u32[]{:S(2)}, u32[]{:S(2)}) collective-permute-start(bf16[32,768]{1,0:T(8,128)(2,1)S(1)} %get-tuple-element.33.after_ref.mine_ref.query_ref), channel_id=1, source_target_pairs={{0,4},{4,0},{8,12},{12,8},{16,20},{20,16},{24,28},{28,24},{1,5},{5... | collective-permute-start | bytes 147464 | tf_op jit(solution)/shard_map/ppermute | solution.py:543
  20.5 1.3 %collective-permute-start.6 = (bf16[8,1536]{1,0:T(8,128)(2,1)S(1)}, bf16[8,1536]{1,0:T(8,128)(2,1)S(1)}, u32[]{:S(2)}, u32[]{:S(2)}) collective-permute-start(bf16[8,1536]{1,0:T(8,128)(2,1)S(1)} %get-tuple-element.40), channel_id=1, source_target_pairs={{0,16},{4,20},{8,24},{12,28},{16,0},{20,4},{24,8},{28,12},{1,17},{... | collective-permute-start | bytes 73736 | tf_op jit(solution)/shard_map/ppermute | solution.py:543
  21.8 1.4 %store_keys.1 = (bf16[24,2,64,768]{3,2,1,0:T(8,128)(2,1)}, f32[8,128]{1,0:T(8,128)S(1)}) custom-call(bf16[32,768]{1,0:T(8,128)(2,1)S(1)} %get-tuple-element.33.after_ref.mine_ref.query_ref, bf16[24,64,768]{2,1,0:T(8,128)(2,1)S(1)} %stage_keys.1.after_ref.keys_ref), custom_call_target="tpu_custom_call" | custom-call | bytes 2359296 | tf_op jit(solution)/shard_map/store_keys/pallas_call | solution.py:644
  23.3 1.4 %attend.1 = (f32[32,768]{1,0:T(8,128)S(1)}, f32[16,128]{1,0:T(8,128)S(1)}) custom-call(bf16[32,768]{1,0:T(8,128)(2,1)S(1)} %get-tuple-element.33.after_ref.mine_ref.query_ref, bf16[32,768]{1,0:T(8,128)(2,1)S(1)} %collective-permute-done.7.other_ref, bf16[192,32]{1,0:T(8,128)(2,1)S(1)} %get-tuple-element.30.planned_ref.pick_mine_ref, ...), custom_call_target="tpu_custom_call" | custom-call | tf_op jit(solution)/shard_map/attend/pallas_call | solution.py:655
  24.7 0.6 %collective-permute-done.6.recv_ref = bf16[8,1536]{1,0:T(8,128)(2,1)S(1)} collective-permute-done((bf16[8,1536]{1,0:T(8,128)(2,1)S(1)}, bf16[8,1536]{1,0:T(8,128)(2,1)S(1)}, u32[]{:S(2)}, u32[]{:S(2)}) %collective-permute-start.6) | collective-permute-done | bytes 24608 | tf_op jit(solution)/shard_map/ppermute | solution.py:543
  25.3 0.3 news.1.after_ref.refs_0_.rest_0_
  25.6 2.3 %collective-permute-start.8 = (bf16[256,128]{1,0:T(8,128)(2,1)S(1)}, bf16[256,128]{1,0:T(8,128)(2,1)S(1)}, u32[]{:S(2)}, u32[]{:S(2)}) collective-permute-start(bf16[256,128]{1,0:T(8,128)(2,1)S(1)} %news.1.after_ref.refs_0_.rest_0_), channel_id=1, source_target_pairs={{0,24},{4,28},{8,16},{12,20},{16,8},{20,12},{24,0},{28,4},{1,25},{... | collective-permute-start | bytes 196616 | tf_op jit(solution)/shard_map/ppermute | solution.py:543
  27.9 2.1 %collective-permute-start.9 = (bf16[256,128]{1,0:T(8,128)(2,1)S(1)}, bf16[256,128]{1,0:T(8,128)(2,1)S(1)}, u32[]{:S(2)}, u32[]{:S(2)}) collective-permute-start(bf16[256,128]{1,0:T(8,128)(2,1)S(1)} %news.1.after_ref.refs_0_.rest_0_), channel_id=1, source_target_pairs={{0,16},{4,20},{8,24},{12,28},{16,0},{20,4},{24,8},{28,12},{1,17},{... | collective-permute-start | bytes 196616 | tf_op jit(solution)/shard_map/ppermute | solution.py:543
  30.0 1.4 %store_values.1 = (bf16[24,2,64,768]{3,2,1,0:T(8,128)(2,1)}, f32[8,128]{1,0:T(8,128)S(1)}) custom-call(bf16[256,128]{1,0:T(8,128)(2,1)S(1)} %news.1.after_ref.refs_0_.rest_0_, bf16[24,64,768]{2,1,0:T(8,128)(2,1)S(1)} %stage_values.1.after_ref.values_ref, bf16[24,2,64,768]{3,2,1,0:T(8,128)(2,1)} %get-tuple-element.47.held_ref), custom_call_target="tpu_custom_call", output_to_operand_aliasing={{0}: (2, {})} | custom-call | bytes 2359296 | tf_op jit(solution)/shard_map/store_values/pallas_call | solution.py:673
  31.7 0.8 %collective-permute-start.11 = (bf16[512,128]{1,0:T(8,128)(2,1)S(1)}, bf16[512,128]{1,0:T(8,128)(2,1)S(1)}, u32[]{:S(2)}, u32[]{:S(2)}) collective-permute-start(bf16[512,128]{1,0:T(8,128)(2,1)S(1)} %join.1), channel_id=1, source_target_pairs={{0,4},{4,0},{8,12},{12,8},{16,20},{20,16},{24,28},{28,24},{1,5},{5... | collective-permute-start | bytes 393224 | tf_op jit(solution)/shard_map/ppermute | solution.py:543
  32.6 1.3 %collective-permute-start.13 = (bf16[256,128]{1,0:T(8,128)(2,1)S(1)}, bf16[256,128]{1,0:T(8,128)(2,1)S(1)}, u32[]{:S(2)}, u32[]{:S(2)}) collective-permute-start(bf16[256,128]{1,0:T(8,128)(2,1)S(1)} %collective-permute-done.10.rest_3_), channel_id=1, source_target_pairs={{0,4},{4,0},{8,12},{12,8},{16,20},{20,16},{24,28},{28,24},{1,5},{5... | collective-permute-start | bytes 196616 | tf_op jit(solution)/shard_map/ppermute | solution.py:543
  33.9 0.8 %collective-permute-start.12 = (bf16[256,128]{1,0:T(8,128)(2,1)S(1)}, bf16[256,128]{1,0:T(8,128)(2,1)S(1)}, u32[]{:S(2)}, u32[]{:S(2)}) collective-permute-start(bf16[256,128]{1,0:T(8,128)(2,1)S(1)} %collective-permute-done.9.rest_2_), channel_id=1, source_target_pairs={{0,4},{4,0},{8,12},{12,8},{16,20},{20,16},{24,28},{28,24},{1,5},{5... | collective-permute-start | bytes 196616 | tf_op jit(solution)/shard_map/ppermute | solution.py:543
  34.6 1.8 %fetch.1.rest_9_.rest_7_ = bf16[24,2,16,768]{3,2,1,0:T(8,128)(2,1)S(1)} custom-call(s32[24]{0:T(128)S(1)} %copy-done.4, s32[24]{0:T(128)S(1)} %copy-done.5, s32[64]{0:T(128)S(1)} %copy-done.6, bf16[256,128]{1,0:T(8,128)(2,1)S(1)} %news.1.after_ref.refs_0_.rest_0_, bf16[24,2,64,768]{3,2,1,0:T(8,128)(2,1)} %cache_ref.5), custom_call_target="tpu_custom_call" | custom-call | bytes 2359296 | tf_op jit(solution)/shard_map/fetch/pallas_call | solution.py:697
  36.5 1.0 %collective-permute-done.13.rest_6_ = bf16[256,128]{1,0:T(8,128)(2,1)S(1)} collective-permute-done((bf16[256,128]{1,0:T(8,128)(2,1)S(1)}, bf16[256,128]{1,0:T(8,128)(2,1)S(1)}, u32[]{:S(2)}, u32[]{:S(2)}) %collective-permute-start.13) | collective-permute-done | bytes 65568 | tf_op jit(solution)/shard_map/ppermute | solution.py:543
  37.5 0.7 %collective-permute-done.12.rest_5_ = bf16[256,128]{1,0:T(8,128)(2,1)S(1)} collective-permute-done((bf16[256,128]{1,0:T(8,128)(2,1)S(1)}, bf16[256,128]{1,0:T(8,128)(2,1)S(1)}, u32[]{:S(2)}, u32[]{:S(2)}) %collective-permute-start.12) | collective-permute-done | bytes 65568 | tf_op jit(solution)/shard_map/ppermute | solution.py:543
  38.2 1.0 %output.1 = (f32[16,384]{1,0:T(8,128)S(1)}, bf16[16,384]{1,0:T(8,128)(2,1)S(1)}, bf16[16,384]{1,0:T(8,128)(2,1)S(1)}, bf16[16,384]{1,0:T(8,128)(2,1)S(1)}) custom-call(s32[1]{0:T(128)} %bitcast.place_ref, bf16[256,128]{1,0:T(8,128)(2,1)S(1)} %news.1.after_ref.refs_0_.rest_0_, bf16[256,128]{1,0:T(8,128)(2,1)S(1)} %collective-permute-done.8.refs_1_.rest_1_, ...), custom_call_target="tpu_custom_call" | custom-call | tf_op jit(solution)/shard_map/output/pallas_call | solution.py:709
  39.3 1.6 %collective-permute-start.15 = (bf16[16,384]{1,0:T(8,128)(2,1)S(1)}, bf16[16,384]{1,0:T(8,128)(2,1)S(1)}, u32[]{:S(2)}, u32[]{:S(2)}) collective-permute-start(bf16[16,384]{1,0:T(8,128)(2,1)S(1)} %get-tuple-element.51), channel_id=1, source_target_pairs={{0,2},{1,3},{2,0},{3,1},{4,6},{5,7},{6,4},{7,5},{8,10},{9,11},{10,... | collective-permute-start | bytes 36872 | tf_op jit(solution)/shard_map/ppermute | solution.py:723
  40.8 0.3 collective-permute-start.16
  41.1 2.0 %patch.1 = bf16[24,2,64,768]{3,2,1,0:T(8,128)(2,1)} custom-call(s32[1]{0:T(128)} %bitcast.1.place_ref, s32[24]{0:T(128)S(1)} %copy-done.4, s32[24]{0:T(128)S(1)} %copy-done.5, s32[64]{0:T(128)S(1)} %copy-done.6, bf16[16,384]{1,0:T(8,128)(2,1)S(1)} %get-tuple-element.52.after_ref, ...), custom_call_target="tpu_custom_call", output_to_operand_aliasing={{}: (13, {})} | custom-call | bytes 2359296 | tf_op jit(solution)/shard_map/patch/pallas_call | solution.py:725
  43.1 0.6 %add_convert_fusion = bf16[16,384]{1,0:T(8,128)(2,1)} fusion(bf16[16,384]{1,0:T(8,128)(2,1)S(1)} %collective-permute-done.16, bf16[16,384]{1,0:T(8,128)(2,1)S(1)} %collective-permute-done.15, f32[16,384]{1,0:T(8,128)S(1)} %get-tuple-element.49, bf16[16,384]{1,0:T(8,128)(2,1)S(1)} %collective-permute-done.14), kind=kLoop, calls=%fused_computation.2 | loop fusion | flops 43008 | bytes 73728 | tf_op jit(solution)/shard_map/convert_element_type | solution.py:740
  (36 shorter events, 0.8 us)
Async XLA Ops:
  0.6 7.5 %copy-start.6 = (s32[64]{0:T(128)S(1)}, s32[64]{0:T(128)}, u32[]{:S(2)}) copy-start(s32[64]{0:T(128)} %length_ref.5) | copy-start | bytes 772
  0.6 7.5 %copy-start.5 = (s32[24]{0:T(128)S(1)}, s32[24]{0:T(128)}, u32[]{:S(2)}) copy-start(s32[24]{0:T(128)} %index_ref.5) | copy-start | bytes 292
  0.7 7.5 %copy-start.4 = (s32[24]{0:T(128)S(1)}, s32[24]{0:T(128)}, u32[]{:S(2)}) copy-start(s32[24]{0:T(128)} %owner_ref.5) | copy-start | bytes 292
  3.3 5.7 %copy-start.3 = (f32[32,896]{1,0:T(8,128)S(1)}, f32[32,896]{1,0:T(8,128)}, u32[]{:S(2)}) copy-start(f32[32,896]{1,0:T(8,128)} %get-tuple-element.28.kept_ref) | copy-start | bytes 344068
  3.3 5.7 %collective-permute-start = (bf16[32,896]{1,0:T(8,128)(2,1)}, bf16[32,896]{1,0:T(8,128)(2,1)S(1)}, u32[]{:S(2)}, u32[]{:S(2)}) collective-permute-start(bf16[32,896]{1,0:T(8,128)(2,1)} %get-tuple-element.29), channel_id=1, source_target_pairs={{0,4},{4,0},{8,12},{12,8},{16,20},{20,16},{24,28},{28,24},{1,5},{5... | collective-permute-start | bytes 172040 | tf_op jit(solution)/shard_map/ppermute | solution.py:543
  6.3 7.8 %collective-permute-start.4 = (bf16[32,1536]{1,0:T(8,128)(2,1)}, bf16[32,1536]{1,0:T(8,128)(2,1)S(1)}, u32[]{:S(2)}, u32[]{:S(2)}) collective-permute-start(bf16[32,1536]{1,0:T(8,128)(2,1)} %get-tuple-element.36), channel_id=1, source_target_pairs={{0,4},{4,0},{8,12},{12,8},{16,20},{20,16},{24,28},{28,24},{1,5},{5... | collective-permute-start | bytes 294920 | tf_op jit(solution)/shard_map/ppermute | solution.py:543
  6.4 7.7 %copy-start.1 = (f32[32,1536]{1,0:T(8,128)S(1)}, f32[32,1536]{1,0:T(8,128)}, u32[]{:S(2)}) copy-start(f32[32,1536]{1,0:T(8,128)} %get-tuple-element.35.kept_ref) | copy-start | bytes 589828
  9.1 9.0 %collective-permute-start.3 = (bf16[208,128]{1,0:T(8,128)(2,1)S(1)}, bf16[208,128]{1,0:T(8,128)(2,1)S(1)}, u32[]{:S(2)}, u32[]{:S(2)}) collective-permute-start(bf16[208,128]{1,0:T(8,128)(2,1)S(1)} %get-tuple-element.32), channel_id=1, source_target_pairs={{0,16},{4,20},{8,24},{12,28},{16,0},{20,4},{24,8},{28,12},{1,17},{... | collective-permute-start | bytes 159752 | tf_op jit(solution)/shard_map/ppermute | solution.py:543
  12.5 6.0 %collective-permute-start.2 = (bf16[208,128]{1,0:T(8,128)(2,1)S(1)}, bf16[208,128]{1,0:T(8,128)(2,1)S(1)}, u32[]{:S(2)}, u32[]{:S(2)}) collective-permute-start(bf16[208,128]{1,0:T(8,128)(2,1)S(1)} %get-tuple-element.32), channel_id=1, source_target_pairs={{0,24},{4,28},{8,16},{12,20},{16,8},{20,12},{24,0},{28,4},{1,25},{... | collective-permute-start | bytes 159752 | tf_op jit(solution)/shard_map/ppermute | solution.py:543
  13.9 4.7 %collective-permute-start.1 = (bf16[208,128]{1,0:T(8,128)(2,1)S(1)}, bf16[208,128]{1,0:T(8,128)(2,1)S(1)}, u32[]{:S(2)}, u32[]{:S(2)}) collective-permute-start(bf16[208,128]{1,0:T(8,128)(2,1)S(1)} %get-tuple-element.32), channel_id=1, source_target_pairs={{0,8},{4,12},{8,0},{12,4},{16,24},{20,28},{24,16},{28,20},{1,9},{5... | collective-permute-start | bytes 159752 | tf_op jit(solution)/shard_map/ppermute | solution.py:543
  14.1 6.4 %collective-permute-start.5 = (bf16[16,1536]{1,0:T(8,128)(2,1)S(1)}, bf16[16,1536]{1,0:T(8,128)(2,1)S(1)}, u32[]{:S(2)}, u32[]{:S(2)}) collective-permute-start(bf16[16,1536]{1,0:T(8,128)(2,1)S(1)} %get-tuple-element.38), channel_id=1, source_target_pairs={{0,8},{4,12},{8,0},{12,4},{16,24},{20,28},{24,16},{28,20},{1,9},{5... | collective-permute-start | bytes 147464 | tf_op jit(solution)/shard_map/ppermute | solution.py:543
  18.9 4.4 %collective-permute-start.7 = (bf16[32,768]{1,0:T(8,128)(2,1)S(1)}, bf16[32,768]{1,0:T(8,128)(2,1)S(1)}, u32[]{:S(2)}, u32[]{:S(2)}) collective-permute-start(bf16[32,768]{1,0:T(8,128)(2,1)S(1)} %get-tuple-element.33.after_ref.mine_ref.query_ref), channel_id=1, source_target_pairs={{0,4},{4,0},{8,12},{12,8},{16,20},{20,16},{24,28},{28,24},{1,5},{5... | collective-permute-start | bytes 147464 | tf_op jit(solution)/shard_map/ppermute | solution.py:543
  20.5 4.8 %collective-permute-start.6 = (bf16[8,1536]{1,0:T(8,128)(2,1)S(1)}, bf16[8,1536]{1,0:T(8,128)(2,1)S(1)}, u32[]{:S(2)}, u32[]{:S(2)}) collective-permute-start(bf16[8,1536]{1,0:T(8,128)(2,1)S(1)} %get-tuple-element.40), channel_id=1, source_target_pairs={{0,16},{4,20},{8,24},{12,28},{16,0},{20,4},{24,8},{28,12},{1,17},{... | collective-permute-start | bytes 73736 | tf_op jit(solution)/shard_map/ppermute | solution.py:543
  25.6 6.2 %collective-permute-start.8 = (bf16[256,128]{1,0:T(8,128)(2,1)S(1)}, bf16[256,128]{1,0:T(8,128)(2,1)S(1)}, u32[]{:S(2)}, u32[]{:S(2)}) collective-permute-start(bf16[256,128]{1,0:T(8,128)(2,1)S(1)} %news.1.after_ref.refs_0_.rest_0_), channel_id=1, source_target_pairs={{0,24},{4,28},{8,16},{12,20},{16,8},{20,12},{24,0},{28,4},{1,25},{... | collective-permute-start | bytes 196616 | tf_op jit(solution)/shard_map/ppermute | solution.py:543
  27.9 4.7 %collective-permute-start.10 = (bf16[256,128]{1,0:T(8,128)(2,1)S(1)}, bf16[256,128]{1,0:T(8,128)(2,1)S(1)}, u32[]{:S(2)}, u32[]{:S(2)}) collective-permute-start(bf16[256,128]{1,0:T(8,128)(2,1)S(1)} %news.1.after_ref.refs_0_.rest_0_), channel_id=1, source_target_pairs={{0,8},{4,12},{8,0},{12,4},{16,24},{20,28},{24,16},{28,20},{1,9},{5... | collective-permute-start | bytes 196616 | tf_op jit(solution)/shard_map/ppermute | solution.py:543
  27.9 5.9 %collective-permute-start.9 = (bf16[256,128]{1,0:T(8,128)(2,1)S(1)}, bf16[256,128]{1,0:T(8,128)(2,1)S(1)}, u32[]{:S(2)}, u32[]{:S(2)}) collective-permute-start(bf16[256,128]{1,0:T(8,128)(2,1)S(1)} %news.1.after_ref.refs_0_.rest_0_), channel_id=1, source_target_pairs={{0,16},{4,20},{8,24},{12,28},{16,0},{20,4},{24,8},{28,12},{1,17},{... | collective-permute-start | bytes 196616 | tf_op jit(solution)/shard_map/ppermute | solution.py:543
  31.5 6.7 %copy-start = (bf16[768,384]{1,0:T(8,128)(2,1)S(1)}, bf16[768,384]{1,0:T(8,128)(2,1)}, u32[]{:S(2)}) copy-start(bf16[768,384]{1,0:T(8,128)(2,1)} %rest_7_.1) | copy-start | bytes 1769476
  31.5 6.7 %copy-start.2 = (bf16[64,384]{1,0:T(8,128)(2,1)S(1)}, bf16[64,384]{1,0:T(8,128)(2,1)}, u32[]{:S(2)}) copy-start(bf16[64,384]{1,0:T(8,128)(2,1)} %rest_8_.1) | copy-start | bytes 147460
  31.7 6.4 %collective-permute-start.11 = (bf16[512,128]{1,0:T(8,128)(2,1)S(1)}, bf16[512,128]{1,0:T(8,128)(2,1)S(1)}, u32[]{:S(2)}, u32[]{:S(2)}) collective-permute-start(bf16[512,128]{1,0:T(8,128)(2,1)S(1)} %join.1), channel_id=1, source_target_pairs={{0,4},{4,0},{8,12},{12,8},{16,20},{20,16},{24,28},{28,24},{1,5},{5... | collective-permute-start | bytes 393224 | tf_op jit(solution)/shard_map/ppermute | solution.py:543
  32.6 4.9 %collective-permute-start.13 = (bf16[256,128]{1,0:T(8,128)(2,1)S(1)}, bf16[256,128]{1,0:T(8,128)(2,1)S(1)}, u32[]{:S(2)}, u32[]{:S(2)}) collective-permute-start(bf16[256,128]{1,0:T(8,128)(2,1)S(1)} %collective-permute-done.10.rest_3_), channel_id=1, source_target_pairs={{0,4},{4,0},{8,12},{12,8},{16,20},{20,16},{24,28},{28,24},{1,5},{5... | collective-permute-start | bytes 196616 | tf_op jit(solution)/shard_map/ppermute | solution.py:543
  33.9 4.3 %collective-permute-start.12 = (bf16[256,128]{1,0:T(8,128)(2,1)S(1)}, bf16[256,128]{1,0:T(8,128)(2,1)S(1)}, u32[]{:S(2)}, u32[]{:S(2)}) collective-permute-start(bf16[256,128]{1,0:T(8,128)(2,1)S(1)} %collective-permute-done.9.rest_2_), channel_id=1, source_target_pairs={{0,4},{4,0},{8,12},{12,8},{16,20},{20,16},{24,28},{28,24},{1,5},{5... | collective-permute-start | bytes 196616 | tf_op jit(solution)/shard_map/ppermute | solution.py:543
  39.2 3.9 %collective-permute-start.14 = (bf16[16,384]{1,0:T(8,128)(2,1)S(1)}, bf16[16,384]{1,0:T(8,128)(2,1)S(1)}, u32[]{:S(2)}, u32[]{:S(2)}) collective-permute-start(bf16[16,384]{1,0:T(8,128)(2,1)S(1)} %get-tuple-element.50), channel_id=1, source_target_pairs={{0,3},{1,2},{2,1},{3,0},{4,7},{5,6},{6,5},{7,4},{8,11},{9,10},{10,... | collective-permute-start | bytes 36872 | tf_op jit(solution)/shard_map/ppermute | solution.py:723
  39.3 3.8 %collective-permute-start.15 = (bf16[16,384]{1,0:T(8,128)(2,1)S(1)}, bf16[16,384]{1,0:T(8,128)(2,1)S(1)}, u32[]{:S(2)}, u32[]{:S(2)}) collective-permute-start(bf16[16,384]{1,0:T(8,128)(2,1)S(1)} %get-tuple-element.51), channel_id=1, source_target_pairs={{0,2},{1,3},{2,0},{3,1},{4,6},{5,7},{6,4},{7,5},{8,10},{9,11},{10,... | collective-permute-start | bytes 36872 | tf_op jit(solution)/shard_map/ppermute | solution.py:723
  40.8 2.3 %collective-permute-start.16 = (bf16[16,384]{1,0:T(8,128)(2,1)S(1)}, bf16[16,384]{1,0:T(8,128)(2,1)S(1)}, u32[]{:S(2)}, u32[]{:S(2)}) collective-permute-start(bf16[16,384]{1,0:T(8,128)(2,1)S(1)} %get-tuple-element.52.after_ref), channel_id=1, source_target_pairs={{0,1},{1,0},{2,3},{3,2},{4,5},{5,4},{6,7},{7,6},{8,9},{9,8},{10,11... | collective-permute-start | bytes 36872 | tf_op jit(solution)/shard_map/ppermute | solution.py:723

commit v8 on v7

--- a/solution.py
+++ b/solution.py
@@ -512,6 +512,13 @@
     for m, send in enumerate(sends, 1):
         theirs = pl.ds(pl.multiple_of((place ^ m) * share, share), share)
         send[...] = product[theirs, :].astype(send.dtype)
+
+
+def add_kernel(own_ref, *rest):
+    total = own_ref[...]
+    for ref in rest[:-1]:
+        total = total + ref[...].astype(jnp.float32)
+    rest[-1][...] = total.astype(jnp.bfloat16)
 
 
 def shards(states, norm_gain, w_qkv, w_out, cache, context_len, block_owner, block_index):
@@ -718,10 +725,16 @@
         compiler_params=limit,
         name="output",
     )(rank.reshape(1).astype(jnp.int32), *pieces, w_out, states, near)
-    total = own
-    for m in range(ranks - 1, 0, -1):
-        moved = lax.ppermute(sends[m - 1], "tp", [(i, i ^ m) for i in range(ranks)])
-        total = total + moved.astype(jnp.float32)
+    moved = [
+        lax.ppermute(sends[m - 1], "tp", [(i, i ^ m) for i in range(ranks)])
+        for m in (1, *range(ranks - 1, 1, -1))
+    ]
+    hidden = pl.pallas_call(
+        add_kernel,
+        out_shape=array(kept_rows, out_columns),
+        compiler_params=limit,
+        name="add",
+    )(own, *moved)
     updated = pl.pallas_call(
         functools.partial(patch_kernel, peers),
         out_shape=array(*cache.shape),
@@ -737,7 +750,7 @@
         cost_estimate=moves(blocks * ROWS * columns * 8),
         name="patch",
     )(at, *table, sends[0], *pieces, near, updated)
-    return (total.astype(jnp.bfloat16), updated)
+    return (hidden, updated)
 
 
 def solution(mesh):

time: 44 us -> 44 us (level)
  Pallas kernels: 16.5 us -> 17.2 us
  other arithmetic: 1.13 us -> 0.52 us
    pallas_call x0 -> x1, Pallas kernels: none -> 0.61 us  [shards(): pl.pallas_call(add_kernel, out_shape=array(kept_rows, out_columns), compi...]
    convert_element_type x1 -> x0, other arithmetic: 0.61 us -> none  [shards(): return (total.astype(jnp.bfloat16), updated)]
where the time goes in v8:
time: 44 us; the launch traced here: 43.8 us
  starting transfers between devices  22.1 us (50%)
  Pallas kernels  17.2 us (39%)
  waiting for transfers between devices  3.03 us (7%)
  between operations  0.9 us (2%)
  other arithmetic  0.52 us (1%)
    ppermute x14, starting transfers between devices, to_peer(): return lax.ppermute(value, 'seq', [(i, i ^ m) for i in range(peers)])  20.2 us
    pallas_call x2, Pallas kernels, stage(): pl.pallas_call(functools.partial(stage_kernel, part), out_shape=array(blo...  3.32 us
    ppermute x14, waiting for transfers between devices, to_peer(): return lax.ppermute(value, 'seq', [(i, i ^ m) for i in range(peers)])  3.02 us
    pallas_call x1, Pallas kernels, shards(): pl.pallas_call(project_kernel, out_shape=(array(half, columns + LANES), a...  2.59 us
    pallas_call x1, Pallas kernels, shards(): pl.pallas_call(functools.partial(patch_kernel, peers), out_shape=array(*c...  1.97 us
    ppermute x3, starting transfers between devices, shards(): lax.ppermute(sends[m - 1], 'tp', [(i, i ^ m) for i in range(ranks)])  1.92 us
    pallas_call x1, Pallas kernels, shards(): pl.pallas_call(fetch_kernel, out_shape=array(blocks, 2, ROWS, columns), i...  1.86 us
    pallas_call x1, Pallas kernels, shards(): pl.pallas_call(store_keys_kernel, out_shape=(array(*cache.shape), array(8...  1.44 us
  transfers between devices with their start and end apart: 17, of which 5 were waited for; matrix products, arithmetic and copies ran while one was open for 1% of the time, Pallas kernels for 29%

profile of v8, /device:TPU:0, one launch (start us, length us, event | category | flops | bytes accessed | tf_op | source)
XLA Modules:
  0.0 43.8 jit_solution(296081139704256764)
XLA Ops:
  0.7 2.6 %project.1 = (bf16[32,896]{1,0:T(8,128)(2,1)}, f32[32,896]{1,0:T(8,128)}, bf16[32,1536]{1,0:T(8,128)(2,1)}, f32[32,1536]{1,0:T(8,128)}) custom-call(s32[1]{0:T(128)} %bitcast.1.place_ref, bf16[64,384]{1,0:T(8,128)(2,1)} %rest_8_.1, bf16[384]{0:T(512)(128)(2,1)} %gain_ref.1, bf16[3,384,768]{2,1,0:T(8,128)(2,1)} %w_ref.1), custom_call_target="tpu_custom_call" | custom-call | tf_op jit(solution)/shard_map/project/pallas_call | solution.py:555
  3.3 3.0 %collective-permute-start = (bf16[32,896]{1,0:T(8,128)(2,1)}, bf16[32,896]{1,0:T(8,128)(2,1)S(1)}, u32[]{:S(2)}, u32[]{:S(2)}) collective-permute-start(bf16[32,896]{1,0:T(8,128)(2,1)} %get-tuple-element.29), channel_id=1, source_target_pairs={{0,4},{4,0},{8,12},{12,8},{16,20},{20,16},{24,28},{28,24},{1,5},{5... | collective-permute-start | bytes 172040 | tf_op jit(solution)/shard_map/ppermute | solution.py:550
  6.4 1.7 %stage_values.1.after_ref.values_ref = bf16[24,64,768]{2,1,0:T(8,128)(2,1)S(1)} custom-call(bf16[24,2,64,768]{3,2,1,0:T(8,128)(2,1)} %cache_ref.5), custom_call_target="tpu_custom_call" | custom-call | bytes 2359296 | tf_op jit(solution)/shard_map/stage_values/pallas_call | solution.py:596
  8.1 0.7 %plan.1 = (bf16[192,32]{1,0:T(8,128)(2,1)S(1)}, bf16[192,32]{1,0:T(8,128)(2,1)S(1)}, s32[192,128]{1,0:T(8,128)S(1)}, f32[192,128]{1,0:T(8,128)S(1)}) custom-call(s32[1]{0:T(128)} %bitcast.1.place_ref, s32[24]{0:T(128)S(1)} %copy-done.4, s32[24]{0:T(128)S(1)} %copy-done.5, s32[64]{0:T(128)S(1)} %copy-done.6), custom_call_target="tpu_custom_call" | custom-call | tf_op jit(solution)/shard_map/plan/pallas_call | solution.py:583
  9.1 3.4 %collective-permute-start.3 = (bf16[208,128]{1,0:T(8,128)(2,1)S(1)}, bf16[208,128]{1,0:T(8,128)(2,1)S(1)}, u32[]{:S(2)}, u32[]{:S(2)}) collective-permute-start(bf16[208,128]{1,0:T(8,128)(2,1)S(1)} %get-tuple-element.32), channel_id=1, source_target_pairs={{0,16},{4,20},{8,24},{12,28},{16,0},{20,4},{24,8},{28,12},{1,17},{... | collective-permute-start | bytes 159752 | tf_op jit(solution)/shard_map/ppermute | solution.py:550
  12.5 1.3 %collective-permute-start.2 = (bf16[208,128]{1,0:T(8,128)(2,1)S(1)}, bf16[208,128]{1,0:T(8,128)(2,1)S(1)}, u32[]{:S(2)}, u32[]{:S(2)}) collective-permute-start(bf16[208,128]{1,0:T(8,128)(2,1)S(1)} %get-tuple-element.32), channel_id=1, source_target_pairs={{0,24},{4,28},{8,16},{12,20},{16,8},{20,12},{24,0},{28,4},{1,25},{... | collective-permute-start | bytes 159752 | tf_op jit(solution)/shard_map/ppermute | solution.py:550
  13.9 0.2 collective-permute-start.1
  14.1 1.9 %collective-permute-start.5 = (bf16[16,1536]{1,0:T(8,128)(2,1)S(1)}, bf16[16,1536]{1,0:T(8,128)(2,1)S(1)}, u32[]{:S(2)}, u32[]{:S(2)}) collective-permute-start(bf16[16,1536]{1,0:T(8,128)(2,1)S(1)} %get-tuple-element.38), channel_id=1, source_target_pairs={{0,8},{4,12},{8,0},{12,4},{16,24},{20,28},{24,16},{28,20},{1,9},{5... | collective-permute-start | bytes 147464 | tf_op jit(solution)/shard_map/ppermute | solution.py:550
  16.0 0.4 multiply_sine_fusion
  16.4 1.6 %stage_keys.1.after_ref.keys_ref = bf16[24,64,768]{2,1,0:T(8,128)(2,1)S(1)} custom-call(bf16[24,2,64,768]{3,2,1,0:T(8,128)(2,1)} %cache_ref.5), custom_call_target="tpu_custom_call" | custom-call | bytes 2359296 | tf_op jit(solution)/shard_map/stage_keys/pallas_call | solution.py:596
  18.1 0.5 %collective-permute-done.2.rest_1_ = bf16[208,128]{1,0:T(8,128)(2,1)S(1)} collective-permute-done((bf16[208,128]{1,0:T(8,128)(2,1)S(1)}, bf16[208,128]{1,0:T(8,128)(2,1)S(1)}, u32[]{:S(2)}, u32[]{:S(2)}) %collective-permute-start.2) | collective-permute-done | bytes 53280 | tf_op jit(solution)/shard_map/ppermute | solution.py:550
  18.6 0.3 query.1
  18.9 1.6 %collective-permute-start.7 = (bf16[32,768]{1,0:T(8,128)(2,1)S(1)}, bf16[32,768]{1,0:T(8,128)(2,1)S(1)}, u32[]{:S(2)}, u32[]{:S(2)}) collective-permute-start(bf16[32,768]{1,0:T(8,128)(2,1)S(1)} %get-tuple-element.33.after_ref.mine_ref.query_ref), channel_id=1, source_target_pairs={{0,4},{4,0},{8,12},{12,8},{16,20},{20,16},{24,28},{28,24},{1,5},{5... | collective-permute-start | bytes 147464 | tf_op jit(solution)/shard_map/ppermute | solution.py:550
  20.5 1.3 %collective-permute-start.6 = (bf16[8,1536]{1,0:T(8,128)(2,1)S(1)}, bf16[8,1536]{1,0:T(8,128)(2,1)S(1)}, u32[]{:S(2)}, u32[]{:S(2)}) collective-permute-start(bf16[8,1536]{1,0:T(8,128)(2,1)S(1)} %get-tuple-element.40), channel_id=1, source_target_pairs={{0,16},{4,20},{8,24},{12,28},{16,0},{20,4},{24,8},{28,12},{1,17},{... | collective-permute-start | bytes 73736 | tf_op jit(solution)/shard_map/ppermute | solution.py:550
  21.8 1.4 %store_keys.1 = (bf16[24,2,64,768]{3,2,1,0:T(8,128)(2,1)}, f32[8,128]{1,0:T(8,128)S(1)}) custom-call(bf16[32,768]{1,0:T(8,128)(2,1)S(1)} %get-tuple-element.33.after_ref.mine_ref.query_ref, bf16[24,64,768]{2,1,0:T(8,128)(2,1)S(1)} %stage_keys.1.after_ref.keys_ref), custom_call_target="tpu_custom_call" | custom-call | bytes 2359296 | tf_op jit(solution)/shard_map/store_keys/pallas_call | solution.py:651
  23.3 1.4 %attend.1 = (f32[32,768]{1,0:T(8,128)S(1)}, f32[16,128]{1,0:T(8,128)S(1)}) custom-call(bf16[32,768]{1,0:T(8,128)(2,1)S(1)} %get-tuple-element.33.after_ref.mine_ref.query_ref, bf16[32,768]{1,0:T(8,128)(2,1)S(1)} %collective-permute-done.7.other_ref, bf16[192,32]{1,0:T(8,128)(2,1)S(1)} %get-tuple-element.30.planned_ref.pick_mine_ref, ...), custom_call_target="tpu_custom_call" | custom-call | tf_op jit(solution)/shard_map/attend/pallas_call | solution.py:662
  24.7 0.6 %collective-permute-done.6.recv_ref = bf16[8,1536]{1,0:T(8,128)(2,1)S(1)} collective-permute-done((bf16[8,1536]{1,0:T(8,128)(2,1)S(1)}, bf16[8,1536]{1,0:T(8,128)(2,1)S(1)}, u32[]{:S(2)}, u32[]{:S(2)}) %collective-permute-start.6) | collective-permute-done | bytes 24608 | tf_op jit(solution)/shard_map/ppermute | solution.py:550
  25.3 0.3 news.1.after_ref.refs_0_.rest_0_
  25.6 2.3 %collective-permute-start.8 = (bf16[256,128]{1,0:T(8,128)(2,1)S(1)}, bf16[256,128]{1,0:T(8,128)(2,1)S(1)}, u32[]{:S(2)}, u32[]{:S(2)}) collective-permute-start(bf16[256,128]{1,0:T(8,128)(2,1)S(1)} %news.1.after_ref.refs_0_.rest_0_), channel_id=1, source_target_pairs={{0,24},{4,28},{8,16},{12,20},{16,8},{20,12},{24,0},{28,4},{1,25},{... | collective-permute-start | bytes 196616 | tf_op jit(solution)/shard_map/ppermute | solution.py:550
  27.9 2.1 %collective-permute-start.9 = (bf16[256,128]{1,0:T(8,128)(2,1)S(1)}, bf16[256,128]{1,0:T(8,128)(2,1)S(1)}, u32[]{:S(2)}, u32[]{:S(2)}) collective-permute-start(bf16[256,128]{1,0:T(8,128)(2,1)S(1)} %news.1.after_ref.refs_0_.rest_0_), channel_id=1, source_target_pairs={{0,16},{4,20},{8,24},{12,28},{16,0},{20,4},{24,8},{28,12},{1,17},{... | collective-permute-start | bytes 196616 | tf_op jit(solution)/shard_map/ppermute | solution.py:550
  30.0 1.4 %store_values.1 = (bf16[24,2,64,768]{3,2,1,0:T(8,128)(2,1)}, f32[8,128]{1,0:T(8,128)S(1)}) custom-call(bf16[256,128]{1,0:T(8,128)(2,1)S(1)} %news.1.after_ref.refs_0_.rest_0_, bf16[24,64,768]{2,1,0:T(8,128)(2,1)S(1)} %stage_values.1.after_ref.values_ref, bf16[24,2,64,768]{3,2,1,0:T(8,128)(2,1)} %get-tuple-element.47.held_ref), custom_call_target="tpu_custom_call", output_to_operand_aliasing={{0}: (2, {})} | custom-call | bytes 2359296 | tf_op jit(solution)/shard_map/store_values/pallas_call | solution.py:680
  31.7 0.8 %collective-permute-start.11 = (bf16[512,128]{1,0:T(8,128)(2,1)S(1)}, bf16[512,128]{1,0:T(8,128)(2,1)S(1)}, u32[]{:S(2)}, u32[]{:S(2)}) collective-permute-start(bf16[512,128]{1,0:T(8,128)(2,1)S(1)} %join.1), channel_id=1, source_target_pairs={{0,4},{4,0},{8,12},{12,8},{16,20},{20,16},{24,28},{28,24},{1,5},{5... | collective-permute-start | bytes 393224 | tf_op jit(solution)/shard_map/ppermute | solution.py:550
  32.6 1.3 %collective-permute-start.13 = (bf16[256,128]{1,0:T(8,128)(2,1)S(1)}, bf16[256,128]{1,0:T(8,128)(2,1)S(1)}, u32[]{:S(2)}, u32[]{:S(2)}) collective-permute-start(bf16[256,128]{1,0:T(8,128)(2,1)S(1)} %collective-permute-done.10.rest_3_), channel_id=1, source_target_pairs={{0,4},{4,0},{8,12},{12,8},{16,20},{20,16},{24,28},{28,24},{1,5},{5... | collective-permute-start | bytes 196616 | tf_op jit(solution)/shard_map/ppermute | solution.py:550
  33.9 0.8 %collective-permute-start.12 = (bf16[256,128]{1,0:T(8,128)(2,1)S(1)}, bf16[256,128]{1,0:T(8,128)(2,1)S(1)}, u32[]{:S(2)}, u32[]{:S(2)}) collective-permute-start(bf16[256,128]{1,0:T(8,128)(2,1)S(1)} %collective-permute-done.9.rest_2_), channel_id=1, source_target_pairs={{0,4},{4,0},{8,12},{12,8},{16,20},{20,16},{24,28},{28,24},{1,5},{5... | collective-permute-start | bytes 196616 | tf_op jit(solution)/shard_map/ppermute | solution.py:550
  34.6 1.9 %fetch.1.rest_9_.rest_7_ = bf16[24,2,16,768]{3,2,1,0:T(8,128)(2,1)S(1)} custom-call(s32[24]{0:T(128)S(1)} %copy-done.4, s32[24]{0:T(128)S(1)} %copy-done.5, s32[64]{0:T(128)S(1)} %copy-done.6, bf16[256,128]{1,0:T(8,128)(2,1)S(1)} %news.1.after_ref.refs_0_.rest_0_, bf16[24,2,64,768]{3,2,1,0:T(8,128)(2,1)} %cache_ref.5), custom_call_target="tpu_custom_call" | custom-call | bytes 2359296 | tf_op jit(solution)/shard_map/fetch/pallas_call | solution.py:704
  36.5 1.0 %collective-permute-done.13.rest_6_ = bf16[256,128]{1,0:T(8,128)(2,1)S(1)} collective-permute-done((bf16[256,128]{1,0:T(8,128)(2,1)S(1)}, bf16[256,128]{1,0:T(8,128)(2,1)S(1)}, u32[]{:S(2)}, u32[]{:S(2)}) %collective-permute-start.13) | collective-permute-done | bytes 65568 | tf_op jit(solution)/shard_map/ppermute | solution.py:550
  37.5 0.7 %collective-permute-done.12.rest_5_ = bf16[256,128]{1,0:T(8,128)(2,1)S(1)} collective-permute-done((bf16[256,128]{1,0:T(8,128)(2,1)S(1)}, bf16[256,128]{1,0:T(8,128)(2,1)S(1)}, u32[]{:S(2)}, u32[]{:S(2)}) %collective-permute-start.12) | collective-permute-done | bytes 65568 | tf_op jit(solution)/shard_map/ppermute | solution.py:550
  38.2 1.0 %output.1 = (f32[16,384]{1,0:T(8,128)S(1)}, bf16[16,384]{1,0:T(8,128)(2,1)S(1)}, bf16[16,384]{1,0:T(8,128)(2,1)S(1)}, bf16[16,384]{1,0:T(8,128)(2,1)S(1)}) custom-call(s32[1]{0:T(128)} %bitcast.place_ref, bf16[256,128]{1,0:T(8,128)(2,1)S(1)} %news.1.after_ref.refs_0_.rest_0_, bf16[256,128]{1,0:T(8,128)(2,1)S(1)} %collective-permute-done.8.refs_1_.rest_1_, ...), custom_call_target="tpu_custom_call" | custom-call | tf_op jit(solution)/shard_map/output/pallas_call | solution.py:716
  39.3 1.6 %collective-permute-start.16 = (bf16[16,384]{1,0:T(8,128)(2,1)S(1)}, bf16[16,384]{1,0:T(8,128)(2,1)S(1)}, u32[]{:S(2)}, u32[]{:S(2)}) collective-permute-start(bf16[16,384]{1,0:T(8,128)(2,1)S(1)} %get-tuple-element.52), channel_id=1, source_target_pairs={{0,2},{1,3},{2,0},{3,1},{4,6},{5,7},{6,4},{7,5},{8,10},{9,11},{10,... | collective-permute-start | bytes 36872 | tf_op jit(solution)/shard_map/ppermute | solution.py:729
  40.8 0.3 collective-permute-start.14
  41.1 2.0 %patch.1 = bf16[24,2,64,768]{3,2,1,0:T(8,128)(2,1)} custom-call(s32[1]{0:T(128)} %bitcast.1.place_ref, s32[24]{0:T(128)S(1)} %copy-done.4, s32[24]{0:T(128)S(1)} %copy-done.5, s32[64]{0:T(128)S(1)} %copy-done.6, bf16[16,384]{1,0:T(8,128)(2,1)S(1)} %get-tuple-element.50.after_ref, ...), custom_call_target="tpu_custom_call", output_to_operand_aliasing={{}: (13, {})} | custom-call | bytes 2359296 | tf_op jit(solution)/shard_map/patch/pallas_call | solution.py:738
  43.1 0.6 %add.31 = bf16[16,384]{1,0:T(8,128)(2,1)} custom-call(f32[16,384]{1,0:T(8,128)S(1)} %get-tuple-element.49.own_ref, bf16[16,384]{1,0:T(8,128)(2,1)S(1)} %collective-permute-done.14.rest_0_, bf16[16,384]{1,0:T(8,128)(2,1)S(1)} %collective-permute-done.15.rest_1_, bf16[16,384]{1,0:T(8,128)(2,1)S(1)} %collective-permute-done.16.rest_2_), custom_call_target="tpu_custom_call" | custom-call | tf_op jit(solution)/shard_map/add/pallas_call | solution.py:732
  (36 shorter events, 0.8 us)
Async XLA Ops:
  0.6 7.5 %copy-start.6 = (s32[64]{0:T(128)S(1)}, s32[64]{0:T(128)}, u32[]{:S(2)}) copy-start(s32[64]{0:T(128)} %length_ref.5) | copy-start | bytes 772
  0.6 7.5 %copy-start.5 = (s32[24]{0:T(128)S(1)}, s32[24]{0:T(128)}, u32[]{:S(2)}) copy-start(s32[24]{0:T(128)} %index_ref.5) | copy-start | bytes 292
  0.7 7.5 %copy-start.4 = (s32[24]{0:T(128)S(1)}, s32[24]{0:T(128)}, u32[]{:S(2)}) copy-start(s32[24]{0:T(128)} %owner_ref.5) | copy-start | bytes 292
  3.3 5.7 %copy-start.3 = (f32[32,896]{1,0:T(8,128)S(1)}, f32[32,896]{1,0:T(8,128)}, u32[]{:S(2)}) copy-start(f32[32,896]{1,0:T(8,128)} %get-tuple-element.28.kept_ref) | copy-start | bytes 344068
  3.3 5.7 %collective-permute-start = (bf16[32,896]{1,0:T(8,128)(2,1)}, bf16[32,896]{1,0:T(8,128)(2,1)S(1)}, u32[]{:S(2)}, u32[]{:S(2)}) collective-permute-start(bf16[32,896]{1,0:T(8,128)(2,1)} %get-tuple-element.29), channel_id=1, source_target_pairs={{0,4},{4,0},{8,12},{12,8},{16,20},{20,16},{24,28},{28,24},{1,5},{5... | collective-permute-start | bytes 172040 | tf_op jit(solution)/shard_map/ppermute | solution.py:550
  6.3 7.8 %collective-permute-start.4 = (bf16[32,1536]{1,0:T(8,128)(2,1)}, bf16[32,1536]{1,0:T(8,128)(2,1)S(1)}, u32[]{:S(2)}, u32[]{:S(2)}) collective-permute-start(bf16[32,1536]{1,0:T(8,128)(2,1)} %get-tuple-element.36), channel_id=1, source_target_pairs={{0,4},{4,0},{8,12},{12,8},{16,20},{20,16},{24,28},{28,24},{1,5},{5... | collective-permute-start | bytes 294920 | tf_op jit(solution)/shard_map/ppermute | solution.py:550
  6.4 7.7 %copy-start.1 = (f32[32,1536]{1,0:T(8,128)S(1)}, f32[32,1536]{1,0:T(8,128)}, u32[]{:S(2)}) copy-start(f32[32,1536]{1,0:T(8,128)} %get-tuple-element.35.kept_ref) | copy-start | bytes 589828
  9.1 9.0 %collective-permute-start.3 = (bf16[208,128]{1,0:T(8,128)(2,1)S(1)}, bf16[208,128]{1,0:T(8,128)(2,1)S(1)}, u32[]{:S(2)}, u32[]{:S(2)}) collective-permute-start(bf16[208,128]{1,0:T(8,128)(2,1)S(1)} %get-tuple-element.32), channel_id=1, source_target_pairs={{0,16},{4,20},{8,24},{12,28},{16,0},{20,4},{24,8},{28,12},{1,17},{... | collective-permute-start | bytes 159752 | tf_op jit(solution)/shard_map/ppermute | solution.py:550
  12.5 6.0 %collective-permute-start.2 = (bf16[208,128]{1,0:T(8,128)(2,1)S(1)}, bf16[208,128]{1,0:T(8,128)(2,1)S(1)}, u32[]{:S(2)}, u32[]{:S(2)}) collective-permute-start(bf16[208,128]{1,0:T(8,128)(2,1)S(1)} %get-tuple-element.32), channel_id=1, source_target_pairs={{0,24},{4,28},{8,16},{12,20},{16,8},{20,12},{24,0},{28,4},{1,25},{... | collective-permute-start | bytes 159752 | tf_op jit(solution)/shard_map/ppermute | solution.py:550
  13.9 4.7 %collective-permute-start.1 = (bf16[208,128]{1,0:T(8,128)(2,1)S(1)}, bf16[208,128]{1,0:T(8,128)(2,1)S(1)}, u32[]{:S(2)}, u32[]{:S(2)}) collective-permute-start(bf16[208,128]{1,0:T(8,128)(2,1)S(1)} %get-tuple-element.32), channel_id=1, source_target_pairs={{0,8},{4,12},{8,0},{12,4},{16,24},{20,28},{24,16},{28,20},{1,9},{5... | collective-permute-start | bytes 159752 | tf_op jit(solution)/shard_map/ppermute | solution.py:550
  14.1 6.4 %collective-permute-start.5 = (bf16[16,1536]{1,0:T(8,128)(2,1)S(1)}, bf16[16,1536]{1,0:T(8,128)(2,1)S(1)}, u32[]{:S(2)}, u32[]{:S(2)}) collective-permute-start(bf16[16,1536]{1,0:T(8,128)(2,1)S(1)} %get-tuple-element.38), channel_id=1, source_target_pairs={{0,8},{4,12},{8,0},{12,4},{16,24},{20,28},{24,16},{28,20},{1,9},{5... | collective-permute-start | bytes 147464 | tf_op jit(solution)/shard_map/ppermute | solution.py:550
  18.9 4.4 %collective-permute-start.7 = (bf16[32,768]{1,0:T(8,128)(2,1)S(1)}, bf16[32,768]{1,0:T(8,128)(2,1)S(1)}, u32[]{:S(2)}, u32[]{:S(2)}) collective-permute-start(bf16[32,768]{1,0:T(8,128)(2,1)S(1)} %get-tuple-element.33.after_ref.mine_ref.query_ref), channel_id=1, source_target_pairs={{0,4},{4,0},{8,12},{12,8},{16,20},{20,16},{24,28},{28,24},{1,5},{5... | collective-permute-start | bytes 147464 | tf_op jit(solution)/shard_map/ppermute | solution.py:550
  20.5 4.8 %collective-permute-start.6 = (bf16[8,1536]{1,0:T(8,128)(2,1)S(1)}, bf16[8,1536]{1,0:T(8,128)(2,1)S(1)}, u32[]{:S(2)}, u32[]{:S(2)}) collective-permute-start(bf16[8,1536]{1,0:T(8,128)(2,1)S(1)} %get-tuple-element.40), channel_id=1, source_target_pairs={{0,16},{4,20},{8,24},{12,28},{16,0},{20,4},{24,8},{28,12},{1,17},{... | collective-permute-start | bytes 73736 | tf_op jit(solution)/shard_map/ppermute | solution.py:550
  25.6 6.2 %collective-permute-start.8 = (bf16[256,128]{1,0:T(8,128)(2,1)S(1)}, bf16[256,128]{1,0:T(8,128)(2,1)S(1)}, u32[]{:S(2)}, u32[]{:S(2)}) collective-permute-start(bf16[256,128]{1,0:T(8,128)(2,1)S(1)} %news.1.after_ref.refs_0_.rest_0_), channel_id=1, source_target_pairs={{0,24},{4,28},{8,16},{12,20},{16,8},{20,12},{24,0},{28,4},{1,25},{... | collective-permute-start | bytes 196616 | tf_op jit(solution)/shard_map/ppermute | solution.py:550
  27.9 4.7 %collective-permute-start.10 = (bf16[256,128]{1,0:T(8,128)(2,1)S(1)}, bf16[256,128]{1,0:T(8,128)(2,1)S(1)}, u32[]{:S(2)}, u32[]{:S(2)}) collective-permute-start(bf16[256,128]{1,0:T(8,128)(2,1)S(1)} %news.1.after_ref.refs_0_.rest_0_), channel_id=1, source_target_pairs={{0,8},{4,12},{8,0},{12,4},{16,24},{20,28},{24,16},{28,20},{1,9},{5... | collective-permute-start | bytes 196616 | tf_op jit(solution)/shard_map/ppermute | solution.py:550
  27.9 5.9 %collective-permute-start.9 = (bf16[256,128]{1,0:T(8,128)(2,1)S(1)}, bf16[256,128]{1,0:T(8,128)(2,1)S(1)}, u32[]{:S(2)}, u32[]{:S(2)}) collective-permute-start(bf16[256,128]{1,0:T(8,128)(2,1)S(1)} %news.1.after_ref.refs_0_.rest_0_), channel_id=1, source_target_pairs={{0,16},{4,20},{8,24},{12,28},{16,0},{20,4},{24,8},{28,12},{1,17},{... | collective-permute-start | bytes 196616 | tf_op jit(solution)/shard_map/ppermute | solution.py:550
  31.5 6.7 %copy-start = (bf16[768,384]{1,0:T(8,128)(2,1)S(1)}, bf16[768,384]{1,0:T(8,128)(2,1)}, u32[]{:S(2)}) copy-start(bf16[768,384]{1,0:T(8,128)(2,1)} %rest_7_.1) | copy-start | bytes 1769476
  31.5 6.7 %copy-start.2 = (bf16[64,384]{1,0:T(8,128)(2,1)S(1)}, bf16[64,384]{1,0:T(8,128)(2,1)}, u32[]{:S(2)}) copy-start(bf16[64,384]{1,0:T(8,128)(2,1)} %rest_8_.1) | copy-start | bytes 147460
  31.7 6.4 %collective-permute-start.11 = (bf16[512,128]{1,0:T(8,128)(2,1)S(1)}, bf16[512,128]{1,0:T(8,128)(2,1)S(1)}, u32[]{:S(2)}, u32[]{:S(2)}) collective-permute-start(bf16[512,128]{1,0:T(8,128)(2,1)S(1)} %join.1), channel_id=1, source_target_pairs={{0,4},{4,0},{8,12},{12,8},{16,20},{20,16},{24,28},{28,24},{1,5},{5... | collective-permute-start | bytes 393224 | tf_op jit(solution)/shard_map/ppermute | solution.py:550
  32.6 4.9 %collective-permute-start.13 = (bf16[256,128]{1,0:T(8,128)(2,1)S(1)}, bf16[256,128]{1,0:T(8,128)(2,1)S(1)}, u32[]{:S(2)}, u32[]{:S(2)}) collective-permute-start(bf16[256,128]{1,0:T(8,128)(2,1)S(1)} %collective-permute-done.10.rest_3_), channel_id=1, source_target_pairs={{0,4},{4,0},{8,12},{12,8},{16,20},{20,16},{24,28},{28,24},{1,5},{5... | collective-permute-start | bytes 196616 | tf_op jit(solution)/shard_map/ppermute | solution.py:550
  33.9 4.3 %collective-permute-start.12 = (bf16[256,128]{1,0:T(8,128)(2,1)S(1)}, bf16[256,128]{1,0:T(8,128)(2,1)S(1)}, u32[]{:S(2)}, u32[]{:S(2)}) collective-permute-start(bf16[256,128]{1,0:T(8,128)(2,1)S(1)} %collective-permute-done.9.rest_2_), channel_id=1, source_target_pairs={{0,4},{4,0},{8,12},{12,8},{16,20},{20,16},{24,28},{28,24},{1,5},{5... | collective-permute-start | bytes 196616 | tf_op jit(solution)/shard_map/ppermute | solution.py:550
  39.2 3.9 %collective-permute-start.15 = (bf16[16,384]{1,0:T(8,128)(2,1)S(1)}, bf16[16,384]{1,0:T(8,128)(2,1)S(1)}, u32[]{:S(2)}, u32[]{:S(2)}) collective-permute-start(bf16[16,384]{1,0:T(8,128)(2,1)S(1)} %get-tuple-element.51), channel_id=1, source_target_pairs={{0,3},{1,2},{2,1},{3,0},{4,7},{5,6},{6,5},{7,4},{8,11},{9,10},{10,... | collective-permute-start | bytes 36872 | tf_op jit(solution)/shard_map/ppermute | solution.py:729
  39.3 3.8 %collective-permute-start.16 = (bf16[16,384]{1,0:T(8,128)(2,1)S(1)}, bf16[16,384]{1,0:T(8,128)(2,1)S(1)}, u32[]{:S(2)}, u32[]{:S(2)}) collective-permute-start(bf16[16,384]{1,0:T(8,128)(2,1)S(1)} %get-tuple-element.52), channel_id=1, source_target_pairs={{0,2},{1,3},{2,0},{3,1},{4,6},{5,7},{6,4},{7,5},{8,10},{9,11},{10,... | collective-permute-start | bytes 36872 | tf_op jit(solution)/shard_map/ppermute | solution.py:729
  40.8 2.3 %collective-permute-start.14 = (bf16[16,384]{1,0:T(8,128)(2,1)S(1)}, bf16[16,384]{1,0:T(8,128)(2,1)S(1)}, u32[]{:S(2)}, u32[]{:S(2)}) collective-permute-start(bf16[16,384]{1,0:T(8,128)(2,1)S(1)} %get-tuple-element.50.after_ref), channel_id=1, source_target_pairs={{0,1},{1,0},{2,3},{3,2},{4,5},{5,4},{6,7},{7,6},{8,9},{9,8},{10,11... | collective-permute-start | bytes 36872 | tf_op jit(solution)/shard_map/ppermute | solution.py:729
